TPU v7x, 512 devices: a whole 4x8x8 slice. The times are simulated.
512 devices in a mesh: gx: 16 (over y, core), gy: 16 (over x_lo, z), gz: 2 (over x_hi).
Axes of the slice: x: 4 (x_hi: 2, x_lo: 2; x = x_hi * 2 + x_lo), y: 8, z: 8, core: 2. Of those that a mesh axis runs over, the one named last changes fastest.
Arguments:
- initial_thermal_state: float32 [1024, 512, 256], P('gx', 'gy', 'gz'), may hold values from -6 to 6
- thermal_spread_rate: float32 [1024, 512, 256], P('gx', 'gy', 'gz'), may hold values from 0.25 to 4
- yz_skew_factor: bfloat16 [1024, 512, 256], P('gx', 'gy', 'gz'), may hold values from -1 to 1
Outputs:
- known_source_vector: float32 [1024, 512, 256], P('gx', 'gy', 'gz')
- half_step: float32 [1024, 512, 256], P('gx', 'gy', 'gz')
All inputs are finite; a program needn't handle non-finite values.
Results may differ from a plain program's by a relative error of at most 0.0003.
Values sent between devices are 32-bit elements; how exact they have to be, the bound alone decides.
No kernel may reach another device: no remote copies, remote signals or barrier semaphores. Data moves between devices by JAX's collectives and lax.ppermute only.
A program may use at most 64 MiB of HBM per device.

v0:
```python
import functools

import jax
import jax.numpy as jnp
from jax import lax
from jax.experimental import pallas as pl
from jax.experimental.pallas import tpu as pltpu
from jax.sharding import PartitionSpec as P

ratio_x = 4096.0
ratio_y = 0.2
ratio_z = 0.2
ratio_mix = 0.25

NI, NJ, NK = 64, 32, 128
ROWS = NI * NJ
BLOCKS = 16
PLANES = 8
F32 = jnp.float32


def call(kernel, outs, n_in, flops, moved, name):
    spec = pl.BlockSpec(memory_space=pltpu.VMEM)
    return pl.pallas_call(
        kernel,
        out_shape=[jax.ShapeDtypeStruct(shape, F32) for shape in outs],
        in_specs=[spec] * n_in,
        out_specs=[spec] * len(outs),
        compiler_params=pltpu.CompilerParams(vmem_limit_bytes=24 * 1024 * 1024),
        cost_estimate=pl.CostEstimate(flops=flops, bytes_accessed=moved, transcendentals=0),
        name=name,
    )


def lanes():
    return lax.broadcasted_iota(jnp.int32, (NJ, NK), 1)


def rows():
    return lax.broadcasted_iota(jnp.int32, (NJ, NK), 0)


def pack_kernel(u_ref, k_ref, col_ref, low_ref, high_ref):
    turn = 1 - lax.axis_index("gz")
    lane = lanes()

    def layer(i, col):
        at = pl.ds(pl.multiple_of(i * NJ, NJ), NJ)
        u = pltpu.roll(u_ref[at, :], i + turn, 1)
        k = pltpu.roll(k_ref[at, :], (i + (NI + turn)) & (NK - 1), 1)
        col = jnp.where(lane == i, u, col)
        return jnp.where(lane == i + NI, k, col)

    def some(n, col):
        for m in range(8):
            col = layer(n * 8 + m, col)
        return col

    col_ref[...] = lax.fori_loop(0, NI // 8, some, jnp.zeros((NJ, NK), F32))
    for ref, row in ((low_ref, 0), (high_ref, NJ - 1)):
        ref[0:NI, :] = u_ref[pl.ds(row, NI, stride=NJ), :]
        ref[NI : 2 * NI, :] = k_ref[pl.ds(row, NI, stride=NJ), :]


def factor_kernel(k_ref, t_ref, q_ref, r_ref, plane_ref):
    half = 0.5 * ratio_x
    zero = jnp.zeros((NJ, NK), F32)
    one = jnp.ones((NJ, NK), F32)
    first = k_ref[0:NJ, :]
    last = k_ref[ROWS - NJ : ROWS, :]
    t_ref[0:NJ, :] = zero
    q_ref[0:NJ, :] = one
    r_ref[0:NJ, :] = zero
    t_ref[ROWS - NJ : ROWS, :] = zero
    q_ref[ROWS - NJ : ROWS, :] = zero
    r_ref[ROWS - NJ : ROWS, :] = zero

    def layer(i, state):
        here, ground, left, total = state
        at = pl.ds(pl.multiple_of(i * NJ, NJ), NJ)
        after = k_ref[pl.ds(pl.multiple_of(i * NJ + NJ, NJ), NJ), :]
        link = half * (here + after)
        r = 1.0 / ((ground + left) + link)
        t = link * r
        q = left * r
        t_ref[at, :] = t
        q_ref[at, :] = q
        r_ref[at, :] = r
        return after, 1.0 + t * ground, t * left, total + q * ground

    def some(n, state):
        for m in range(2):
            state = layer(1 + n * 2 + m, state)
        return state

    second = k_ref[NJ : 2 * NJ, :]
    start = (second, one, half * (first + second), one)
    _, ground, left, total = lax.fori_loop(0, (NI - 2) // 2, some, start)
    for c, plane in enumerate((total, left, ground, first, last)):
        plane_ref[c * NJ : c * NJ + NJ, :] = plane


def source_kernel(
    u_ref, k_ref, skew_ref, col_ref, below_ref, above_ref, t_ref, q_ref, r_ref, plane_ref,
    f_ref, b_ref, send_ref,
):
    right = lax.axis_index("gz") == 0
    lane, row = lanes(), rows()
    first_lane, last_lane = lane == 0, lane == NK - 1
    first_row, last_row = row == 0, row == NJ - 1
    far_l = jnp.where(right, 0.0, 1.0).astype(F32)
    far_r = jnp.where(right, 1.0, 0.0).astype(F32)

    wide = lax.broadcasted_iota(jnp.int32, (NI, NK), 1)
    deep = lax.broadcasted_iota(jnp.int32, (NI, NK), 0)
    slope = []
    for ref in (below_ref, above_ref):
        beyond = ref[0:NI, :]
        corner = jnp.sum(
            jnp.where(wide == deep, jnp.broadcast_to(ref[2 * NI : 2 * NI + 1, :], (NI, NK)), 0.0),
            axis=1, keepdims=True,
        )
        ahead = jnp.where(wide == NK - 1, corner * far_r, pltpu.roll(beyond, NK - 1, 1))
        back = jnp.where(wide == 0, corner * far_l, pltpu.roll(beyond, 1, 1))
        slope.append(ahead - back)

    def body_with(slope_refs):
        slope_refs[0][...] = slope[0]
        slope_refs[1][...] = slope[1]

        def layer(i, state):
            col, s, total = state
            at = pl.ds(pl.multiple_of(i * NJ, NJ), NJ)
            u, k = u_ref[at, :], k_ref[at, :]
            cu = jnp.broadcast_to(col[:, 0:1], (NJ, NK))
            ck = jnp.broadcast_to(col[:, NI : NI + 1], (NJ, NK))
            u_kp = jnp.where(last_lane, cu * far_r, pltpu.roll(u, NK - 1, 1))
            u_km = jnp.where(first_lane, cu * far_l, pltpu.roll(u, 1, 1))
            k_kp = jnp.where(last_lane, ck * far_r, pltpu.roll(k, NK - 1, 1))
            k_km = jnp.where(first_lane, ck * far_l, pltpu.roll(k, 1, 1))
            d = u_kp - u_km

            def beside(x, below, above):
                below = jnp.broadcast_to(below, (NJ, NK))
                above = jnp.broadcast_to(above, (NJ, NK))
                return (
                    jnp.where(first_row, below, pltpu.roll(x, 1, 0)),
                    jnp.where(last_row, above, pltpu.roll(x, NJ - 1, 0)),
                )

            one = pl.ds(i, 1)
            two = pl.ds(NI + i, 1)
            u_jm, u_jp = beside(u, below_ref[one, :], above_ref[one, :])
            k_jm, k_jp = beside(k, below_ref[two, :], above_ref[two, :])
            d_jm, d_jp = beside(d, slope_refs[0][one, :], slope_refs[1][one, :])
            flux_y = (k + k_jp) * (u_jp - u) - (k + k_jm) * (u - u_jm)
            flux_z = (k + k_kp) * (u_kp - u) - (k + k_km) * (u - u_km)
            f = (
                u
                + (0.5 * ratio_y) * flux_y
                + (0.5 * ratio_z) * flux_z
                + ratio_mix * skew_ref[i].astype(F32) * (d_jp - d_jm)
            )
            f_ref[at, :] = f
            s = f + s
            b_ref[at, :] = r_ref[at, :] * s
            total = total + q_ref[at, :] * s
            return pltpu.roll(col, NK - 1, 1), t_ref[at, :] * s, total, s

        def some(n, state):
            col, carried, total, s = state
            for m in range(2):
                col, carried, total, s = layer(n * 2 + m, (col, carried, total))
            return col, carried, total, s

        zero = jnp.zeros((NJ, NK), F32)
        _, _, total, s = lax.fori_loop(0, NI // 2, some, (col_ref[...], zero, zero, zero))
        planes = [plane_ref[c * NJ : c * NJ + NJ, :] for c in range(5)] + [total, s]
        half = NJ // 2
        for c, plane in enumerate(planes):
            send_ref[pl.ds(2 * c, half, stride=2 * PLANES), :] = plane[0:half]
            send_ref[pl.ds(2 * c + 1, half, stride=2 * PLANES), :] = plane[half:NJ]
        for c in range(2 * len(planes), 2 * PLANES):
            send_ref[pl.ds(c, half, stride=2 * PLANES), :] = zero[0:half]

    pl.run_scoped(
        lambda a, b: body_with((a, b)), pltpu.VMEM((NI, NK), F32), pltpu.VMEM((NI, NK), F32)
    )


def separator_kernel(got_ref, out_ref):
    half = 0.5 * ratio_x

    def plane(p, c):
        at = p * 2 * PLANES + 2 * c
        return got_ref[at : at + 2, :]

    def inner(p):
        return plane(p, 1)

    def link(p):
        return half * (plane(p, 4) + plane(p + 1, 3))

    middle = BLOCKS // 2
    left, right = [], []
    ground = plane(0, 0) + half * plane(0, 3)
    side = plane(0, 5)
    ground_r = plane(BLOCKS - 1, 2) + half * plane(BLOCKS - 1, 4)
    side_r = plane(BLOCKS - 1, 6)
    for m in range(middle):
        p, o = m, BLOCKS - 1 - m
        r = 1.0 / (ground + inner(p))
        t = inner(p) * r
        left.append((side * r, t))
        ground, side = plane(p, 2) + t * ground, plane(p, 6) + t * side
        r = 1.0 / (ground_r + inner(o))
        t = inner(o) * r
        right.append((side_r * r, t))
        ground_r, side_r = plane(o, 0) + t * ground_r, plane(o, 5) + t * side_r
        if m < middle - 1:
            r = 1.0 / (ground + link(p))
            t = link(p) * r
            left.append((side * r, t))
            ground, side = plane(p + 1, 0) + t * ground, plane(p + 1, 5) + t * side
            r = 1.0 / (ground_r + link(o - 1))
            t = link(o - 1) * r
            right.append((side_r * r, t))
            ground_r, side_r = plane(o - 1, 2) + t * ground_r, plane(o - 1, 6) + t * side_r
    joint = link(middle - 1)
    r = 1.0 / (ground + joint)
    t = joint * r
    left.append((side * r, t))
    value = (side_r + t * side) / (ground_r + t * ground)
    there = value
    values_r = [there]
    for b, t in reversed(right):
        there = b + t * there
        values_r.append(there)
    here = value
    values_l = []
    for b, t in reversed(left):
        here = b + t * here
        values_l.append(here)
    values = values_l[::-1] + values_r
    for n, v in enumerate(values):
        out_ref[2 * n : 2 * n + 2, :] = v


def back_kernel(v_ref, b_ref, t_ref, q_ref, w_ref):
    half = NJ // 2
    ends = []
    for c in range(2):
        ends.append(
            jnp.concatenate(
                [v_ref[pl.ds(2 * c, half, stride=4), :], v_ref[pl.ds(2 * c + 1, half, stride=4), :]]
            )
        )
    head, tail = ends
    w_ref[ROWS - NJ : ROWS, :] = tail

    def layer(i, w):
        at = pl.ds(pl.multiple_of(i * NJ, NJ), NJ)
        w = (b_ref[at, :] + q_ref[at, :] * head) + t_ref[at, :] * w
        w_ref[at, :] = w
        return w

    def some(n, w):
        for m in range(7):
            w = layer(NI - 2 - n * 7 - m, w)
        return w

    lax.fori_loop(0, (NI - 1) // 7, some, tail)


def body(initial_thermal_state, thermal_spread_rate, yz_skew_factor):
    u = initial_thermal_state.reshape(ROWS, NK)
    k = thermal_spread_rate.reshape(ROWS, NK)
    block = ROWS * NK
    col, low, high = call(
        pack_kernel, [(NJ, NK), (2 * NI, NK), (2 * NI, NK)], 2, block, 8 * block, "pack"
    )(u, k)
    got_col = lax.ppermute(col, "gz", [(0, 1), (1, 0)])
    t, q, r, planes = call(
        factor_kernel, [(ROWS, NK)] * 3 + [(5 * NJ, NK)], 1, 20 * block, 16 * block, "factor"
    )(k)
    ends = lax.axis_size("gy") - 1
    up = jnp.concatenate([high, jnp.broadcast_to(got_col[NJ - 1 :], (8, NK))])
    down = jnp.concatenate([low, jnp.broadcast_to(got_col[:1], (8, NK))])
    below = lax.ppermute(up, "gy", [(i, i + 1) for i in range(ends)])
    above = lax.ppermute(down, "gy", [(i + 1, i) for i in range(ends)])
    f, b, send = call(
        source_kernel, [(ROWS, NK)] * 2 + [(BLOCKS * 2 * PLANES, NK)], 10,
        50 * block, 32 * block, "source",
    )(u, k, yz_skew_factor, got_col, below, above, t, q, r, planes)
    got = lax.all_to_all(send, "gx", 0, 0, tiled=True)
    (values,) = call(
        separator_kernel, [(4 * BLOCKS, NK)], 1, block, block, "separator"
    )(got)
    mine = lax.all_to_all(values, "gx", 0, 0, tiled=True)
    (w,) = call(back_kernel, [(ROWS, NK)], 4, 4 * block, 16 * block, "back")(mine, b, t, q)
    shape = initial_thermal_state.shape
    return f.reshape(shape), w.reshape(shape)


def solution(mesh):
    spec = P("gx", "gy", "gz")
    return jax.shard_map(
        body, mesh=mesh, in_specs=(spec, spec, spec), out_specs=(spec, spec), check_vma=False
    )
```

profile of v0, /device:TPU:7, one launch (start us, length us, event | category | flops | bytes accessed | tf_op | source)
XLA Modules:
  0.0 61.0 jit_solution(3496297691494500601)
XLA Ops:
  0.6 0.0 copy-start
  0.6 1.2 %copy-done = f32[64,32,128]{2,1,0:T(8,128)S(1)} copy-done((f32[64,32,128]{2,1,0:T(8,128)S(1)}, f32[64,32,128]{2,1,0:T(8,128)}, u32[]{:S(2)}) %copy-start) | copy-done | bytes 1048600
  1.9 0.0 copy-start.2
  1.9 1.2 %copy-done.2 = f32[64,32,128]{2,1,0:T(8,128)S(1)} copy-done((f32[64,32,128]{2,1,0:T(8,128)S(1)}, f32[64,32,128]{2,1,0:T(8,128)}, u32[]{:S(2)}) %copy-start.2) | copy-done | bytes 1048600
  3.1 0.0 copy-start.1
  3.1 1.2 %pack.1 = (f32[32,128]{1,0:T(8,128)S(1)}, f32[128,128]{1,0:T(8,128)S(1)}, f32[128,128]{1,0:T(8,128)S(1)}) custom-call(f32[2048,128]{1,0:T(8,128)S(1)} %bitcast.15, f32[2048,128]{1,0:T(8,128)S(1)} %bitcast.12), custom_call_target="tpu_custom_call" | custom-call | flops 262144 | bytes 2097152 | tf_op jit(solution)/shard_map/pack/pallas_call | solution.py:279
  4.3 3.0 %collective-permute-start = (f32[32,128]{1,0:T(8,128)S(1)}, f32[32,128]{1,0:T(8,128)S(1)}, u32[]{:S(2)}, u32[]{:S(2)}) collective-permute-start(f32[32,128]{1,0:T(8,128)S(1)} %get-tuple-element.12), channel_id=1, source_target_pairs={{0,1},{1,0},{2,3},{3,2},{4,5},{5,4},{6,7},{7,6},{8,9},{9,8},{10,11... | collective-permute-start | bytes 49160 | tf_op jit(solution)/shard_map/ppermute | solution.py:282
  7.3 2.9 %collective-permute-done.col_ref = f32[32,128]{1,0:T(8,128)S(1)} collective-permute-done((f32[32,128]{1,0:T(8,128)S(1)}, f32[32,128]{1,0:T(8,128)S(1)}, u32[]{:S(2)}, u32[]{:S(2)}) %collective-permute-start) | collective-permute-done | bytes 16416 | tf_op jit(solution)/shard_map/ppermute | solution.py:282
  10.3 4.0 %collective-permute-start.1 = (f32[136,128]{1,0:T(8,128)S(1)}, f32[136,128]{1,0:T(8,128)S(1)}, u32[]{:S(2)}, u32[]{:S(2)}) collective-permute-start(f32[136,128]{1,0:T(8,128)S(1)} %pad_maximum_fusion), channel_id=1, source_target_pairs={{0,2},{2,4},{4,6},{6,8},{8,10},{10,12},{12,14},{14,16},{16,18},{18... | collective-permute-start | bytes 208904 | tf_op jit(solution)/shard_map/ppermute | solution.py:289
  14.3 0.0 copy-start.3
  14.3 9.0 %collective-permute-start.2 = (f32[136,128]{1,0:T(8,128)S(1)}, f32[136,128]{1,0:T(8,128)S(1)}, u32[]{:S(2)}, u32[]{:S(2)}) collective-permute-start(f32[136,128]{1,0:T(8,128)S(1)} %pad_maximum_fusion.1), channel_id=1, source_target_pairs={{2,0},{4,2},{6,4},{8,6},{10,8},{12,10},{14,12},{16,14},{18,16},{20... | collective-permute-start | bytes 208904 | tf_op jit(solution)/shard_map/ppermute | solution.py:290
  23.3 0.0 copy-done.1
  23.3 0.9 %factor.1 = (f32[2048,128]{1,0:T(8,128)S(1)}, f32[2048,128]{1,0:T(8,128)S(1)}, f32[2048,128]{1,0:T(8,128)S(1)}, f32[160,128]{1,0:T(8,128)S(1)}) custom-call(f32[2048,128]{1,0:T(8,128)S(1)} %bitcast.13), custom_call_target="tpu_custom_call" | custom-call | flops 5242880 | bytes 4194304 | tf_op jit(solution)/shard_map/factor/pallas_call | solution.py:283
  24.2 0.0 collective-permute-done.1.below_ref
  24.2 0.4 collective-permute-done.2.above_ref
  24.6 0.0 copy-done.3
  24.7 6.3 %source.1 = (f32[2048,128]{1,0:T(8,128)}, f32[2048,128]{1,0:T(8,128)S(1)}, f32[256,128]{1,0:T(8,128)S(1)}) custom-call(f32[2048,128]{1,0:T(8,128)S(1)} %bitcast.16, f32[2048,128]{1,0:T(8,128)S(1)} %bitcast.14, bf16[64,32,128]{2,1,0:T(8,128)(2,1)S(1)} %copy-done.3, f32[32,128]{1,0:T(8,128)S(1)} %collective-permute-done.col_ref, ...), custom_call_target="tpu_custom_call" | custom-call | flops 13107200 | bytes 8388608 | tf_op jit(solution)/shard_map/source/pallas_call | solution.py:291
  31.0 18.7 %all_to_all.22 = f32[16,16,128]{2,1,0:T(8,128)S(1)} all-to-all(f32[16,16,128]{2,1,0:T(8,128)S(1)} %bitcast.20), channel_id=1, replica_groups=mesh['gx'=16,'gy'=16,'gz'=2] {'gx'}, dimensions={0} | all-to-all | bytes 262144 | tf_op jit(solution)/shard_map/all_to_all | solution.py:295
  49.7 0.2 separator.1
  49.9 9.8 %all_to_all.23 = f32[16,4,128]{2,1,0:T(4,128)S(1)} all-to-all(f32[16,4,128]{2,1,0:T(4,128)S(1)} %bitcast.19), channel_id=1, replica_groups=mesh['gx'=16,'gy'=16,'gz'=2] {'gx'}, dimensions={0} | all-to-all | bytes 65536 | tf_op jit(solution)/shard_map/all_to_all | solution.py:299
  59.7 1.2 %back.1 = f32[2048,128]{1,0:T(8,128)} custom-call(f32[64,128]{1,0:T(8,128)S(1)} %bitcast.18, f32[2048,128]{1,0:T(8,128)S(1)} %get-tuple-element.21.b_ref, f32[2048,128]{1,0:T(8,128)S(1)} %get-tuple-element.15.t_ref, f32[2048,128]{1,0:T(8,128)S(1)} %get-tuple-element.16.q_ref), custom_call_target="tpu_custom_call" | custom-call | flops 1048576 | bytes 4194304 | tf_op jit(solution)/shard_map/back/pallas_call | solution.py:300
  (5 shorter events, 0.0 us)
Async XLA Ops:
  0.6 1.2 %copy-start = (f32[64,32,128]{2,1,0:T(8,128)S(1)}, f32[64,32,128]{2,1,0:T(8,128)}, u32[]{:S(2)}) copy-start(f32[64,32,128]{2,1,0:T(8,128)} %param.4) | copy-start | bytes 3145732
  1.9 1.2 %copy-start.2 = (f32[64,32,128]{2,1,0:T(8,128)S(1)}, f32[64,32,128]{2,1,0:T(8,128)}, u32[]{:S(2)}) copy-start(f32[64,32,128]{2,1,0:T(8,128)} %param.3) | copy-start | bytes 3145732
  3.1 20.2 %copy-start.1 = (f32[64,32,128]{2,1,0:T(8,128)S(1)}, f32[64,32,128]{2,1,0:T(8,128)}, u32[]{:S(2)}) copy-start(f32[64,32,128]{2,1,0:T(8,128)} %param.4) | copy-start | bytes 3145732
  4.3 6.0 %collective-permute-start = (f32[32,128]{1,0:T(8,128)S(1)}, f32[32,128]{1,0:T(8,128)S(1)}, u32[]{:S(2)}, u32[]{:S(2)}) collective-permute-start(f32[32,128]{1,0:T(8,128)S(1)} %get-tuple-element.12), channel_id=1, source_target_pairs={{0,1},{1,0},{2,3},{3,2},{4,5},{5,4},{6,7},{7,6},{8,9},{9,8},{10,11... | collective-permute-start | bytes 49160 | tf_op jit(solution)/shard_map/ppermute | solution.py:282
  10.3 13.9 %collective-permute-start.1 = (f32[136,128]{1,0:T(8,128)S(1)}, f32[136,128]{1,0:T(8,128)S(1)}, u32[]{:S(2)}, u32[]{:S(2)}) collective-permute-start(f32[136,128]{1,0:T(8,128)S(1)} %pad_maximum_fusion), channel_id=1, source_target_pairs={{0,2},{2,4},{4,6},{6,8},{8,10},{10,12},{12,14},{14,16},{16,18},{18... | collective-permute-start | bytes 208904 | tf_op jit(solution)/shard_map/ppermute | solution.py:289
  14.3 10.4 %copy-start.3 = (bf16[64,32,128]{2,1,0:T(8,128)(2,1)S(1)}, bf16[64,32,128]{2,1,0:T(8,128)(2,1)}, u32[]{:S(2)}) copy-start(bf16[64,32,128]{2,1,0:T(8,128)(2,1)} %skew_ref.1) | copy-start | bytes 1572868
  14.3 10.3 %collective-permute-start.2 = (f32[136,128]{1,0:T(8,128)S(1)}, f32[136,128]{1,0:T(8,128)S(1)}, u32[]{:S(2)}, u32[]{:S(2)}) collective-permute-start(f32[136,128]{1,0:T(8,128)S(1)} %pad_maximum_fusion.1), channel_id=1, source_target_pairs={{2,0},{4,2},{6,4},{8,6},{10,8},{12,10},{14,12},{16,14},{18,16},{20... | collective-permute-start | bytes 208904 | tf_op jit(solution)/shard_map/ppermute | solution.py:290
where the time goes:
time: 61.3 us; the launch traced here: 61 us
  blocking collectives  28.6 us (47%)
  starting transfers between devices  16 us (26%)
  Pallas kernels  9.82 us (16%)
  waiting for transfers between devices  3.38 us (6%)
  local copies, waits for them, and re-layouts  2.46 us (4%)
  between operations  0.72 us (1%)
    all_to_all x1, blocking collectives, body(): got = lax.all_to_all(send, 'gx', 0, 0, tiled=True)  18.7 us
    all_to_all x1, blocking collectives, body(): mine = lax.all_to_all(values, 'gx', 0, 0, tiled=True)  9.81 us
    ppermute x1, starting transfers between devices, body(): above = lax.ppermute(down, 'gy', [(i + 1, i) for i in range(ends)])  8.98 us
    pallas_call x1, Pallas kernels, body(): call(source_kernel, [(ROWS, NK)] * 2 + [(BLOCKS * 2 * PLANES, NK)], 10, 5...  6.33 us
    ppermute x1, starting transfers between devices, body(): below = lax.ppermute(up, 'gy', [(i, i + 1) for i in range(ends)])  4 us
    ppermute x1, starting transfers between devices, body(): got_col = lax.ppermute(col, 'gz', [(0, 1), (1, 0)])  3.03 us
    ppermute x1, waiting for transfers between devices, body(): got_col = lax.ppermute(col, 'gz', [(0, 1), (1, 0)])  2.95 us
    unnamed x8, local copies, waits for them, and re-layouts  2.45 us
  transfers between devices with their start and end apart: 3, of which 2 were waited for; matrix products, arithmetic and copies ran while one was open for 0% of the time, Pallas kernels for 1%

commit v1 on v0

v1 whole, which is shorter than its diff:
```python
import jax
import jax.numpy as jnp
from jax import lax
from jax.experimental import pallas as pl
from jax.experimental.pallas import tpu as pltpu
from jax.sharding import PartitionSpec as P

ratio_x = 4096.0
ratio_y = 0.2
ratio_z = 0.2
ratio_mix = 0.25

NI, NJ, NK = 64, 32, 128
ROWS = NI * NJ
BLOCKS = 16
PLANES = 8
F32 = jnp.float32


def call(kernel, outs, n_in, flops, moved, name):
    spec = pl.BlockSpec(memory_space=pltpu.VMEM)
    return pl.pallas_call(
        kernel,
        out_shape=[jax.ShapeDtypeStruct(shape, F32) for shape in outs],
        in_specs=[spec] * n_in,
        out_specs=[spec] * len(outs),
        compiler_params=pltpu.CompilerParams(vmem_limit_bytes=24 * 1024 * 1024),
        cost_estimate=pl.CostEstimate(flops=flops, bytes_accessed=moved, transcendentals=0),
        name=name,
    )


def lanes():
    return lax.broadcasted_iota(jnp.int32, (NJ, NK), 1)


def rows():
    return lax.broadcasted_iota(jnp.int32, (NJ, NK), 0)


def edge_kernel(u_ref, k_ref, first_ref, second_ref, sems):
    odd = lax.rem(lax.axis_index("gy"), 2)
    copies = []
    for n, (ref, row) in enumerate(((first_ref, odd * (NJ - 1)), (second_ref, (1 - odd) * (NJ - 1)))):
        for m, source in enumerate((u_ref, k_ref)):
            copies.append(
                pltpu.make_async_copy(
                    source.at[:, row, 0, :], ref.at[m * NI : m * NI + NI, :], sems.at[2 * n + m]
                )
            )
    for copy in copies:
        copy.start()
    for copy in copies:
        copy.wait()


def pack_kernel(u_ref, k_ref, skew_ref, col_ref, skew_col_ref, wide_ref):
    turn = 1 - lax.axis_index("gz")
    lane = lanes()

    def layer(i, state):
        col, skew_col = state
        at = pl.ds(pl.multiple_of(i * NJ, NJ), NJ)
        g = skew_ref[i].astype(F32)
        wide_ref[at, :] = g
        u = pltpu.roll(u_ref[at, :], i + turn, 1)
        k = pltpu.roll(k_ref[at, :], (i + (NI + turn)) & (NK - 1), 1)
        g = pltpu.roll(g, i + turn, 1)
        here = lane == i
        col = jnp.where(here, u, col)
        return jnp.where(lane == i + NI, k, col), jnp.where(here, g, skew_col)

    def some(n, state):
        for m in range(8):
            state = layer(n * 8 + m, state)
        return state

    zero = jnp.zeros((NJ, NK), F32)
    col, skew_col = lax.fori_loop(0, NI // 8, some, (zero, zero))
    col_ref[...] = col
    skew_col_ref[...] = skew_col


def factor_kernel(k_ref, t_ref, q_ref, r_ref, plane_ref):
    half = 0.5 * ratio_x
    zero = jnp.zeros((NJ, NK), F32)
    one = jnp.ones((NJ, NK), F32)
    first = k_ref[0:NJ, :]
    last = k_ref[ROWS - NJ : ROWS, :]
    t_ref[0:NJ, :] = zero
    q_ref[0:NJ, :] = one
    r_ref[0:NJ, :] = zero
    t_ref[ROWS - NJ : ROWS, :] = zero
    q_ref[ROWS - NJ : ROWS, :] = zero
    r_ref[ROWS - NJ : ROWS, :] = zero

    def layer(i, state):
        here, ground, left, total = state
        at = pl.ds(pl.multiple_of(i * NJ, NJ), NJ)
        after = k_ref[pl.ds(pl.multiple_of(i * NJ + NJ, NJ), NJ), :]
        link = half * (here + after)
        r = 1.0 / ((ground + left) + link)
        t = link * r
        q = left * r
        t_ref[at, :] = t
        q_ref[at, :] = q
        r_ref[at, :] = r
        return after, 1.0 + t * ground, t * left, total + q * ground

    def some(n, state):
        for m in range(2):
            state = layer(1 + n * 2 + m, state)
        return state

    second = k_ref[NJ : 2 * NJ, :]
    start = (second, one, half * (first + second), one)
    _, ground, left, total = lax.fori_loop(0, (NI - 2) // 2, some, start)
    for c, plane in enumerate((total, left, ground, first, last)):
        plane_ref[c * NJ : c * NJ + NJ, :] = plane


def beside(first_ref, second_ref, at):
    odd = lax.rem(lax.axis_index("gy"), 2) == 1
    first, second = first_ref[at, :], second_ref[at, :]
    return jnp.where(odd, second, first), jnp.where(odd, first, second)


def corner_kernel(first_ref, second_ref, col_ref, out_ref):
    edge = jnp.where(lax.axis_index("gz") == 0, NK - 1, 0)
    wide = lax.broadcasted_iota(jnp.int32, (NI, NK), 1)
    deep = lax.broadcasted_iota(jnp.int32, (NI, NK), 0)
    out_ref[0:NJ, :] = col_ref[...]
    out_ref[NJ : NJ + 8, :] = jnp.zeros((8, NK), F32)
    for n, beyond in enumerate(beside(first_ref, second_ref, slice(0, NI))):
        value = jnp.sum(jnp.where(wide == edge, beyond, 0.0), axis=1, keepdims=True)
        value = jnp.where(wide == deep, jnp.broadcast_to(value, (NI, NK)), 0.0)
        out_ref[NJ + n : NJ + n + 1, :] = jnp.sum(value, axis=0, keepdims=True)


def source_kernel(u_ref, k_ref, skew_ref, first_ref, second_ref, f_ref):
    lane = lax.broadcasted_iota(jnp.int32, (8, NK), 1)
    first_lane, last_lane = lane == 0, lane == NK - 1

    def slope(u):
        ahead = jnp.where(last_lane, 0.0, pltpu.roll(u, NK - 1, 1))
        back = jnp.where(first_lane, 0.0, pltpu.roll(u, 1, 1))
        return ahead, ahead - back

    def some(n, nothing):
        base = pl.multiple_of(n * (8 * NJ), 8 * NJ)
        near = pl.ds(pl.multiple_of(n * 8, 8), 8)
        deep = pl.ds(pl.multiple_of(NI + n * 8, 8), 8)
        u_below, u_above = beside(first_ref, second_ref, near)
        k_below, k_above = beside(first_ref, second_ref, deep)

        def tile(ref, j):
            return ref[pl.ds(base + j, 8, stride=NJ), :]

        u, k = tile(u_ref, 0), tile(k_ref, 0)
        _, d_before = slope(u_below)
        flux_before = (k + k_below) * (u - u_below)
        ahead, d = slope(u)
        for j in range(NJ):
            if j < NJ - 1:
                u_next, k_next = tile(u_ref, j + 1), tile(k_ref, j + 1)
            else:
                u_next, k_next = u_above, k_above
            ahead_next, d_next = slope(u_next)
            flux = (k + k_next) * (u_next - u)
            k_ahead = jnp.where(last_lane, 0.0, pltpu.roll(k, NK - 1, 1))
            across = (k + k_ahead) * (ahead - u)
            before = jnp.where(first_lane, k * u, pltpu.roll(across, 1, 1))
            f_ref[pl.ds(base + j, 8, stride=NJ), :] = (
                u
                + (0.5 * ratio_y) * (flux - flux_before)
                + (0.5 * ratio_z) * (across - before)
                + (ratio_mix * tile(skew_ref, j)) * (d_next - d_before)
            )
            u, k, ahead, flux_before, d_before, d = u_next, k_next, ahead_next, flux, d, d_next
        return nothing

    lax.fori_loop(0, NI // 8, some, 0)


def sweep_kernel(
    f0_ref, col_ref, skew_col_ref, got_ref, t_ref, q_ref, r_ref, plane_ref,
    f_ref, b_ref, send_ref,
):
    right = lax.axis_index("gz") == 0
    lane, row = lanes(), rows()
    own, far = col_ref[...], got_ref[0:NJ, :]
    own_k, far_k = pltpu.roll(own, NI, 1), pltpu.roll(far, NI, 1)
    below = jnp.broadcast_to(got_ref[NJ : NJ + 1, :], (NJ, NK))
    above = jnp.broadcast_to(got_ref[NJ + 1 : NJ + 2, :], (NJ, NK))
    up = jnp.where(row == NJ - 1, above, pltpu.roll(far, NJ - 1, 0))
    down = jnp.where(row == 0, below, pltpu.roll(far, 1, 0))
    sign = jnp.where(right, ratio_mix, -ratio_mix).astype(F32)
    extra = (0.5 * ratio_z) * (own_k * far + far_k * (far - own)) + (
        sign * skew_col_ref[...]
    ) * (up - down)
    edge = lane == jnp.where(right, NK - 1, 0)
    extra = pltpu.roll(extra, jnp.where(right, NK - 1, 0), 1)

    def layer(i, state):
        extra, s, total = state
        at = pl.ds(pl.multiple_of(i * NJ, NJ), NJ)
        f = f0_ref[at, :] + jnp.where(edge, extra, 0.0)
        f_ref[at, :] = f
        s = f + s
        b_ref[at, :] = r_ref[at, :] * s
        total = total + q_ref[at, :] * s
        return pltpu.roll(extra, NK - 1, 1), t_ref[at, :] * s, total, s

    def some(n, state):
        extra, carried, total, s = state
        for m in range(4):
            extra, carried, total, s = layer(n * 4 + m, (extra, carried, total))
        return extra, carried, total, s

    zero = jnp.zeros((NJ, NK), F32)
    _, _, total, s = lax.fori_loop(0, NI // 4, some, (extra, zero, zero, zero))
    planes = [plane_ref[c * NJ : c * NJ + NJ, :] for c in range(5)] + [total, s]
    half = NJ // 2
    for c, plane in enumerate(planes):
        send_ref[pl.ds(2 * c, half, stride=2 * PLANES), :] = plane[0:half]
        send_ref[pl.ds(2 * c + 1, half, stride=2 * PLANES), :] = plane[half:NJ]
    for c in range(2 * len(planes), 2 * PLANES):
        send_ref[pl.ds(c, half, stride=2 * PLANES), :] = zero[0:half]


def separator_kernel(got_ref, out_ref):
    half = 0.5 * ratio_x

    def plane(p, c):
        at = p * 2 * PLANES + 2 * c
        return got_ref[at : at + 2, :]

    def inner(p):
        return plane(p, 1)

    def link(p):
        return half * (plane(p, 4) + plane(p + 1, 3))

    middle = BLOCKS // 2
    left, right = [], []
    ground = plane(0, 0) + half * plane(0, 3)
    side = plane(0, 5)
    ground_r = plane(BLOCKS - 1, 2) + half * plane(BLOCKS - 1, 4)
    side_r = plane(BLOCKS - 1, 6)
    for m in range(middle):
        p, o = m, BLOCKS - 1 - m
        r = 1.0 / (ground + inner(p))
        t = inner(p) * r
        left.append((side * r, t))
        ground, side = plane(p, 2) + t * ground, plane(p, 6) + t * side
        r = 1.0 / (ground_r + inner(o))
        t = inner(o) * r
        right.append((side_r * r, t))
        ground_r, side_r = plane(o, 0) + t * ground_r, plane(o, 5) + t * side_r
        if m < middle - 1:
            r = 1.0 / (ground + link(p))
            t = link(p) * r
            left.append((side * r, t))
            ground, side = plane(p + 1, 0) + t * ground, plane(p + 1, 5) + t * side
            r = 1.0 / (ground_r + link(o - 1))
            t = link(o - 1) * r
            right.append((side_r * r, t))
            ground_r, side_r = plane(o - 1, 2) + t * ground_r, plane(o - 1, 6) + t * side_r
    joint = link(middle - 1)
    r = 1.0 / (ground + joint)
    t = joint * r
    left.append((side * r, t))
    value = (side_r + t * side) / (ground_r + t * ground)
    there = value
    values_r = [there]
    for b, t in reversed(right):
        there = b + t * there
        values_r.append(there)
    here = value
    values_l = []
    for b, t in reversed(left):
        here = b + t * here
        values_l.append(here)
    values = values_l[::-1] + values_r
    for n, v in enumerate(values):
        out_ref[2 * n : 2 * n + 2, :] = v


def back_kernel(v_ref, b_ref, t_ref, q_ref, w_ref):
    half = NJ // 2
    ends = []
    for c in range(2):
        ends.append(
            jnp.concatenate(
                [v_ref[pl.ds(2 * c, half, stride=4), :], v_ref[pl.ds(2 * c + 1, half, stride=4), :]]
            )
        )
    head, tail = ends
    w_ref[ROWS - NJ : ROWS, :] = tail

    def layer(i, w):
        at = pl.ds(pl.multiple_of(i * NJ, NJ), NJ)
        w = (b_ref[at, :] + q_ref[at, :] * head) + t_ref[at, :] * w
        w_ref[at, :] = w
        return w

    def some(n, w):
        for m in range(7):
            w = layer(NI - 2 - n * 7 - m, w)
        return w

    lax.fori_loop(0, (NI - 1) // 7, some, tail)


def body(initial_thermal_state, thermal_spread_rate, yz_skew_factor):
    u = initial_thermal_state.reshape(ROWS, NK)
    k = thermal_spread_rate.reshape(ROWS, NK)
    block = ROWS * NK
    single = (NI, NJ, 1, NK)
    anywhere = pl.BlockSpec(memory_space=pltpu.HBM)
    whole = pl.BlockSpec(memory_space=pltpu.VMEM)
    to_first, to_second = pl.pallas_call(
        edge_kernel,
        out_shape=[jax.ShapeDtypeStruct((2 * NI, NK), F32)] * 2,
        in_specs=[anywhere] * 2,
        out_specs=[whole] * 2,
        scratch_shapes=[pltpu.SemaphoreType.DMA((4,))],
        compiler_params=pltpu.CompilerParams(vmem_limit_bytes=56 * 1024 * 1024),
        cost_estimate=pl.CostEstimate(flops=0, bytes_accessed=8 * NI * NK * 4, transcendentals=0),
        name="edges",
    )(initial_thermal_state.reshape(single), thermal_spread_rate.reshape(single))
    count = lax.axis_size("gy")
    odd_pairs = [(i, i + 1) for i in range(1, count - 1, 2)]
    even_pairs = [(i, i + 1) for i in range(0, count, 2)]
    first = lax.ppermute(to_first, "gy", [r for a, b in odd_pairs for r in ((a, b), (b, a))])
    second = lax.ppermute(to_second, "gy", [r for a, b in even_pairs for r in ((a, b), (b, a))])
    col, skew_col, skew = call(
        pack_kernel, [(NJ, NK)] * 2 + [(ROWS, NK)], 3, 3 * block, 10 * block, "pack"
    )(u, k, yz_skew_factor)
    t, q, r, planes = call(
        factor_kernel, [(ROWS, NK)] * 3 + [(5 * NJ, NK)], 1, 20 * block, 16 * block, "factor"
    )(k)
    (to_half,) = call(corner_kernel, [(NJ + 8, NK)], 3, NI * NK, 0, "corner")(first, second, col)
    got_col = lax.ppermute(to_half, "gz", [(0, 1), (1, 0)])
    (f0,) = call(source_kernel, [(ROWS, NK)], 5, 40 * block, 16 * block, "source")(
        u, k, skew, first, second
    )
    f, b, send = call(
        sweep_kernel, [(ROWS, NK)] * 2 + [(BLOCKS * 2 * PLANES, NK)], 8,
        8 * block, 24 * block, "sweep",
    )(f0, col, skew_col, got_col, t, q, r, planes)
    got = lax.all_to_all(send, "gx", 0, 0, tiled=True)
    (values,) = call(
        separator_kernel, [(4 * BLOCKS, NK)], 1, block, block, "separator"
    )(got)
    mine = lax.all_to_all(values, "gx", 0, 0, tiled=True)
    (w,) = call(back_kernel, [(ROWS, NK)], 4, 4 * block, 16 * block, "back")(mine, b, t, q)
    shape = initial_thermal_state.shape
    return f.reshape(shape), w.reshape(shape)


def solution(mesh):
    spec = P("gx", "gy", "gz")
    return jax.shard_map(
        body, mesh=mesh, in_specs=(spec, spec, spec), out_specs=(spec, spec), check_vma=False
    )
```

time: 61.3 us -> 61.5 us (level)
  Pallas kernels: 9.82 us -> 13.6 us
  waiting for transfers between devices: 3.38 us -> 1 us
  local copies, waits for them, and re-layouts: 2.46 us -> 1.05 us
    pallas_call x2 -> x5, Pallas kernels: 7.5 us -> 11.3 us  [the longest x1 5.48 us: body(): call(sweep_kernel, [(ROWS, NK)] * 2 + [(BLOCKS * 2 * PLANES, NK)], 8, 8 *...]
    ppermute x3, waiting for transfers between devices: 3.38 us -> 1 us  [the longest x1 1 us: body(): lax.ppermute(to_second, 'gy', [r for a, b in even_pairs for r in ((a, b),...]
    unnamed x8 -> x6, local copies, waits for them, and re-layouts: 2.45 us -> 1.05 us
  transfers between devices with their start and end apart: 3 -> 3, of which waited for: 2 -> 1; matrix products, arithmetic and copies ran while one was open for 0% -> 0% of each run, Pallas kernels for 1% -> 8%
where the time goes in v1:
time: 61.5 us; the launch traced here: 60.7 us
  blocking collectives  28.7 us (47%)
  starting transfers between devices  15.6 us (25%)
  Pallas kernels  13.6 us (22%)
  local copies, waits for them, and re-layouts  1.05 us (2%)
  waiting for transfers between devices  1 us (2%)
  between operations  0.75 us (1%)
    all_to_all x1, blocking collectives, body(): got = lax.all_to_all(send, 'gx', 0, 0, tiled=True)  18.9 us
    ppermute x1, starting transfers between devices, body(): lax.ppermute(to_first, 'gy', [r for a, b in odd_pairs for r in ((a, b), (...  10.9 us
    all_to_all x1, blocking collectives, body(): mine = lax.all_to_all(values, 'gx', 0, 0, tiled=True)  9.81 us
    pallas_call x1, Pallas kernels, body(): call(sweep_kernel, [(ROWS, NK)] * 2 + [(BLOCKS * 2 * PLANES, NK)], 8, 8 *...  5.48 us
    pallas_call x1, Pallas kernels, body(): call(source_kernel, [(ROWS, NK)], 5, 40 * block, 16 * block, 'source')  2.82 us
    ppermute x1, starting transfers between devices, body(): got_col = lax.ppermute(to_half, 'gz', [(0, 1), (1, 0)])  2.74 us
    ppermute x1, starting transfers between devices, body(): lax.ppermute(to_second, 'gy', [r for a, b in even_pairs for r in ((a, b),...  1.92 us
    pallas_call x1, Pallas kernels, body(): pl.pallas_call(edge_kernel, out_shape=[jax.ShapeDtypeStruct((2 * NI, NK),...  1.66 us
  transfers between devices with their start and end apart: 3, of which 1 were waited for; matrix products, arithmetic and copies ran while one was open for 0% of the time, Pallas kernels for 8%

profile of v1, /device:TPU:7, one launch (start us, length us, event | category | flops | bytes accessed | tf_op | source)
XLA Modules:
  0.0 60.7 jit_solution(12814916347669850419)
XLA Ops:
  0.6 0.0 copy-start
  0.6 0.0 copy-start.1
  0.6 1.7 %edges.1 = (f32[128,128]{1,0:T(8,128)}, f32[128,128]{1,0:T(8,128)}) custom-call(f32[64,32,1,128]{3,2,1,0:T(1,128)} %bitcast.14, f32[64,32,1,128]{3,2,1,0:T(1,128)} %bitcast.10), custom_call_target="tpu_custom_call" | custom-call | bytes 262144 | tf_op jit(solution)/shard_map/edges/pallas_call | solution.py:322
  2.3 10.9 %collective-permute-start = (f32[128,128]{1,0:T(8,128)}, f32[128,128]{1,0:T(8,128)S(1)}, u32[]{:S(2)}, u32[]{:S(2)}) collective-permute-start(f32[128,128]{1,0:T(8,128)} %get-tuple-element.15), channel_id=1, source_target_pairs={{2,4},{4,2},{6,8},{8,6},{10,12},{12,10},{14,16},{16,14},{18,20},{2... | collective-permute-start | bytes 196616 | tf_op jit(solution)/shard_map/ppermute | solution.py:335
  13.3 1.9 %collective-permute-start.1 = (f32[128,128]{1,0:T(8,128)}, f32[128,128]{1,0:T(8,128)S(1)}, u32[]{:S(2)}, u32[]{:S(2)}) collective-permute-start(f32[128,128]{1,0:T(8,128)} %get-tuple-element.16), channel_id=1, source_target_pairs={{0,2},{2,0},{4,6},{6,4},{8,10},{10,8},{12,14},{14,12},{16,18},{18,... | collective-permute-start | bytes 196616 | tf_op jit(solution)/shard_map/ppermute | solution.py:336
  15.2 0.0 copy-done
  15.2 0.0 copy-done.1
  15.2 0.0 copy-start.2
  15.2 1.0 %copy-done.2 = bf16[64,32,128]{2,1,0:T(8,128)(2,1)S(1)} copy-done((bf16[64,32,128]{2,1,0:T(8,128)(2,1)S(1)}, bf16[64,32,128]{2,1,0:T(8,128)(2,1)}, u32[]{:S(2)}) %copy-start.2) | copy-done | bytes 524312
  16.2 1.2 %pack.1 = (f32[32,128]{1,0:T(8,128)S(1)}, f32[32,128]{1,0:T(8,128)S(1)}, f32[2048,128]{1,0:T(8,128)S(1)}) custom-call(f32[2048,128]{1,0:T(8,128)S(1)} %bitcast.15, f32[2048,128]{1,0:T(8,128)S(1)} %bitcast.11, bf16[64,32,128]{2,1,0:T(8,128)(2,1)S(1)} %copy-done.2), custom_call_target="tpu_custom_call" | custom-call | flops 786432 | bytes 2621440 | tf_op jit(solution)/shard_map/pack/pallas_call | solution.py:337
  17.5 0.0 collective-permute-done.first_ref
  17.5 1.0 %collective-permute-done.1.second_ref = f32[128,128]{1,0:T(8,128)S(1)} collective-permute-done((f32[128,128]{1,0:T(8,128)}, f32[128,128]{1,0:T(8,128)S(1)}, u32[]{:S(2)}, u32[]{:S(2)}) %collective-permute-start.1) | collective-permute-done | bytes 65568 | tf_op jit(solution)/shard_map/ppermute | solution.py:336
  18.5 0.1 corner.1
  18.6 2.7 %collective-permute-start.2 = (f32[40,128]{1,0:T(8,128)S(1)}, f32[40,128]{1,0:T(8,128)S(1)}, u32[]{:S(2)}, u32[]{:S(2)}) collective-permute-start(f32[40,128]{1,0:T(8,128)S(1)} %corner.1), channel_id=1, source_target_pairs={{0,1},{1,0},{2,3},{3,2},{4,5},{5,4},{6,7},{7,6},{8,9},{9,8},{10,11... | collective-permute-start | bytes 61448 | tf_op jit(solution)/shard_map/ppermute | solution.py:344
  21.3 0.9 %factor.1 = (f32[2048,128]{1,0:T(8,128)S(1)}, f32[2048,128]{1,0:T(8,128)S(1)}, f32[2048,128]{1,0:T(8,128)S(1)}, f32[160,128]{1,0:T(8,128)S(1)}) custom-call(f32[2048,128]{1,0:T(8,128)S(1)} %bitcast.12), custom_call_target="tpu_custom_call" | custom-call | flops 5242880 | bytes 4194304 | tf_op jit(solution)/shard_map/factor/pallas_call | solution.py:340
  22.2 2.8 %source.1.f0_ref = f32[2048,128]{1,0:T(8,128)S(1)} custom-call(f32[2048,128]{1,0:T(8,128)S(1)} %bitcast.16, f32[2048,128]{1,0:T(8,128)S(1)} %bitcast.13, f32[2048,128]{1,0:T(8,128)S(1)} %get-tuple-element.14.skew_ref, f32[128,128]{1,0:T(8,128)S(1)} %collective-permute-done.first_ref, f32[128,128]{1,0:T(8,128)S(1)} %collective-permute-done.1.second_ref), custom_call_target="tpu_custom_call" | custom-call | flops 10485760 | bytes 4194304 | tf_op jit(solution)/shard_map/source/pallas_call | solution.py:345
  25.1 0.0 collective-permute-done.2.got_ref
  25.1 5.5 %sweep.1 = (f32[2048,128]{1,0:T(8,128)}, f32[2048,128]{1,0:T(8,128)S(1)}, f32[256,128]{1,0:T(8,128)S(1)}) custom-call(f32[2048,128]{1,0:T(8,128)S(1)} %source.1.f0_ref, f32[32,128]{1,0:T(8,128)S(1)} %get-tuple-element.17.col_ref, f32[32,128]{1,0:T(8,128)S(1)} %get-tuple-element.18.skew_col_ref, f32[40,128]{1,0:T(8,128)S(1)} %collective-permute-done.2.got_ref, ...), custom_call_target="tpu_custom_call" | custom-call | flops 2097152 | bytes 6291456 | tf_op jit(solution)/shard_map/sweep/pallas_call | solution.py:348
  30.5 18.9 %all_to_all.22 = f32[16,16,128]{2,1,0:T(8,128)S(1)} all-to-all(f32[16,16,128]{2,1,0:T(8,128)S(1)} %bitcast.20), channel_id=1, replica_groups=mesh['gx'=16,'gy'=16,'gz'=2] {'gx'}, dimensions={0} | all-to-all | bytes 262144 | tf_op jit(solution)/shard_map/all_to_all | solution.py:352
  49.4 0.2 separator.1
  49.6 9.8 %all_to_all.23 = f32[16,4,128]{2,1,0:T(4,128)S(1)} all-to-all(f32[16,4,128]{2,1,0:T(4,128)S(1)} %bitcast.19), channel_id=1, replica_groups=mesh['gx'=16,'gy'=16,'gz'=2] {'gx'}, dimensions={0} | all-to-all | bytes 65536 | tf_op jit(solution)/shard_map/all_to_all | solution.py:356
  59.4 1.2 %back.1 = f32[2048,128]{1,0:T(8,128)} custom-call(f32[64,128]{1,0:T(8,128)S(1)} %bitcast.18, f32[2048,128]{1,0:T(8,128)S(1)} %get-tuple-element.25.b_ref, f32[2048,128]{1,0:T(8,128)S(1)} %get-tuple-element.19.t_ref, f32[2048,128]{1,0:T(8,128)S(1)} %get-tuple-element.20.q_ref), custom_call_target="tpu_custom_call" | custom-call | flops 1048576 | bytes 4194304 | tf_op jit(solution)/shard_map/back/pallas_call | solution.py:357
Async XLA Ops:
  0.6 14.6 %copy-start = (f32[64,32,128]{2,1,0:T(8,128)S(1)}, f32[64,32,128]{2,1,0:T(8,128)}, u32[]{:S(2)}) copy-start(f32[64,32,128]{2,1,0:T(8,128)} %param.4) | copy-start | bytes 3145732
  0.6 14.6 %copy-start.1 = (f32[64,32,128]{2,1,0:T(8,128)S(1)}, f32[64,32,128]{2,1,0:T(8,128)}, u32[]{:S(2)}) copy-start(f32[64,32,128]{2,1,0:T(8,128)} %param.3) | copy-start | bytes 3145732
  2.3 15.2 %collective-permute-start = (f32[128,128]{1,0:T(8,128)}, f32[128,128]{1,0:T(8,128)S(1)}, u32[]{:S(2)}, u32[]{:S(2)}) collective-permute-start(f32[128,128]{1,0:T(8,128)} %get-tuple-element.15), channel_id=1, source_target_pairs={{2,4},{4,2},{6,8},{8,6},{10,12},{12,10},{14,16},{16,14},{18,20},{2... | collective-permute-start | bytes 196616 | tf_op jit(solution)/shard_map/ppermute | solution.py:335
  13.3 5.2 %collective-permute-start.1 = (f32[128,128]{1,0:T(8,128)}, f32[128,128]{1,0:T(8,128)S(1)}, u32[]{:S(2)}, u32[]{:S(2)}) collective-permute-start(f32[128,128]{1,0:T(8,128)} %get-tuple-element.16), channel_id=1, source_target_pairs={{0,2},{2,0},{4,6},{6,4},{8,10},{10,8},{12,14},{14,12},{16,18},{18,... | collective-permute-start | bytes 196616 | tf_op jit(solution)/shard_map/ppermute | solution.py:336
  15.2 1.0 %copy-start.2 = (bf16[64,32,128]{2,1,0:T(8,128)(2,1)S(1)}, bf16[64,32,128]{2,1,0:T(8,128)(2,1)}, u32[]{:S(2)}) copy-start(bf16[64,32,128]{2,1,0:T(8,128)(2,1)} %skew_ref.1) | copy-start | bytes 1572868
  18.6 6.5 %collective-permute-start.2 = (f32[40,128]{1,0:T(8,128)S(1)}, f32[40,128]{1,0:T(8,128)S(1)}, u32[]{:S(2)}, u32[]{:S(2)}) collective-permute-start(f32[40,128]{1,0:T(8,128)S(1)} %corner.1), channel_id=1, source_target_pairs={{0,1},{1,0},{2,3},{3,2},{4,5},{5,4},{6,7},{7,6},{8,9},{9,8},{10,11... | collective-permute-start | bytes 61448 | tf_op jit(solution)/shard_map/ppermute | solution.py:344

commit v2 on v1

--- a/solution.py
+++ b/solution.py
@@ -14,16 +14,23 @@
 ROWS = NI * NJ
 BLOCKS = 16
 PLANES = 8
+PART = 512
 F32 = jnp.float32
 
 
-def call(kernel, outs, n_in, flops, moved, name):
+def call(kernel, outs, n_in, flops, moved, name, leaving=False):
     spec = pl.BlockSpec(memory_space=pltpu.VMEM)
+    out_specs = [spec] * len(outs)
+    scratch = []
+    if leaving:
+        out_specs[0] = pl.BlockSpec(memory_space=pl.ANY)
+        scratch = [pltpu.VMEM(outs[0], F32), pltpu.SemaphoreType.DMA((ROWS // PART,))]
     return pl.pallas_call(
         kernel,
         out_shape=[jax.ShapeDtypeStruct(shape, F32) for shape in outs],
         in_specs=[spec] * n_in,
-        out_specs=[spec] * len(outs),
+        out_specs=out_specs,
+        scratch_shapes=scratch,
         compiler_params=pltpu.CompilerParams(vmem_limit_bytes=24 * 1024 * 1024),
         cost_estimate=pl.CostEstimate(flops=flops, bytes_accessed=moved, transcendentals=0),
         name=name,
@@ -41,7 +48,7 @@
 def edge_kernel(u_ref, k_ref, first_ref, second_ref, sems):
     odd = lax.rem(lax.axis_index("gy"), 2)
     copies = []
-    for n, (ref, row) in enumerate(((first_ref, odd * (NJ - 1)), (second_ref, (1 - odd) * (NJ - 1)))):
+    for n, (ref, row) in enumerate(((first_ref, (1 - odd) * (NJ - 1)), (second_ref, odd * (NJ - 1)))):
         for m, source in enumerate((u_ref, k_ref)):
             copies.append(
                 pltpu.make_async_copy(
@@ -54,34 +61,40 @@
         copy.wait()
 
 
-def pack_kernel(u_ref, k_ref, skew_ref, col_ref, skew_col_ref, wide_ref):
+def pack_kernel(u_ref, k_ref, col_ref):
     turn = 1 - lax.axis_index("gz")
     lane = lanes()
 
-    def layer(i, state):
-        col, skew_col = state
+    def layer(i, col):
         at = pl.ds(pl.multiple_of(i * NJ, NJ), NJ)
-        g = skew_ref[i].astype(F32)
-        wide_ref[at, :] = g
         u = pltpu.roll(u_ref[at, :], i + turn, 1)
         k = pltpu.roll(k_ref[at, :], (i + (NI + turn)) & (NK - 1), 1)
-        g = pltpu.roll(g, i + turn, 1)
-        here = lane == i
-        col = jnp.where(here, u, col)
-        return jnp.where(lane == i + NI, k, col), jnp.where(here, g, skew_col)
-
-    def some(n, state):
+        col = jnp.where(lane == i, u, col)
+        return jnp.where(lane == i + NI, k, col)
+
+    def some(n, col):
         for m in range(8):
-            state = layer(n * 8 + m, state)
-        return state
-
-    zero = jnp.zeros((NJ, NK), F32)
-    col, skew_col = lax.fori_loop(0, NI // 8, some, (zero, zero))
-    col_ref[...] = col
-    skew_col_ref[...] = skew_col
-
-
-def factor_kernel(k_ref, t_ref, q_ref, r_ref, plane_ref):
+            col = layer(n * 8 + m, col)
+        return col
+
+    col_ref[...] = lax.fori_loop(0, NI // 8, some, jnp.zeros((NJ, NK), F32))
+
+
+def factor_kernel(k_ref, skew_ref, t_ref, q_ref, r_ref, plane_ref, skew_col_ref, wide_ref):
+    turn = 1 - lax.axis_index("gz")
+    lane = lanes()
+
+    def skew(i, col):
+        g = skew_ref[i].astype(F32)
+        wide_ref[pl.ds(pl.multiple_of(i * NJ, NJ), NJ), :] = g
+        return jnp.where(lane == i, pltpu.roll(g, i + turn, 1), col)
+
+    def skews(n, col):
+        for m in range(8):
+            col = skew(n * 8 + m, col)
+        return col
+
+    skew_col_ref[...] = lax.fori_loop(0, NI // 8, skews, jnp.zeros((NJ, NK), F32))
     half = 0.5 * ratio_x
     zero = jnp.zeros((NJ, NK), F32)
     one = jnp.ones((NJ, NK), F32)
@@ -122,7 +135,7 @@
 def beside(first_ref, second_ref, at):
     odd = lax.rem(lax.axis_index("gy"), 2) == 1
     first, second = first_ref[at, :], second_ref[at, :]
-    return jnp.where(odd, second, first), jnp.where(odd, first, second)
+    return jnp.where(odd, first, second), jnp.where(odd, second, first)
 
 
 def corner_kernel(first_ref, second_ref, col_ref, out_ref):
@@ -184,7 +197,7 @@
 
 def sweep_kernel(
     f0_ref, col_ref, skew_col_ref, got_ref, t_ref, q_ref, r_ref, plane_ref,
-    f_ref, b_ref, send_ref,
+    f_out, b_ref, send_ref, f_ref, sems,
 ):
     right = lax.axis_index("gz") == 0
     lane, row = lanes(), rows()
@@ -199,26 +212,32 @@
         sign * skew_col_ref[...]
     ) * (up - down)
     edge = lane == jnp.where(right, NK - 1, 0)
-    extra = pltpu.roll(extra, jnp.where(right, NK - 1, 0), 1)
+    turn = jnp.where(right, NK - 1, NK)
 
     def layer(i, state):
-        extra, s, total = state
+        s, total = state
         at = pl.ds(pl.multiple_of(i * NJ, NJ), NJ)
-        f = f0_ref[at, :] + jnp.where(edge, extra, 0.0)
+        here = pltpu.roll(extra, (turn - i) & (NK - 1), 1)
+        f = f0_ref[at, :] + jnp.where(edge, here, 0.0)
         f_ref[at, :] = f
         s = f + s
         b_ref[at, :] = r_ref[at, :] * s
         total = total + q_ref[at, :] * s
-        return pltpu.roll(extra, NK - 1, 1), t_ref[at, :] * s, total, s
+        return t_ref[at, :] * s, total, s
+
+    def leave(n):
+        at = pl.ds(pl.multiple_of(n * PART, PART), PART)
+        return pltpu.make_async_copy(f_ref.at[at, :], f_out.at[at, :], sems.at[n])
 
     def some(n, state):
-        extra, carried, total, s = state
-        for m in range(4):
-            extra, carried, total, s = layer(n * 4 + m, (extra, carried, total))
-        return extra, carried, total, s
+        carried, total, s = state
+        for m in range(PART // NJ):
+            carried, total, s = layer(n * (PART // NJ) + m, (carried, total))
+        leave(n).start()
+        return carried, total, s
 
     zero = jnp.zeros((NJ, NK), F32)
-    _, _, total, s = lax.fori_loop(0, NI // 4, some, (extra, zero, zero, zero))
+    _, total, s = lax.fori_loop(0, ROWS // PART, some, (zero, zero, zero))
     planes = [plane_ref[c * NJ : c * NJ + NJ, :] for c in range(5)] + [total, s]
     half = NJ // 2
     for c, plane in enumerate(planes):
@@ -226,6 +245,8 @@
         send_ref[pl.ds(2 * c + 1, half, stride=2 * PLANES), :] = plane[half:NJ]
     for c in range(2 * len(planes), 2 * PLANES):
         send_ref[pl.ds(c, half, stride=2 * PLANES), :] = zero[0:half]
+    for n in range(ROWS // PART):
+        leave(n).wait()
 
 
 def separator_kernel(got_ref, out_ref):
@@ -286,7 +307,7 @@
         out_ref[2 * n : 2 * n + 2, :] = v
 
 
-def back_kernel(v_ref, b_ref, t_ref, q_ref, w_ref):
+def back_kernel(v_ref, b_ref, t_ref, q_ref, w_out, w_ref, sems):
     half = NJ // 2
     ends = []
     for c in range(2):
@@ -296,20 +317,23 @@
             )
         )
     head, tail = ends
-    w_ref[ROWS - NJ : ROWS, :] = tail
-
     def layer(i, w):
-        at = pl.ds(pl.multiple_of(i * NJ, NJ), NJ)
+        at = pl.ds(i * NJ, NJ)
         w = (b_ref[at, :] + q_ref[at, :] * head) + t_ref[at, :] * w
         w_ref[at, :] = w
         return w
 
-    def some(n, w):
-        for m in range(7):
-            w = layer(NI - 2 - n * 7 - m, w)
-        return w
-
-    lax.fori_loop(0, (NI - 1) // 7, some, tail)
+    w_ref[ROWS - NJ : ROWS, :] = tail
+    w = tail
+    copies = []
+    for n in reversed(range(ROWS // PART)):
+        for i in reversed(range(n * (PART // NJ), min((n + 1) * (PART // NJ), NI - 1))):
+            w = layer(i, w)
+        at = pl.ds(n * PART, PART)
+        copies.append(pltpu.make_async_copy(w_ref.at[at, :], w_out.at[at, :], sems.at[n]))
+        copies[-1].start()
+    for copy in copies:
+        copy.wait()
 
 
 def body(initial_thermal_state, thermal_spread_rate, yz_skew_factor):
@@ -332,14 +356,13 @@
     count = lax.axis_size("gy")
     odd_pairs = [(i, i + 1) for i in range(1, count - 1, 2)]
     even_pairs = [(i, i + 1) for i in range(0, count, 2)]
-    first = lax.ppermute(to_first, "gy", [r for a, b in odd_pairs for r in ((a, b), (b, a))])
-    second = lax.ppermute(to_second, "gy", [r for a, b in even_pairs for r in ((a, b), (b, a))])
-    col, skew_col, skew = call(
-        pack_kernel, [(NJ, NK)] * 2 + [(ROWS, NK)], 3, 3 * block, 10 * block, "pack"
-    )(u, k, yz_skew_factor)
-    t, q, r, planes = call(
-        factor_kernel, [(ROWS, NK)] * 3 + [(5 * NJ, NK)], 1, 20 * block, 16 * block, "factor"
-    )(k)
+    first = lax.ppermute(to_first, "gy", [r for a, b in even_pairs for r in ((a, b), (b, a))])
+    second = lax.ppermute(to_second, "gy", [r for a, b in odd_pairs for r in ((a, b), (b, a))])
+    (col,) = call(pack_kernel, [(NJ, NK)], 2, 3 * block, 8 * block, "pack")(u, k)
+    t, q, r, planes, skew_col, skew = call(
+        factor_kernel, [(ROWS, NK)] * 3 + [(5 * NJ, NK), (NJ, NK), (ROWS, NK)], 2,
+        20 * block, 22 * block, "factor",
+    )(k, yz_skew_factor)
     (to_half,) = call(corner_kernel, [(NJ + 8, NK)], 3, NI * NK, 0, "corner")(first, second, col)
     got_col = lax.ppermute(to_half, "gz", [(0, 1), (1, 0)])
     (f0,) = call(source_kernel, [(ROWS, NK)], 5, 40 * block, 16 * block, "source")(
@@ -347,14 +370,14 @@
     )
     f, b, send = call(
         sweep_kernel, [(ROWS, NK)] * 2 + [(BLOCKS * 2 * PLANES, NK)], 8,
-        8 * block, 24 * block, "sweep",
+        8 * block, 24 * block, "sweep", True,
     )(f0, col, skew_col, got_col, t, q, r, planes)
     got = lax.all_to_all(send, "gx", 0, 0, tiled=True)
     (values,) = call(
         separator_kernel, [(4 * BLOCKS, NK)], 1, block, block, "separator"
     )(got)
     mine = lax.all_to_all(values, "gx", 0, 0, tiled=True)
-    (w,) = call(back_kernel, [(ROWS, NK)], 4, 4 * block, 16 * block, "back")(mine, b, t, q)
+    (w,) = call(back_kernel, [(ROWS, NK)], 4, 4 * block, 16 * block, "back", True)(mine, b, t, q)
     shape = initial_thermal_state.shape
     return f.reshape(shape), w.reshape(shape)
 

time: 61.5 us -> 56.5 us (0.919)
  the two profiles are of different devices: /device:TPU:7 before, /device:TPU:3 now
where the time goes in v2:
time: 56.5 us; the launch traced here: 56.2 us
  blocking collectives  28 us (50%)
  starting transfers between devices  16.9 us (30%)
  Pallas kernels  9.84 us (17%)
  between operations  0.76 us (1%)
  waiting for transfers between devices  0.73 us (1%)
    all_to_all x1, blocking collectives, body(): got = lax.all_to_all(send, 'gx', 0, 0, tiled=True)  18.2 us
    all_to_all x1, blocking collectives, body(): mine = lax.all_to_all(values, 'gx', 0, 0, tiled=True)  9.81 us
    ppermute x1, starting transfers between devices, body(): lax.ppermute(to_second, 'gy', [r for a, b in odd_pairs for r in ((a, b),...  8.82 us
    ppermute x1, starting transfers between devices, body(): got_col = lax.ppermute(to_half, 'gz', [(0, 1), (1, 0)])  4.05 us
    ppermute x1, starting transfers between devices, body(): lax.ppermute(to_first, 'gy', [r for a, b in even_pairs for r in ((a, b),...  4 us
    pallas_call x1, Pallas kernels, body(): call(source_kernel, [(ROWS, NK)], 5, 40 * block, 16 * block, 'source')  2.82 us
    pallas_call x1, Pallas kernels, body(): pl.pallas_call(edge_kernel, out_shape=[jax.ShapeDtypeStruct((2 * NI, NK),...  1.66 us
    pallas_call x1, Pallas kernels, body(): call(factor_kernel, [(ROWS, NK)] * 3 + [(5 * NJ, NK), (NJ, NK), (ROWS, NK...  1.58 us
  transfers between devices with their start and end apart: 3, of which 1 were waited for; matrix products, arithmetic and copies ran while one was open for 0% of the time, Pallas kernels for 10%

profile of v2, /device:TPU:3, one launch (start us, length us, event | category | flops | bytes accessed | tf_op | source)
XLA Modules:
  0.0 56.2 jit_solution(8302851248821135545)
XLA Ops:
  0.6 0.0 copy-start
  0.6 0.0 copy-start.1
  0.6 1.7 %edges.1 = (f32[128,128]{1,0:T(8,128)}, f32[128,128]{1,0:T(8,128)}) custom-call(f32[64,32,1,128]{3,2,1,0:T(1,128)} %bitcast.14, f32[64,32,1,128]{3,2,1,0:T(1,128)} %bitcast.10), custom_call_target="tpu_custom_call" | custom-call | bytes 262144 | tf_op jit(solution)/shard_map/edges/pallas_call | solution.py:346
  2.3 4.0 %collective-permute-start = (f32[128,128]{1,0:T(8,128)}, f32[128,128]{1,0:T(8,128)S(1)}, u32[]{:S(2)}, u32[]{:S(2)}) collective-permute-start(f32[128,128]{1,0:T(8,128)} %get-tuple-element.14), channel_id=1, source_target_pairs={{0,2},{2,0},{4,6},{6,4},{8,10},{10,8},{12,14},{14,12},{16,18},{18,... | collective-permute-start | bytes 196616 | tf_op jit(solution)/shard_map/ppermute | solution.py:359
  6.3 8.8 %collective-permute-start.1 = (f32[128,128]{1,0:T(8,128)}, f32[128,128]{1,0:T(8,128)S(1)}, u32[]{:S(2)}, u32[]{:S(2)}) collective-permute-start(f32[128,128]{1,0:T(8,128)} %get-tuple-element.15), channel_id=1, source_target_pairs={{2,4},{4,2},{6,8},{8,6},{10,12},{12,10},{14,16},{16,14},{18,20},{2... | collective-permute-start | bytes 196616 | tf_op jit(solution)/shard_map/ppermute | solution.py:360
  15.2 0.0 copy-done
  15.2 0.0 copy-done.1
  15.2 0.0 copy-start.2
  15.2 1.1 %pack.1.col_ref = f32[32,128]{1,0:T(8,128)S(1)} custom-call(f32[2048,128]{1,0:T(8,128)S(1)} %bitcast.15, f32[2048,128]{1,0:T(8,128)S(1)} %bitcast.11), custom_call_target="tpu_custom_call" | custom-call | flops 786432 | bytes 2097152 | tf_op jit(solution)/shard_map/pack/pallas_call | solution.py:361
  16.3 0.0 collective-permute-done.first_ref
  16.3 0.7 %collective-permute-done.1.second_ref = f32[128,128]{1,0:T(8,128)S(1)} collective-permute-done((f32[128,128]{1,0:T(8,128)}, f32[128,128]{1,0:T(8,128)S(1)}, u32[]{:S(2)}, u32[]{:S(2)}) %collective-permute-start.1) | collective-permute-done | bytes 65568 | tf_op jit(solution)/shard_map/ppermute | solution.py:360
  17.0 0.1 corner.1
  17.1 4.0 %collective-permute-start.2 = (f32[40,128]{1,0:T(8,128)S(1)}, f32[40,128]{1,0:T(8,128)S(1)}, u32[]{:S(2)}, u32[]{:S(2)}) collective-permute-start(f32[40,128]{1,0:T(8,128)S(1)} %corner.1), channel_id=1, source_target_pairs={{0,1},{1,0},{2,3},{3,2},{4,5},{5,4},{6,7},{7,6},{8,9},{9,8},{10,11... | collective-permute-start | bytes 61448 | tf_op jit(solution)/shard_map/ppermute | solution.py:367
  21.2 0.0 copy-done.2
  21.2 1.6 %factor.1 = (f32[2048,128]{1,0:T(8,128)S(1)}, f32[2048,128]{1,0:T(8,128)S(1)}, f32[2048,128]{1,0:T(8,128)S(1)}, f32[160,128]{1,0:T(8,128)S(1)}, f32[32,128]{1,0:T(8,128)S(1)}, /*index=5*/f32[2048,128]{1,0:T(8,128)S(1)}) custom-call(f32[2048,128]{1,0:T(8,128)S(1)} %bitcast.12, bf16[64,32,128]{2,1,0:T(8,128)(2,1)S(1)} %copy-done.2), custom_call_target="tpu_custom_call" | custom-call | flops 5242880 | bytes 5767168 | tf_op jit(solution)/shard_map/factor/pallas_call | solution.py:362
  22.8 2.8 %source.1.f0_ref = f32[2048,128]{1,0:T(8,128)S(1)} custom-call(f32[2048,128]{1,0:T(8,128)S(1)} %bitcast.16, f32[2048,128]{1,0:T(8,128)S(1)} %bitcast.13, f32[2048,128]{1,0:T(8,128)S(1)} %get-tuple-element.13.skew_ref, f32[128,128]{1,0:T(8,128)S(1)} %collective-permute-done.first_ref, f32[128,128]{1,0:T(8,128)S(1)} %collective-permute-done.1.second_ref), custom_call_target="tpu_custom_call" | custom-call | flops 10485760 | bytes 4194304 | tf_op jit(solution)/shard_map/source/pallas_call | solution.py:368
  25.6 0.0 collective-permute-done.2.got_ref
  25.6 1.4 %sweep.1 = (f32[2048,128]{1,0:T(8,128)}, f32[2048,128]{1,0:T(8,128)S(1)}, f32[256,128]{1,0:T(8,128)S(1)}) custom-call(f32[2048,128]{1,0:T(8,128)S(1)} %source.1.f0_ref, f32[32,128]{1,0:T(8,128)S(1)} %pack.1.col_ref, f32[32,128]{1,0:T(8,128)S(1)} %get-tuple-element.16.skew_col_ref, f32[40,128]{1,0:T(8,128)S(1)} %collective-permute-done.2.got_ref, ...), custom_call_target="tpu_custom_call" | custom-call | flops 2097152 | bytes 6291456 | tf_op jit(solution)/shard_map/sweep/pallas_call | solution.py:371
  27.0 18.2 %all_to_all.22 = f32[16,16,128]{2,1,0:T(8,128)S(1)} all-to-all(f32[16,16,128]{2,1,0:T(8,128)S(1)} %bitcast.20), channel_id=1, replica_groups=mesh['gx'=16,'gy'=16,'gz'=2] {'gx'}, dimensions={0} | all-to-all | bytes 262144 | tf_op jit(solution)/shard_map/all_to_all | solution.py:375
  45.2 0.2 separator.1
  45.4 9.8 %all_to_all.23 = f32[16,4,128]{2,1,0:T(4,128)S(1)} all-to-all(f32[16,4,128]{2,1,0:T(4,128)S(1)} %bitcast.19), channel_id=1, replica_groups=mesh['gx'=16,'gy'=16,'gz'=2] {'gx'}, dimensions={0} | all-to-all | bytes 65536 | tf_op jit(solution)/shard_map/all_to_all | solution.py:379
  55.2 1.0 %back.1 = f32[2048,128]{1,0:T(8,128)} custom-call(f32[64,128]{1,0:T(8,128)S(1)} %bitcast.18, f32[2048,128]{1,0:T(8,128)S(1)} %get-tuple-element.23.b_ref, f32[2048,128]{1,0:T(8,128)S(1)} %get-tuple-element.17.t_ref, f32[2048,128]{1,0:T(8,128)S(1)} %get-tuple-element.18.q_ref), custom_call_target="tpu_custom_call" | custom-call | flops 1048576 | bytes 4194304 | tf_op jit(solution)/shard_map/back/pallas_call | solution.py:380
Async XLA Ops:
  0.6 14.5 %copy-start = (f32[64,32,128]{2,1,0:T(8,128)S(1)}, f32[64,32,128]{2,1,0:T(8,128)}, u32[]{:S(2)}) copy-start(f32[64,32,128]{2,1,0:T(8,128)} %param.4) | copy-start | bytes 3145732
  0.6 14.5 %copy-start.1 = (f32[64,32,128]{2,1,0:T(8,128)S(1)}, f32[64,32,128]{2,1,0:T(8,128)}, u32[]{:S(2)}) copy-start(f32[64,32,128]{2,1,0:T(8,128)} %param.3) | copy-start | bytes 3145732
  2.3 14.0 %collective-permute-start = (f32[128,128]{1,0:T(8,128)}, f32[128,128]{1,0:T(8,128)S(1)}, u32[]{:S(2)}, u32[]{:S(2)}) collective-permute-start(f32[128,128]{1,0:T(8,128)} %get-tuple-element.14), channel_id=1, source_target_pairs={{0,2},{2,0},{4,6},{6,4},{8,10},{10,8},{12,14},{14,12},{16,18},{18,... | collective-permute-start | bytes 196616 | tf_op jit(solution)/shard_map/ppermute | solution.py:359
  6.3 10.7 %collective-permute-start.1 = (f32[128,128]{1,0:T(8,128)}, f32[128,128]{1,0:T(8,128)S(1)}, u32[]{:S(2)}, u32[]{:S(2)}) collective-permute-start(f32[128,128]{1,0:T(8,128)} %get-tuple-element.15), channel_id=1, source_target_pairs={{2,4},{4,2},{6,8},{8,6},{10,12},{12,10},{14,16},{16,14},{18,20},{2... | collective-permute-start | bytes 196616 | tf_op jit(solution)/shard_map/ppermute | solution.py:360
  15.2 6.0 %copy-start.2 = (bf16[64,32,128]{2,1,0:T(8,128)(2,1)S(1)}, bf16[64,32,128]{2,1,0:T(8,128)(2,1)}, u32[]{:S(2)}) copy-start(bf16[64,32,128]{2,1,0:T(8,128)(2,1)} %skew_ref.1) | copy-start | bytes 1572868
  17.1 8.5 %collective-permute-start.2 = (f32[40,128]{1,0:T(8,128)S(1)}, f32[40,128]{1,0:T(8,128)S(1)}, u32[]{:S(2)}, u32[]{:S(2)}) collective-permute-start(f32[40,128]{1,0:T(8,128)S(1)} %corner.1), channel_id=1, source_target_pairs={{0,1},{1,0},{2,3},{3,2},{4,5},{5,4},{6,7},{7,6},{8,9},{9,8},{10,11... | collective-permute-start | bytes 61448 | tf_op jit(solution)/shard_map/ppermute | solution.py:367

commit v3 on v2

--- a/solution.py
+++ b/solution.py
@@ -45,10 +45,20 @@
     return lax.broadcasted_iota(jnp.int32, (NJ, NK), 0)
 
 
-def edge_kernel(u_ref, k_ref, first_ref, second_ref, sems):
-    odd = lax.rem(lax.axis_index("gy"), 2)
+def rows_to_send():
+    run = lax.axis_size("gy") // 2
+    place = lax.axis_index("gy")
+    odd = lax.rem(place, 2) == 1
+    lower = place < run
+    last = place == run - 1
+    ahead = (odd == lower, jnp.where(lower, jnp.logical_or(~odd, last), odd), ~odd)
+    return [jnp.where(way, NJ - 1, 0) for way in ahead]
+
+
+def edge_kernel(u_ref, k_ref, *refs):
+    sems = refs[-1]
     copies = []
-    for n, (ref, row) in enumerate(((first_ref, (1 - odd) * (NJ - 1)), (second_ref, odd * (NJ - 1)))):
+    for n, (ref, row) in enumerate(zip(refs, rows_to_send())):
         for m, source in enumerate((u_ref, k_ref)):
             copies.append(
                 pltpu.make_async_copy(
@@ -132,25 +142,33 @@
         plane_ref[c * NJ : c * NJ + NJ, :] = plane
 
 
-def beside(first_ref, second_ref, at):
-    odd = lax.rem(lax.axis_index("gy"), 2) == 1
-    first, second = first_ref[at, :], second_ref[at, :]
-    return jnp.where(odd, first, second), jnp.where(odd, second, first)
-
-
-def corner_kernel(first_ref, second_ref, col_ref, out_ref):
+def beside(refs, at):
+    run = lax.axis_size("gy") // 2
+    place = lax.axis_index("gy")
+    odd = lax.rem(place, 2) == 1
+    lower = place < run
+    last, before = place == run - 1, place == run - 2
+    first, second, third = [ref[at, :] for ref in refs]
+    below = jnp.where(odd == lower, second, first)
+    below = jnp.where(last, third, below)
+    above = jnp.where(odd == lower, first, second)
+    above = jnp.where(last, second, jnp.where(before, third, above))
+    return below, above
+
+
+def corner_kernel(first_ref, second_ref, third_ref, col_ref, out_ref):
     edge = jnp.where(lax.axis_index("gz") == 0, NK - 1, 0)
     wide = lax.broadcasted_iota(jnp.int32, (NI, NK), 1)
     deep = lax.broadcasted_iota(jnp.int32, (NI, NK), 0)
     out_ref[0:NJ, :] = col_ref[...]
     out_ref[NJ : NJ + 8, :] = jnp.zeros((8, NK), F32)
-    for n, beyond in enumerate(beside(first_ref, second_ref, slice(0, NI))):
+    for n, beyond in enumerate(beside((first_ref, second_ref, third_ref), slice(0, NI))):
         value = jnp.sum(jnp.where(wide == edge, beyond, 0.0), axis=1, keepdims=True)
         value = jnp.where(wide == deep, jnp.broadcast_to(value, (NI, NK)), 0.0)
         out_ref[NJ + n : NJ + n + 1, :] = jnp.sum(value, axis=0, keepdims=True)
 
 
-def source_kernel(u_ref, k_ref, skew_ref, first_ref, second_ref, f_ref):
+def source_kernel(u_ref, k_ref, skew_ref, first_ref, second_ref, third_ref, f_ref):
     lane = lax.broadcasted_iota(jnp.int32, (8, NK), 1)
     first_lane, last_lane = lane == 0, lane == NK - 1
 
@@ -163,8 +181,8 @@
         base = pl.multiple_of(n * (8 * NJ), 8 * NJ)
         near = pl.ds(pl.multiple_of(n * 8, 8), 8)
         deep = pl.ds(pl.multiple_of(NI + n * 8, 8), 8)
-        u_below, u_above = beside(first_ref, second_ref, near)
-        k_below, k_above = beside(first_ref, second_ref, deep)
+        u_below, u_above = beside((first_ref, second_ref, third_ref), near)
+        k_below, k_above = beside((first_ref, second_ref, third_ref), deep)
 
         def tile(ref, j):
             return ref[pl.ds(base + j, 8, stride=NJ), :]
@@ -343,30 +361,36 @@
     single = (NI, NJ, 1, NK)
     anywhere = pl.BlockSpec(memory_space=pltpu.HBM)
     whole = pl.BlockSpec(memory_space=pltpu.VMEM)
-    to_first, to_second = pl.pallas_call(
+    sent = pl.pallas_call(
         edge_kernel,
-        out_shape=[jax.ShapeDtypeStruct((2 * NI, NK), F32)] * 2,
+        out_shape=[jax.ShapeDtypeStruct((2 * NI, NK), F32)] * 3,
         in_specs=[anywhere] * 2,
-        out_specs=[whole] * 2,
-        scratch_shapes=[pltpu.SemaphoreType.DMA((4,))],
+        out_specs=[whole] * 3,
+        scratch_shapes=[pltpu.SemaphoreType.DMA((6,))],
         compiler_params=pltpu.CompilerParams(vmem_limit_bytes=56 * 1024 * 1024),
         cost_estimate=pl.CostEstimate(flops=0, bytes_accessed=8 * NI * NK * 4, transcendentals=0),
         name="edges",
     )(initial_thermal_state.reshape(single), thermal_spread_rate.reshape(single))
     count = lax.axis_size("gy")
-    odd_pairs = [(i, i + 1) for i in range(1, count - 1, 2)]
-    even_pairs = [(i, i + 1) for i in range(0, count, 2)]
-    first = lax.ppermute(to_first, "gy", [r for a, b in even_pairs for r in ((a, b), (b, a))])
-    second = lax.ppermute(to_second, "gy", [r for a, b in odd_pairs for r in ((a, b), (b, a))])
+    run = count // 2
+    swaps = (
+        [(i, i + 1) for i in (*range(1, run - 1, 2), *range(run, count, 2))],
+        [(i, i + 1) for i in (*range(0, run - 2, 2), *range(run - 1, count - 1, 2))],
+        [(run - 2, run - 1)],
+    )
+    beyond = [
+        lax.ppermute(rows, "gy", [way for a, b in pairs for way in ((a, b), (b, a))])
+        for rows, pairs in zip(sent, swaps)
+    ]
     (col,) = call(pack_kernel, [(NJ, NK)], 2, 3 * block, 8 * block, "pack")(u, k)
     t, q, r, planes, skew_col, skew = call(
         factor_kernel, [(ROWS, NK)] * 3 + [(5 * NJ, NK), (NJ, NK), (ROWS, NK)], 2,
         20 * block, 22 * block, "factor",
     )(k, yz_skew_factor)
-    (to_half,) = call(corner_kernel, [(NJ + 8, NK)], 3, NI * NK, 0, "corner")(first, second, col)
+    (to_half,) = call(corner_kernel, [(NJ + 8, NK)], 4, NI * NK, 0, "corner")(*beyond, col)
     got_col = lax.ppermute(to_half, "gz", [(0, 1), (1, 0)])
-    (f0,) = call(source_kernel, [(ROWS, NK)], 5, 40 * block, 16 * block, "source")(
-        u, k, skew, first, second
+    (f0,) = call(source_kernel, [(ROWS, NK)], 6, 40 * block, 16 * block, "source")(
+        u, k, skew, *beyond
     )
     f, b, send = call(
         sweep_kernel, [(ROWS, NK)] * 2 + [(BLOCKS * 2 * PLANES, NK)], 8,

time: 56.5 us -> 54.9 us (0.972)
  starting transfers between devices: 16.9 us -> 16 us
  waiting for transfers between devices: 0.73 us -> 0.06 us
    ppermute x2 -> x3, starting transfers between devices: 12.8 us -> 12 us  [body(): lax.ppermute(rows, 'gy', [way for a, b in pairs for way in ((a, b), (b, a...]
    ppermute x2 -> x3, waiting for transfers between devices: 0.73 us -> 0.06 us  [body(): lax.ppermute(rows, 'gy', [way for a, b in pairs for way in ((a, b), (b, a...]
  transfers between devices with their start and end apart: 3 -> 4, of which waited for: 1 -> 1; matrix products, arithmetic and copies ran while one was open for 0% -> 0% of each run, Pallas kernels for 10% -> 10%
where the time goes in v3:
time: 54.9 us; the launch traced here: 54.6 us
  blocking collectives  27.8 us (51%)
  starting transfers between devices  16 us (29%)
  Pallas kernels  9.94 us (18%)
  between operations  0.77 us (1%)
    all_to_all x1, blocking collectives, body(): got = lax.all_to_all(send, 'gx', 0, 0, tiled=True)  18 us
    ppermute x3, starting transfers between devices, body(): lax.ppermute(rows, 'gy', [way for a, b in pairs for way in ((a, b), (b, a...  12 us
    all_to_all x1, blocking collectives, body(): mine = lax.all_to_all(values, 'gx', 0, 0, tiled=True)  9.81 us
    ppermute x1, starting transfers between devices, body(): got_col = lax.ppermute(to_half, 'gz', [(0, 1), (1, 0)])  4.05 us
    pallas_call x1, Pallas kernels, body(): call(source_kernel, [(ROWS, NK)], 6, 40 * block, 16 * block, 'source')  2.84 us
    pallas_call x1, Pallas kernels, body(): pl.pallas_call(edge_kernel, out_shape=[jax.ShapeDtypeStruct((2 * NI, NK),...  1.73 us
    pallas_call x1, Pallas kernels, body(): call(factor_kernel, [(ROWS, NK)] * 3 + [(5 * NJ, NK), (NJ, NK), (ROWS, NK...  1.58 us
    pallas_call x1, Pallas kernels, body(): call(sweep_kernel, [(ROWS, NK)] * 2 + [(BLOCKS * 2 * PLANES, NK)], 8, 8 *...  1.37 us
  transfers between devices with their start and end apart: 4, of which 1 were waited for; matrix products, arithmetic and copies ran while one was open for 0% of the time, Pallas kernels for 10%

profile of v3, /device:TPU:3, one launch (start us, length us, event | category | flops | bytes accessed | tf_op | source)
XLA Modules:
  0.0 54.6 jit_solution(4837303738255155093)
XLA Ops:
  0.6 0.0 copy-start
  0.6 0.0 copy-start.1
  0.6 1.7 %edges.1 = (f32[128,128]{1,0:T(8,128)}, f32[128,128]{1,0:T(8,128)}, f32[128,128]{1,0:T(8,128)}) custom-call(f32[64,32,1,128]{3,2,1,0:T(1,128)} %bitcast.14, f32[64,32,1,128]{3,2,1,0:T(1,128)} %bitcast.10), custom_call_target="tpu_custom_call" | custom-call | bytes 262144 | tf_op jit(solution)/shard_map/edges/pallas_call | solution.py:364
  2.4 4.0 %collective-permute-start = (f32[128,128]{1,0:T(8,128)}, f32[128,128]{1,0:T(8,128)S(1)}, u32[]{:S(2)}, u32[]{:S(2)}) collective-permute-start(f32[128,128]{1,0:T(8,128)} %get-tuple-element.15), channel_id=1, source_target_pairs={{2,4},{4,2},{6,8},{8,6},{10,12},{12,10},{16,18},{18,16},{20,22},{2... | collective-permute-start | bytes 196616 | tf_op jit(solution)/shard_map/ppermute | solution.py:382
  6.4 7.3 %collective-permute-start.1 = (f32[128,128]{1,0:T(8,128)}, f32[128,128]{1,0:T(8,128)S(1)}, u32[]{:S(2)}, u32[]{:S(2)}) collective-permute-start(f32[128,128]{1,0:T(8,128)} %get-tuple-element.16), channel_id=1, source_target_pairs={{0,2},{2,0},{4,6},{6,4},{8,10},{10,8},{14,16},{16,14},{18,20},{20,... | collective-permute-start | bytes 196616 | tf_op jit(solution)/shard_map/ppermute | solution.py:382
  13.7 0.7 %collective-permute-start.2 = (f32[128,128]{1,0:T(8,128)}, f32[128,128]{1,0:T(8,128)S(1)}, u32[]{:S(2)}, u32[]{:S(2)}) collective-permute-start(f32[128,128]{1,0:T(8,128)} %get-tuple-element.17), channel_id=1, source_target_pairs={{12,14},{14,12},{13,15},{15,13},{44,46},{46,44},{45,47},{47,45},{7... | collective-permute-start | bytes 196616 | tf_op jit(solution)/shard_map/ppermute | solution.py:382
  14.4 0.0 copy-done
  14.4 0.0 copy-done.1
  14.4 0.0 copy-start.2
  14.4 1.1 %pack.1.col_ref = f32[32,128]{1,0:T(8,128)S(1)} custom-call(f32[2048,128]{1,0:T(8,128)S(1)} %bitcast.15, f32[2048,128]{1,0:T(8,128)S(1)} %bitcast.11), custom_call_target="tpu_custom_call" | custom-call | flops 786432 | bytes 2097152 | tf_op jit(solution)/shard_map/pack/pallas_call | solution.py:385
  15.5 0.0 collective-permute-done.first_ref
  15.5 0.1 collective-permute-done.1.second_ref
  15.6 0.0 collective-permute-done.2.third_ref
  15.6 0.1 corner.1
  15.7 4.0 %collective-permute-start.3 = (f32[40,128]{1,0:T(8,128)S(1)}, f32[40,128]{1,0:T(8,128)S(1)}, u32[]{:S(2)}, u32[]{:S(2)}) collective-permute-start(f32[40,128]{1,0:T(8,128)S(1)} %corner.1), channel_id=1, source_target_pairs={{0,1},{1,0},{2,3},{3,2},{4,5},{5,4},{6,7},{7,6},{8,9},{9,8},{10,11... | collective-permute-start | bytes 61448 | tf_op jit(solution)/shard_map/ppermute | solution.py:391
  19.7 0.0 copy-done.2
  19.7 1.6 %factor.1 = (f32[2048,128]{1,0:T(8,128)S(1)}, f32[2048,128]{1,0:T(8,128)S(1)}, f32[2048,128]{1,0:T(8,128)S(1)}, f32[160,128]{1,0:T(8,128)S(1)}, f32[32,128]{1,0:T(8,128)S(1)}, /*index=5*/f32[2048,128]{1,0:T(8,128)S(1)}) custom-call(f32[2048,128]{1,0:T(8,128)S(1)} %bitcast.12, bf16[64,32,128]{2,1,0:T(8,128)(2,1)S(1)} %copy-done.2), custom_call_target="tpu_custom_call" | custom-call | flops 5242880 | bytes 5767168 | tf_op jit(solution)/shard_map/factor/pallas_call | solution.py:386
  21.3 2.8 %source.1.f0_ref = f32[2048,128]{1,0:T(8,128)S(1)} custom-call(f32[2048,128]{1,0:T(8,128)S(1)} %bitcast.16, f32[2048,128]{1,0:T(8,128)S(1)} %bitcast.13, f32[2048,128]{1,0:T(8,128)S(1)} %get-tuple-element.14.skew_ref, f32[128,128]{1,0:T(8,128)S(1)} %collective-permute-done.first_ref, f32[128,128]{1,0:T(8,128)S(1)} %collective-permute-done.1.second_ref, ...), custom_call_target="tpu_custom_call" | custom-call | flops 10485760 | bytes 4194304 | tf_op jit(solution)/shard_map/source/pallas_call | solution.py:392
  24.2 0.0 collective-permute-done.3.got_ref
  24.2 1.4 %sweep.1 = (f32[2048,128]{1,0:T(8,128)}, f32[2048,128]{1,0:T(8,128)S(1)}, f32[256,128]{1,0:T(8,128)S(1)}) custom-call(f32[2048,128]{1,0:T(8,128)S(1)} %source.1.f0_ref, f32[32,128]{1,0:T(8,128)S(1)} %pack.1.col_ref, f32[32,128]{1,0:T(8,128)S(1)} %get-tuple-element.18.skew_col_ref, f32[40,128]{1,0:T(8,128)S(1)} %collective-permute-done.3.got_ref, ...), custom_call_target="tpu_custom_call" | custom-call | flops 2097152 | bytes 6291456 | tf_op jit(solution)/shard_map/sweep/pallas_call | solution.py:395
  25.6 18.0 %all_to_all.22 = f32[16,16,128]{2,1,0:T(8,128)S(1)} all-to-all(f32[16,16,128]{2,1,0:T(8,128)S(1)} %bitcast.20), channel_id=1, replica_groups=mesh['gx'=16,'gy'=16,'gz'=2] {'gx'}, dimensions={0} | all-to-all | bytes 262144 | tf_op jit(solution)/shard_map/all_to_all | solution.py:399
  43.6 0.2 separator.1
  43.8 9.8 %all_to_all.23 = f32[16,4,128]{2,1,0:T(4,128)S(1)} all-to-all(f32[16,4,128]{2,1,0:T(4,128)S(1)} %bitcast.19), channel_id=1, replica_groups=mesh['gx'=16,'gy'=16,'gz'=2] {'gx'}, dimensions={0} | all-to-all | bytes 65536 | tf_op jit(solution)/shard_map/all_to_all | solution.py:403
  53.6 1.0 %back.1 = f32[2048,128]{1,0:T(8,128)} custom-call(f32[64,128]{1,0:T(8,128)S(1)} %bitcast.18, f32[2048,128]{1,0:T(8,128)S(1)} %get-tuple-element.25.b_ref, f32[2048,128]{1,0:T(8,128)S(1)} %get-tuple-element.19.t_ref, f32[2048,128]{1,0:T(8,128)S(1)} %get-tuple-element.20.q_ref), custom_call_target="tpu_custom_call" | custom-call | flops 1048576 | bytes 4194304 | tf_op jit(solution)/shard_map/back/pallas_call | solution.py:404
Async XLA Ops:
  0.6 13.8 %copy-start = (f32[64,32,128]{2,1,0:T(8,128)S(1)}, f32[64,32,128]{2,1,0:T(8,128)}, u32[]{:S(2)}) copy-start(f32[64,32,128]{2,1,0:T(8,128)} %param.4) | copy-start | bytes 3145732
  0.6 13.8 %copy-start.1 = (f32[64,32,128]{2,1,0:T(8,128)S(1)}, f32[64,32,128]{2,1,0:T(8,128)}, u32[]{:S(2)}) copy-start(f32[64,32,128]{2,1,0:T(8,128)} %param.3) | copy-start | bytes 3145732
  2.4 13.1 %collective-permute-start = (f32[128,128]{1,0:T(8,128)}, f32[128,128]{1,0:T(8,128)S(1)}, u32[]{:S(2)}, u32[]{:S(2)}) collective-permute-start(f32[128,128]{1,0:T(8,128)} %get-tuple-element.15), channel_id=1, source_target_pairs={{2,4},{4,2},{6,8},{8,6},{10,12},{12,10},{16,18},{18,16},{20,22},{2... | collective-permute-start | bytes 196616 | tf_op jit(solution)/shard_map/ppermute | solution.py:382
  6.4 9.2 %collective-permute-start.1 = (f32[128,128]{1,0:T(8,128)}, f32[128,128]{1,0:T(8,128)S(1)}, u32[]{:S(2)}, u32[]{:S(2)}) collective-permute-start(f32[128,128]{1,0:T(8,128)} %get-tuple-element.16), channel_id=1, source_target_pairs={{0,2},{2,0},{4,6},{6,4},{8,10},{10,8},{14,16},{16,14},{18,20},{20,... | collective-permute-start | bytes 196616 | tf_op jit(solution)/shard_map/ppermute | solution.py:382
  13.7 1.9 %collective-permute-start.2 = (f32[128,128]{1,0:T(8,128)}, f32[128,128]{1,0:T(8,128)S(1)}, u32[]{:S(2)}, u32[]{:S(2)}) collective-permute-start(f32[128,128]{1,0:T(8,128)} %get-tuple-element.17), channel_id=1, source_target_pairs={{12,14},{14,12},{13,15},{15,13},{44,46},{46,44},{45,47},{47,45},{7... | collective-permute-start | bytes 196616 | tf_op jit(solution)/shard_map/ppermute | solution.py:382
  14.4 5.3 %copy-start.2 = (bf16[64,32,128]{2,1,0:T(8,128)(2,1)S(1)}, bf16[64,32,128]{2,1,0:T(8,128)(2,1)}, u32[]{:S(2)}) copy-start(bf16[64,32,128]{2,1,0:T(8,128)(2,1)} %skew_ref.1) | copy-start | bytes 1572868
  15.7 8.5 %collective-permute-start.3 = (f32[40,128]{1,0:T(8,128)S(1)}, f32[40,128]{1,0:T(8,128)S(1)}, u32[]{:S(2)}, u32[]{:S(2)}) collective-permute-start(f32[40,128]{1,0:T(8,128)S(1)} %corner.1), channel_id=1, source_target_pairs={{0,1},{1,0},{2,3},{3,2},{4,5},{5,4},{6,7},{7,6},{8,9},{9,8},{10,11... | collective-permute-start | bytes 61448 | tf_op jit(solution)/shard_map/ppermute | solution.py:391

commit v4 on v3

--- a/solution.py
+++ b/solution.py
@@ -15,6 +15,7 @@
 BLOCKS = 16
 PLANES = 8
 PART = 512
+PITCH = NJ + 8
 F32 = jnp.float32
 
 
@@ -71,40 +72,45 @@
         copy.wait()
 
 
-def pack_kernel(u_ref, k_ref, col_ref):
+def by_eights(layer, start):
+    def some(n, state):
+        for m in range(8):
+            state = layer(n * 8 + m, state)
+        return state
+
+    return lax.fori_loop(0, NI // 8, some, start)
+
+
+def pack_kernel(u_ref, k_ref, col_ref, u_wide_ref, k_wide_ref, sum_ref):
     turn = 1 - lax.axis_index("gz")
     lane = lanes()
 
     def layer(i, col):
         at = pl.ds(pl.multiple_of(i * NJ, NJ), NJ)
-        u = pltpu.roll(u_ref[at, :], i + turn, 1)
-        k = pltpu.roll(k_ref[at, :], (i + (NI + turn)) & (NK - 1), 1)
-        col = jnp.where(lane == i, u, col)
-        return jnp.where(lane == i + NI, k, col)
-
-    def some(n, col):
-        for m in range(8):
-            col = layer(n * 8 + m, col)
-        return col
-
-    col_ref[...] = lax.fori_loop(0, NI // 8, some, jnp.zeros((NJ, NK), F32))
-
-
-def factor_kernel(k_ref, skew_ref, t_ref, q_ref, r_ref, plane_ref, skew_col_ref, wide_ref):
+        to = pl.ds(pl.multiple_of(i * PITCH, 8), NJ)
+        u, k = u_ref[at, :], k_ref[at, :]
+        u_wide_ref[to, :] = u
+        k_wide_ref[to, :] = k
+        sum_ref[to, :] = k + jnp.where(lane == NK - 1, 0.0, pltpu.roll(k, NK - 1, 1))
+        col = jnp.where(lane == i, pltpu.roll(u, i + turn, 1), col)
+        return jnp.where(lane == i + NI, pltpu.roll(k, (i + (NI + turn)) & (NK - 1), 1), col)
+
+    col_ref[...] = by_eights(layer, jnp.zeros((NJ, NK), F32))
+
+
+def skew_kernel(skew_ref, col_ref, wide_ref):
     turn = 1 - lax.axis_index("gz")
     lane = lanes()
 
-    def skew(i, col):
+    def layer(i, col):
         g = skew_ref[i].astype(F32)
-        wide_ref[pl.ds(pl.multiple_of(i * NJ, NJ), NJ), :] = g
+        wide_ref[pl.ds(pl.multiple_of(i * PITCH, 8), NJ), :] = g
         return jnp.where(lane == i, pltpu.roll(g, i + turn, 1), col)
 
-    def skews(n, col):
-        for m in range(8):
-            col = skew(n * 8 + m, col)
-        return col
-
-    skew_col_ref[...] = lax.fori_loop(0, NI // 8, skews, jnp.zeros((NJ, NK), F32))
+    col_ref[...] = by_eights(layer, jnp.zeros((NJ, NK), F32))
+
+
+def factor_kernel(k_ref, t_ref, q_ref, r_ref, plane_ref):
     half = 0.5 * ratio_x
     zero = jnp.zeros((NJ, NK), F32)
     one = jnp.ones((NJ, NK), F32)
@@ -156,7 +162,7 @@
     return below, above
 
 
-def corner_kernel(first_ref, second_ref, third_ref, col_ref, out_ref):
+def corner_kernel(first_ref, second_ref, third_ref, col_ref, ready_ref, out_ref):
     edge = jnp.where(lax.axis_index("gz") == 0, NK - 1, 0)
     wide = lax.broadcasted_iota(jnp.int32, (NI, NK), 1)
     deep = lax.broadcasted_iota(jnp.int32, (NI, NK), 0)
@@ -168,7 +174,7 @@
         out_ref[NJ + n : NJ + n + 1, :] = jnp.sum(value, axis=0, keepdims=True)
 
 
-def source_kernel(u_ref, k_ref, skew_ref, first_ref, second_ref, third_ref, f_ref):
+def source_kernel(u_ref, k_ref, sum_ref, skew_ref, first_ref, second_ref, third_ref, f_ref):
     lane = lax.broadcasted_iota(jnp.int32, (8, NK), 1)
     first_lane, last_lane = lane == 0, lane == NK - 1
 
@@ -178,14 +184,14 @@
         return ahead, ahead - back
 
     def some(n, nothing):
-        base = pl.multiple_of(n * (8 * NJ), 8 * NJ)
+        base = n * (8 * PITCH)
         near = pl.ds(pl.multiple_of(n * 8, 8), 8)
         deep = pl.ds(pl.multiple_of(NI + n * 8, 8), 8)
         u_below, u_above = beside((first_ref, second_ref, third_ref), near)
         k_below, k_above = beside((first_ref, second_ref, third_ref), deep)
 
         def tile(ref, j):
-            return ref[pl.ds(base + j, 8, stride=NJ), :]
+            return ref[pl.ds(base + j, 8, stride=PITCH), :]
 
         u, k = tile(u_ref, 0), tile(k_ref, 0)
         _, d_before = slope(u_below)
@@ -198,10 +204,9 @@
                 u_next, k_next = u_above, k_above
             ahead_next, d_next = slope(u_next)
             flux = (k + k_next) * (u_next - u)
-            k_ahead = jnp.where(last_lane, 0.0, pltpu.roll(k, NK - 1, 1))
-            across = (k + k_ahead) * (ahead - u)
+            across = tile(sum_ref, j) * (ahead - u)
             before = jnp.where(first_lane, k * u, pltpu.roll(across, 1, 1))
-            f_ref[pl.ds(base + j, 8, stride=NJ), :] = (
+            f_ref[pl.ds(base + j, 8, stride=PITCH), :] = (
                 u
                 + (0.5 * ratio_y) * (flux - flux_before)
                 + (0.5 * ratio_z) * (across - before)
@@ -236,7 +241,7 @@
         s, total = state
         at = pl.ds(pl.multiple_of(i * NJ, NJ), NJ)
         here = pltpu.roll(extra, (turn - i) & (NK - 1), 1)
-        f = f0_ref[at, :] + jnp.where(edge, here, 0.0)
+        f = f0_ref[pl.ds(pl.multiple_of(i * PITCH, 8), NJ), :] + jnp.where(edge, here, 0.0)
         f_ref[at, :] = f
         s = f + s
         b_ref[at, :] = r_ref[at, :] * s
@@ -382,15 +387,22 @@
         lax.ppermute(rows, "gy", [way for a, b in pairs for way in ((a, b), (b, a))])
         for rows, pairs in zip(sent, swaps)
     ]
-    (col,) = call(pack_kernel, [(NJ, NK)], 2, 3 * block, 8 * block, "pack")(u, k)
-    t, q, r, planes, skew_col, skew = call(
-        factor_kernel, [(ROWS, NK)] * 3 + [(5 * NJ, NK), (NJ, NK), (ROWS, NK)], 2,
-        20 * block, 22 * block, "factor",
-    )(k, yz_skew_factor)
-    (to_half,) = call(corner_kernel, [(NJ + 8, NK)], 4, NI * NK, 0, "corner")(*beyond, col)
+    spread = (NI * PITCH, NK)
+    col, u_wide, k_wide, k_sum = call(
+        pack_kernel, [(NJ, NK)] + [spread] * 3, 2, 6 * block, 20 * block, "pack"
+    )(u, k)
+    skew_col, skew = call(skew_kernel, [(NJ, NK), spread], 1, block, 6 * block, "skew")(
+        yz_skew_factor
+    )
+    t, q, r, planes = call(
+        factor_kernel, [(ROWS, NK)] * 3 + [(5 * NJ, NK)], 1, 20 * block, 16 * block, "factor"
+    )(k)
+    (to_half,) = call(corner_kernel, [(NJ + 8, NK)], 5, NI * NK, 0, "corner")(
+        *beyond, col, skew_col
+    )
     got_col = lax.ppermute(to_half, "gz", [(0, 1), (1, 0)])
-    (f0,) = call(source_kernel, [(ROWS, NK)], 6, 40 * block, 16 * block, "source")(
-        u, k, skew, *beyond
+    (f0,) = call(source_kernel, [spread], 7, 40 * block, 16 * block, "source")(
+        u_wide, k_wide, k_sum, skew, *beyond
     )
     f, b, send = call(
         sweep_kernel, [(ROWS, NK)] * 2 + [(BLOCKS * 2 * PLANES, NK)], 8,

time: 54.9 us -> 53.9 us (0.982)
  the two profiles are of different devices: /device:TPU:3 before, /device:TPU:7 now
where the time goes in v4:
time: 53.9 us; the launch traced here: 53.6 us
  blocking collectives  28 us (52%)
  starting transfers between devices  15 us (28%)
  Pallas kernels  9.16 us (17%)
  between operations  0.79 us (1%)
  waiting for transfers between devices  0.65 us (1%)
    all_to_all x1, blocking collectives, body(): got = lax.all_to_all(send, 'gx', 0, 0, tiled=True)  18.2 us
    ppermute x3, starting transfers between devices, body(): lax.ppermute(rows, 'gy', [way for a, b in pairs for way in ((a, b), (b, a...  12.3 us
    all_to_all x1, blocking collectives, body(): mine = lax.all_to_all(values, 'gx', 0, 0, tiled=True)  9.81 us
    ppermute x1, starting transfers between devices, body(): got_col = lax.ppermute(to_half, 'gz', [(0, 1), (1, 0)])  2.74 us
    pallas_call x1, Pallas kernels, body(): call(source_kernel, [spread], 7, 40 * block, 16 * block, 'source')  1.75 us
    pallas_call x1, Pallas kernels, body(): pl.pallas_call(edge_kernel, out_shape=[jax.ShapeDtypeStruct((2 * NI, NK),...  1.74 us
    pallas_call x1, Pallas kernels, body(): call(pack_kernel, [(NJ, NK)] + [spread] * 3, 2, 6 * block, 20 * block, 'p...  1.38 us
    pallas_call x1, Pallas kernels, body(): call(sweep_kernel, [(ROWS, NK)] * 2 + [(BLOCKS * 2 * PLANES, NK)], 8, 8 *...  1.37 us
  transfers between devices with their start and end apart: 4, of which 1 were waited for; matrix products, arithmetic and copies ran while one was open for 0% of the time, Pallas kernels for 9%

profile of v4, /device:TPU:7, one launch (start us, length us, event | category | flops | bytes accessed | tf_op | source)
XLA Modules:
  0.0 53.6 jit_solution(10739778808314094824)
XLA Ops:
  0.6 0.0 copy-start.2
  0.6 0.0 copy-start
  0.6 0.0 copy-start.1
  0.7 1.7 %edges.1 = (f32[128,128]{1,0:T(8,128)}, f32[128,128]{1,0:T(8,128)}, f32[128,128]{1,0:T(8,128)}) custom-call(f32[64,32,1,128]{3,2,1,0:T(1,128)} %bitcast.13, f32[64,32,1,128]{3,2,1,0:T(1,128)} %bitcast.10), custom_call_target="tpu_custom_call" | custom-call | bytes 262144 | tf_op jit(solution)/shard_map/edges/pallas_call | solution.py:369
  2.4 4.0 %collective-permute-start = (f32[128,128]{1,0:T(8,128)}, f32[128,128]{1,0:T(8,128)S(1)}, u32[]{:S(2)}, u32[]{:S(2)}) collective-permute-start(f32[128,128]{1,0:T(8,128)} %get-tuple-element.22), channel_id=1, source_target_pairs={{2,4},{4,2},{6,8},{8,6},{10,12},{12,10},{16,18},{18,16},{20,22},{2... | collective-permute-start | bytes 196616 | tf_op jit(solution)/shard_map/ppermute | solution.py:387
  6.4 7.6 %collective-permute-start.1 = (f32[128,128]{1,0:T(8,128)}, f32[128,128]{1,0:T(8,128)S(1)}, u32[]{:S(2)}, u32[]{:S(2)}) collective-permute-start(f32[128,128]{1,0:T(8,128)} %get-tuple-element.23), channel_id=1, source_target_pairs={{0,2},{2,0},{4,6},{6,4},{8,10},{10,8},{14,16},{16,14},{18,20},{20,... | collective-permute-start | bytes 196616 | tf_op jit(solution)/shard_map/ppermute | solution.py:387
  14.0 0.7 %collective-permute-start.2 = (f32[128,128]{1,0:T(8,128)}, f32[128,128]{1,0:T(8,128)S(1)}, u32[]{:S(2)}, u32[]{:S(2)}) collective-permute-start(f32[128,128]{1,0:T(8,128)} %get-tuple-element.24), channel_id=1, source_target_pairs={{12,14},{14,12},{13,15},{15,13},{44,46},{46,44},{45,47},{47,45},{7... | collective-permute-start | bytes 196616 | tf_op jit(solution)/shard_map/ppermute | solution.py:387
  14.7 0.0 copy-done.2
  14.7 0.7 %skew.1 = (f32[32,128]{1,0:T(8,128)S(1)}, f32[2560,128]{1,0:T(8,128)S(1)}) custom-call(bf16[64,32,128]{2,1,0:T(8,128)(2,1)S(1)} %copy-done.2), custom_call_target="tpu_custom_call" | custom-call | flops 262144 | bytes 1572864 | tf_op jit(solution)/shard_map/skew/pallas_call | solution.py:394
  15.4 0.0 copy-done
  15.4 0.0 copy-done.1
  15.4 1.4 %pack.1 = (f32[32,128]{1,0:T(8,128)S(1)}, f32[2560,128]{1,0:T(8,128)S(1)}, f32[2560,128]{1,0:T(8,128)S(1)}, f32[2560,128]{1,0:T(8,128)S(1)}) custom-call(f32[2048,128]{1,0:T(8,128)S(1)} %bitcast.14, f32[2048,128]{1,0:T(8,128)S(1)} %bitcast.11), custom_call_target="tpu_custom_call" | custom-call | flops 1572864 | bytes 5242880 | tf_op jit(solution)/shard_map/pack/pallas_call | solution.py:391
  16.8 0.0 collective-permute-done.first_ref
  16.8 0.0 collective-permute-done.1.second_ref
  16.8 0.0 collective-permute-done.2.third_ref
  16.8 0.1 corner.1
  17.0 2.7 %collective-permute-start.3 = (f32[40,128]{1,0:T(8,128)S(1)}, f32[40,128]{1,0:T(8,128)S(1)}, u32[]{:S(2)}, u32[]{:S(2)}) collective-permute-start(f32[40,128]{1,0:T(8,128)S(1)} %corner.1), channel_id=1, source_target_pairs={{0,1},{1,0},{2,3},{3,2},{4,5},{5,4},{6,7},{7,6},{8,9},{9,8},{10,11... | collective-permute-start | bytes 61448 | tf_op jit(solution)/shard_map/ppermute | solution.py:403
  19.7 0.9 %factor.1 = (f32[2048,128]{1,0:T(8,128)S(1)}, f32[2048,128]{1,0:T(8,128)S(1)}, f32[2048,128]{1,0:T(8,128)S(1)}, f32[160,128]{1,0:T(8,128)S(1)}) custom-call(f32[2048,128]{1,0:T(8,128)S(1)} %bitcast.12), custom_call_target="tpu_custom_call" | custom-call | flops 5242880 | bytes 4194304 | tf_op jit(solution)/shard_map/factor/pallas_call | solution.py:397
  20.6 1.7 %source.1.f0_ref = f32[2560,128]{1,0:T(8,128)S(1)} custom-call(f32[2560,128]{1,0:T(8,128)S(1)} %get-tuple-element.18.u_ref, f32[2560,128]{1,0:T(8,128)S(1)} %get-tuple-element.19.k_ref, f32[2560,128]{1,0:T(8,128)S(1)} %get-tuple-element.20.sum_ref, f32[2560,128]{1,0:T(8,128)S(1)} %get-tuple-element.21.skew_ref, ...), custom_call_target="tpu_custom_call" | custom-call | flops 10485760 | bytes 4194304 | tf_op jit(solution)/shard_map/source/pallas_call | solution.py:404
  22.4 0.6 %collective-permute-done.3.got_ref = f32[40,128]{1,0:T(8,128)S(1)} collective-permute-done((f32[40,128]{1,0:T(8,128)S(1)}, f32[40,128]{1,0:T(8,128)S(1)}, u32[]{:S(2)}, u32[]{:S(2)}) %collective-permute-start.3) | collective-permute-done | bytes 20512 | tf_op jit(solution)/shard_map/ppermute | solution.py:403
  23.0 1.4 %sweep.1 = (f32[2048,128]{1,0:T(8,128)}, f32[2048,128]{1,0:T(8,128)S(1)}, f32[256,128]{1,0:T(8,128)S(1)}) custom-call(f32[2560,128]{1,0:T(8,128)S(1)} %source.1.f0_ref, f32[32,128]{1,0:T(8,128)S(1)} %get-tuple-element.25.col_ref, f32[32,128]{1,0:T(8,128)S(1)} %get-tuple-element.26.ready_ref.skew_col_ref, f32[40,128]{1,0:T(8,128)S(1)} %collective-permute-done.3.got_ref, ...), custom_call_target="tpu_custom_call" | custom-call | flops 2097152 | bytes 6291456 | tf_op jit(solution)/shard_map/sweep/pallas_call | solution.py:407
  24.4 18.2 %all_to_all.22 = f32[16,16,128]{2,1,0:T(8,128)S(1)} all-to-all(f32[16,16,128]{2,1,0:T(8,128)S(1)} %bitcast.18), channel_id=1, replica_groups=mesh['gx'=16,'gy'=16,'gz'=2] {'gx'}, dimensions={0} | all-to-all | bytes 262144 | tf_op jit(solution)/shard_map/all_to_all | solution.py:411
  42.6 0.2 separator.1
  42.8 9.8 %all_to_all.23 = f32[16,4,128]{2,1,0:T(4,128)S(1)} all-to-all(f32[16,4,128]{2,1,0:T(4,128)S(1)} %bitcast.17), channel_id=1, replica_groups=mesh['gx'=16,'gy'=16,'gz'=2] {'gx'}, dimensions={0} | all-to-all | bytes 65536 | tf_op jit(solution)/shard_map/all_to_all | solution.py:415
  52.6 1.0 %back.1 = f32[2048,128]{1,0:T(8,128)} custom-call(f32[64,128]{1,0:T(8,128)S(1)} %bitcast.16, f32[2048,128]{1,0:T(8,128)S(1)} %get-tuple-element.33.b_ref, f32[2048,128]{1,0:T(8,128)S(1)} %get-tuple-element.27.t_ref, f32[2048,128]{1,0:T(8,128)S(1)} %get-tuple-element.28.q_ref), custom_call_target="tpu_custom_call" | custom-call | flops 1048576 | bytes 4194304 | tf_op jit(solution)/shard_map/back/pallas_call | solution.py:416
Async XLA Ops:
  0.6 14.1 %copy-start.2 = (bf16[64,32,128]{2,1,0:T(8,128)(2,1)S(1)}, bf16[64,32,128]{2,1,0:T(8,128)(2,1)}, u32[]{:S(2)}) copy-start(bf16[64,32,128]{2,1,0:T(8,128)(2,1)} %skew_ref.1) | copy-start | bytes 1572868
  0.6 14.8 %copy-start = (f32[64,32,128]{2,1,0:T(8,128)S(1)}, f32[64,32,128]{2,1,0:T(8,128)}, u32[]{:S(2)}) copy-start(f32[64,32,128]{2,1,0:T(8,128)} %param.4) | copy-start | bytes 3145732
  0.6 14.8 %copy-start.1 = (f32[64,32,128]{2,1,0:T(8,128)S(1)}, f32[64,32,128]{2,1,0:T(8,128)}, u32[]{:S(2)}) copy-start(f32[64,32,128]{2,1,0:T(8,128)} %param.3) | copy-start | bytes 3145732
  2.4 14.4 %collective-permute-start = (f32[128,128]{1,0:T(8,128)}, f32[128,128]{1,0:T(8,128)S(1)}, u32[]{:S(2)}, u32[]{:S(2)}) collective-permute-start(f32[128,128]{1,0:T(8,128)} %get-tuple-element.22), channel_id=1, source_target_pairs={{2,4},{4,2},{6,8},{8,6},{10,12},{12,10},{16,18},{18,16},{20,22},{2... | collective-permute-start | bytes 196616 | tf_op jit(solution)/shard_map/ppermute | solution.py:387
  6.4 10.4 %collective-permute-start.1 = (f32[128,128]{1,0:T(8,128)}, f32[128,128]{1,0:T(8,128)S(1)}, u32[]{:S(2)}, u32[]{:S(2)}) collective-permute-start(f32[128,128]{1,0:T(8,128)} %get-tuple-element.23), channel_id=1, source_target_pairs={{0,2},{2,0},{4,6},{6,4},{8,10},{10,8},{14,16},{16,14},{18,20},{20,... | collective-permute-start | bytes 196616 | tf_op jit(solution)/shard_map/ppermute | solution.py:387
  14.0 2.8 %collective-permute-start.2 = (f32[128,128]{1,0:T(8,128)}, f32[128,128]{1,0:T(8,128)S(1)}, u32[]{:S(2)}, u32[]{:S(2)}) collective-permute-start(f32[128,128]{1,0:T(8,128)} %get-tuple-element.24), channel_id=1, source_target_pairs={{12,14},{14,12},{13,15},{15,13},{44,46},{46,44},{45,47},{47,45},{7... | collective-permute-start | bytes 196616 | tf_op jit(solution)/shard_map/ppermute | solution.py:387
  17.0 6.0 %collective-permute-start.3 = (f32[40,128]{1,0:T(8,128)S(1)}, f32[40,128]{1,0:T(8,128)S(1)}, u32[]{:S(2)}, u32[]{:S(2)}) collective-permute-start(f32[40,128]{1,0:T(8,128)S(1)} %corner.1), channel_id=1, source_target_pairs={{0,1},{1,0},{2,3},{3,2},{4,5},{5,4},{6,7},{7,6},{8,9},{9,8},{10,11... | collective-permute-start | bytes 61448 | tf_op jit(solution)/shard_map/ppermute | solution.py:403

commit v5 on v4

--- a/solution.py
+++ b/solution.py
@@ -162,7 +162,7 @@
     return below, above
 
 
-def corner_kernel(first_ref, second_ref, third_ref, col_ref, ready_ref, out_ref):
+def corner_kernel(first_ref, second_ref, third_ref, col_ref, out_ref):
     edge = jnp.where(lax.axis_index("gz") == 0, NK - 1, 0)
     wide = lax.broadcasted_iota(jnp.int32, (NI, NK), 1)
     deep = lax.broadcasted_iota(jnp.int32, (NI, NK), 0)
@@ -260,7 +260,10 @@
         return carried, total, s
 
     zero = jnp.zeros((NJ, NK), F32)
-    _, total, s = lax.fori_loop(0, ROWS // PART, some, (zero, zero, zero))
+    state = (zero, zero, zero)
+    for n in range(ROWS // PART):
+        state = some(n, state)
+    _, total, s = state
     planes = [plane_ref[c * NJ : c * NJ + NJ, :] for c in range(5)] + [total, s]
     half = NJ // 2
     for c, plane in enumerate(planes):
@@ -368,7 +371,7 @@
     whole = pl.BlockSpec(memory_space=pltpu.VMEM)
     sent = pl.pallas_call(
         edge_kernel,
-        out_shape=[jax.ShapeDtypeStruct((2 * NI, NK), F32)] * 3,
+        out_shape=[pltpu.VMEM((2 * NI, NK), F32)] * 3,
         in_specs=[anywhere] * 2,
         out_specs=[whole] * 3,
         scratch_shapes=[pltpu.SemaphoreType.DMA((6,))],
@@ -397,9 +400,7 @@
     t, q, r, planes = call(
         factor_kernel, [(ROWS, NK)] * 3 + [(5 * NJ, NK)], 1, 20 * block, 16 * block, "factor"
     )(k)
-    (to_half,) = call(corner_kernel, [(NJ + 8, NK)], 5, NI * NK, 0, "corner")(
-        *beyond, col, skew_col
-    )
+    (to_half,) = call(corner_kernel, [(NJ + 8, NK)], 4, NI * NK, 0, "corner")(*beyond, col)
     got_col = lax.ppermute(to_half, "gz", [(0, 1), (1, 0)])
     (f0,) = call(source_kernel, [spread], 7, 40 * block, 16 * block, "source")(
         u_wide, k_wide, k_sum, skew, *beyond

time: 53.9 us -> 52.8 us (0.980)
  Pallas kernels: 9.16 us -> 8.36 us
  waiting for transfers between devices: 0.65 us -> 0.01 us
    pallas_call x2, Pallas kernels: 1.85 us -> 1.19 us  [the longest x1 1.07 us: body(): pl.pallas_call(edge_kernel, out_shape=[pltpu.VMEM((2 * NI, NK), F32)] * 3...]
    ppermute x1, waiting for transfers between devices: 0.64 us -> 0.01 us  [body(): got_col = lax.ppermute(to_half, 'gz', [(0, 1), (1, 0)])]
  transfers between devices with their start and end apart: 4 -> 4, of which waited for: 1 -> 0; matrix products, arithmetic and copies ran while one was open for 0% -> 0% of each run, Pallas kernels for 9% -> 9%
where the time goes in v5:
time: 52.8 us; the launch traced here: 52.3 us
  blocking collectives  28 us (53%)
  starting transfers between devices  15.1 us (29%)
  Pallas kernels  8.36 us (16%)
  between operations  0.8 us (2%)
    all_to_all x1, blocking collectives, body(): got = lax.all_to_all(send, 'gx', 0, 0, tiled=True)  18.2 us
    ppermute x3, starting transfers between devices, body(): lax.ppermute(rows, 'gy', [way for a, b in pairs for way in ((a, b), (b, a...  12.4 us
    all_to_all x1, blocking collectives, body(): mine = lax.all_to_all(values, 'gx', 0, 0, tiled=True)  9.81 us
    ppermute x1, starting transfers between devices, body(): got_col = lax.ppermute(to_half, 'gz', [(0, 1), (1, 0)])  2.74 us
    pallas_call x1, Pallas kernels, body(): call(source_kernel, [spread], 7, 40 * block, 16 * block, 'source')  1.75 us
    pallas_call x1, Pallas kernels, body(): call(pack_kernel, [(NJ, NK)] + [spread] * 3, 2, 6 * block, 20 * block, 'p...  1.38 us
    pallas_call x1, Pallas kernels, body(): call(sweep_kernel, [(ROWS, NK)] * 2 + [(BLOCKS * 2 * PLANES, NK)], 8, 8 *...  1.23 us
    pallas_call x1, Pallas kernels, body(): pl.pallas_call(edge_kernel, out_shape=[pltpu.VMEM((2 * NI, NK), F32)] * 3...  1.07 us
  transfers between devices with their start and end apart: 4, of which 0 were waited for; matrix products, arithmetic and copies ran while one was open for 0% of the time, Pallas kernels for 9%

profile of v5, /device:TPU:7, one launch (start us, length us, event | category | flops | bytes accessed | tf_op | source)
XLA Modules:
  0.0 52.3 jit_solution(3221184272421171874)
XLA Ops:
  0.6 0.0 copy-start.1
  0.6 0.0 copy-start
  0.6 1.1 %edges.1 = (f32[128,128]{1,0:T(8,128)S(1)}, f32[128,128]{1,0:T(8,128)S(1)}, f32[128,128]{1,0:T(8,128)S(1)}) custom-call(f32[64,32,1,128]{3,2,1,0:T(1,128)} %bitcast.13, f32[64,32,1,128]{3,2,1,0:T(1,128)} %bitcast.10), custom_call_target="tpu_custom_call" | custom-call | bytes 262144 | tf_op jit(solution)/shard_map/edges/pallas_call | solution.py:372
  1.7 0.0 copy-start.2
  1.7 4.1 %collective-permute-start = (f32[128,128]{1,0:T(8,128)S(1)}, f32[128,128]{1,0:T(8,128)S(1)}, u32[]{:S(2)}, u32[]{:S(2)}) collective-permute-start(f32[128,128]{1,0:T(8,128)S(1)} %get-tuple-element.22), channel_id=1, source_target_pairs={{2,4},{4,2},{6,8},{8,6},{10,12},{12,10},{16,18},{18,16},{20,22},{2... | collective-permute-start | bytes 196616 | tf_op jit(solution)/shard_map/ppermute | solution.py:390
  5.9 7.6 %collective-permute-start.1 = (f32[128,128]{1,0:T(8,128)S(1)}, f32[128,128]{1,0:T(8,128)S(1)}, u32[]{:S(2)}, u32[]{:S(2)}) collective-permute-start(f32[128,128]{1,0:T(8,128)S(1)} %get-tuple-element.23), channel_id=1, source_target_pairs={{0,2},{2,0},{4,6},{6,4},{8,10},{10,8},{14,16},{16,14},{18,20},{20,... | collective-permute-start | bytes 196616 | tf_op jit(solution)/shard_map/ppermute | solution.py:390
  13.5 0.7 %collective-permute-start.2 = (f32[128,128]{1,0:T(8,128)S(1)}, f32[128,128]{1,0:T(8,128)S(1)}, u32[]{:S(2)}, u32[]{:S(2)}) collective-permute-start(f32[128,128]{1,0:T(8,128)S(1)} %get-tuple-element.24), channel_id=1, source_target_pairs={{12,14},{14,12},{13,15},{15,13},{44,46},{46,44},{45,47},{47,45},{7... | collective-permute-start | bytes 196616 | tf_op jit(solution)/shard_map/ppermute | solution.py:390
  14.2 0.0 copy-done.1
  14.2 0.0 copy-done
  14.2 1.4 %pack.1 = (f32[32,128]{1,0:T(8,128)S(1)}, f32[2560,128]{1,0:T(8,128)S(1)}, f32[2560,128]{1,0:T(8,128)S(1)}, f32[2560,128]{1,0:T(8,128)S(1)}) custom-call(f32[2048,128]{1,0:T(8,128)S(1)} %bitcast.14, f32[2048,128]{1,0:T(8,128)S(1)} %bitcast.11), custom_call_target="tpu_custom_call" | custom-call | flops 1572864 | bytes 5242880 | tf_op jit(solution)/shard_map/pack/pallas_call | solution.py:394
  15.6 0.0 collective-permute-done.first_ref
  15.6 0.0 collective-permute-done.1.second_ref
  15.6 0.0 collective-permute-done.2.third_ref
  15.6 0.1 corner.1
  15.7 2.7 %collective-permute-start.3 = (f32[40,128]{1,0:T(8,128)S(1)}, f32[40,128]{1,0:T(8,128)S(1)}, u32[]{:S(2)}, u32[]{:S(2)}) collective-permute-start(f32[40,128]{1,0:T(8,128)S(1)} %corner.1), channel_id=1, source_target_pairs={{0,1},{1,0},{2,3},{3,2},{4,5},{5,4},{6,7},{7,6},{8,9},{9,8},{10,11... | collective-permute-start | bytes 61448 | tf_op jit(solution)/shard_map/ppermute | solution.py:404
  18.5 0.0 copy-done.2
  18.5 0.7 %skew.1 = (f32[32,128]{1,0:T(8,128)S(1)}, f32[2560,128]{1,0:T(8,128)S(1)}) custom-call(bf16[64,32,128]{2,1,0:T(8,128)(2,1)S(1)} %copy-done.2), custom_call_target="tpu_custom_call" | custom-call | flops 262144 | bytes 1572864 | tf_op jit(solution)/shard_map/skew/pallas_call | solution.py:397
  19.2 0.9 %factor.1 = (f32[2048,128]{1,0:T(8,128)S(1)}, f32[2048,128]{1,0:T(8,128)S(1)}, f32[2048,128]{1,0:T(8,128)S(1)}, f32[160,128]{1,0:T(8,128)S(1)}) custom-call(f32[2048,128]{1,0:T(8,128)S(1)} %bitcast.12), custom_call_target="tpu_custom_call" | custom-call | flops 5242880 | bytes 4194304 | tf_op jit(solution)/shard_map/factor/pallas_call | solution.py:400
  20.1 1.7 %source.1.f0_ref = f32[2560,128]{1,0:T(8,128)S(1)} custom-call(f32[2560,128]{1,0:T(8,128)S(1)} %get-tuple-element.18.u_ref, f32[2560,128]{1,0:T(8,128)S(1)} %get-tuple-element.19.k_ref, f32[2560,128]{1,0:T(8,128)S(1)} %get-tuple-element.20.sum_ref, f32[2560,128]{1,0:T(8,128)S(1)} %get-tuple-element.21.skew_ref, ...), custom_call_target="tpu_custom_call" | custom-call | flops 10485760 | bytes 4194304 | tf_op jit(solution)/shard_map/source/pallas_call | solution.py:405
  21.8 0.0 collective-permute-done.3.got_ref
  21.8 1.2 %sweep.1 = (f32[2048,128]{1,0:T(8,128)}, f32[2048,128]{1,0:T(8,128)S(1)}, f32[256,128]{1,0:T(8,128)S(1)}) custom-call(f32[2560,128]{1,0:T(8,128)S(1)} %source.1.f0_ref, f32[32,128]{1,0:T(8,128)S(1)} %get-tuple-element.25.col_ref, f32[32,128]{1,0:T(8,128)S(1)} %get-tuple-element.26.skew_col_ref, f32[40,128]{1,0:T(8,128)S(1)} %collective-permute-done.3.got_ref, ...), custom_call_target="tpu_custom_call" | custom-call | flops 2097152 | bytes 6291456 | tf_op jit(solution)/shard_map/sweep/pallas_call | solution.py:408
  23.1 18.2 %all_to_all.22 = f32[16,16,128]{2,1,0:T(8,128)S(1)} all-to-all(f32[16,16,128]{2,1,0:T(8,128)S(1)} %bitcast.18), channel_id=1, replica_groups=mesh['gx'=16,'gy'=16,'gz'=2] {'gx'}, dimensions={0} | all-to-all | bytes 262144 | tf_op jit(solution)/shard_map/all_to_all | solution.py:412
  41.3 0.2 separator.1
  41.5 9.8 %all_to_all.23 = f32[16,4,128]{2,1,0:T(4,128)S(1)} all-to-all(f32[16,4,128]{2,1,0:T(4,128)S(1)} %bitcast.17), channel_id=1, replica_groups=mesh['gx'=16,'gy'=16,'gz'=2] {'gx'}, dimensions={0} | all-to-all | bytes 65536 | tf_op jit(solution)/shard_map/all_to_all | solution.py:416
  51.3 1.0 %back.1 = f32[2048,128]{1,0:T(8,128)} custom-call(f32[64,128]{1,0:T(8,128)S(1)} %bitcast.16, f32[2048,128]{1,0:T(8,128)S(1)} %get-tuple-element.33.b_ref, f32[2048,128]{1,0:T(8,128)S(1)} %get-tuple-element.27.t_ref, f32[2048,128]{1,0:T(8,128)S(1)} %get-tuple-element.28.q_ref), custom_call_target="tpu_custom_call" | custom-call | flops 1048576 | bytes 4194304 | tf_op jit(solution)/shard_map/back/pallas_call | solution.py:417
Async XLA Ops:
  0.6 13.5 %copy-start.1 = (f32[64,32,128]{2,1,0:T(8,128)S(1)}, f32[64,32,128]{2,1,0:T(8,128)}, u32[]{:S(2)}) copy-start(f32[64,32,128]{2,1,0:T(8,128)} %param.3) | copy-start | bytes 3145732
  0.6 13.5 %copy-start = (f32[64,32,128]{2,1,0:T(8,128)S(1)}, f32[64,32,128]{2,1,0:T(8,128)}, u32[]{:S(2)}) copy-start(f32[64,32,128]{2,1,0:T(8,128)} %param.4) | copy-start | bytes 3145732
  1.7 16.7 %copy-start.2 = (bf16[64,32,128]{2,1,0:T(8,128)(2,1)S(1)}, bf16[64,32,128]{2,1,0:T(8,128)(2,1)}, u32[]{:S(2)}) copy-start(bf16[64,32,128]{2,1,0:T(8,128)(2,1)} %skew_ref.1) | copy-start | bytes 1572868
  1.7 13.8 %collective-permute-start = (f32[128,128]{1,0:T(8,128)S(1)}, f32[128,128]{1,0:T(8,128)S(1)}, u32[]{:S(2)}, u32[]{:S(2)}) collective-permute-start(f32[128,128]{1,0:T(8,128)S(1)} %get-tuple-element.22), channel_id=1, source_target_pairs={{2,4},{4,2},{6,8},{8,6},{10,12},{12,10},{16,18},{18,16},{20,22},{2... | collective-permute-start | bytes 196616 | tf_op jit(solution)/shard_map/ppermute | solution.py:390
  5.9 9.7 %collective-permute-start.1 = (f32[128,128]{1,0:T(8,128)S(1)}, f32[128,128]{1,0:T(8,128)S(1)}, u32[]{:S(2)}, u32[]{:S(2)}) collective-permute-start(f32[128,128]{1,0:T(8,128)S(1)} %get-tuple-element.23), channel_id=1, source_target_pairs={{0,2},{2,0},{4,6},{6,4},{8,10},{10,8},{14,16},{16,14},{18,20},{20,... | collective-permute-start | bytes 196616 | tf_op jit(solution)/shard_map/ppermute | solution.py:390
  13.5 2.1 %collective-permute-start.2 = (f32[128,128]{1,0:T(8,128)S(1)}, f32[128,128]{1,0:T(8,128)S(1)}, u32[]{:S(2)}, u32[]{:S(2)}) collective-permute-start(f32[128,128]{1,0:T(8,128)S(1)} %get-tuple-element.24), channel_id=1, source_target_pairs={{12,14},{14,12},{13,15},{15,13},{44,46},{46,44},{45,47},{47,45},{7... | collective-permute-start | bytes 196616 | tf_op jit(solution)/shard_map/ppermute | solution.py:390
  15.7 6.1 %collective-permute-start.3 = (f32[40,128]{1,0:T(8,128)S(1)}, f32[40,128]{1,0:T(8,128)S(1)}, u32[]{:S(2)}, u32[]{:S(2)}) collective-permute-start(f32[40,128]{1,0:T(8,128)S(1)} %corner.1), channel_id=1, source_target_pairs={{0,1},{1,0},{2,3},{3,2},{4,5},{5,4},{6,7},{7,6},{8,9},{9,8},{10,11... | collective-permute-start | bytes 61448 | tf_op jit(solution)/shard_map/ppermute | solution.py:404

commit v6 on v5

--- a/solution.py
+++ b/solution.py
@@ -13,7 +13,7 @@
 NI, NJ, NK = 64, 32, 128
 ROWS = NI * NJ
 BLOCKS = 16
-PLANES = 8
+PLANES = 7
 PART = 512
 PITCH = NJ + 8
 F32 = jnp.float32
@@ -265,12 +265,9 @@
         state = some(n, state)
     _, total, s = state
     planes = [plane_ref[c * NJ : c * NJ + NJ, :] for c in range(5)] + [total, s]
-    half = NJ // 2
     for c, plane in enumerate(planes):
-        send_ref[pl.ds(2 * c, half, stride=2 * PLANES), :] = plane[0:half]
-        send_ref[pl.ds(2 * c + 1, half, stride=2 * PLANES), :] = plane[half:NJ]
-    for c in range(2 * len(planes), 2 * PLANES):
-        send_ref[pl.ds(c, half, stride=2 * PLANES), :] = zero[0:half]
+        for q in range(BLOCKS):
+            send_ref[q, :, c * NK : c * NK + NK] = plane[2 * q : 2 * q + 2]
     for n in range(ROWS // PART):
         leave(n).wait()
 
@@ -279,8 +276,7 @@
     half = 0.5 * ratio_x
 
     def plane(p, c):
-        at = p * 2 * PLANES + 2 * c
-        return got_ref[at : at + 2, :]
+        return got_ref[p, :, c * NK : c * NK + NK]
 
     def inner(p):
         return plane(p, 1)
@@ -335,14 +331,10 @@
 
 def back_kernel(v_ref, b_ref, t_ref, q_ref, w_out, w_ref, sems):
     half = NJ // 2
-    ends = []
-    for c in range(2):
-        ends.append(
-            jnp.concatenate(
-                [v_ref[pl.ds(2 * c, half, stride=4), :], v_ref[pl.ds(2 * c + 1, half, stride=4), :]]
-            )
-        )
-    head, tail = ends
+    for c in range(4):
+        w_ref[pl.ds(c // 2 * NJ + c % 2, half, stride=2), :] = v_ref[pl.ds(c, half, stride=4), :]
+    head, tail = w_ref[0:NJ, :], w_ref[NJ : 2 * NJ, :]
+
     def layer(i, w):
         at = pl.ds(i * NJ, NJ)
         w = (b_ref[at, :] + q_ref[at, :] * head) + t_ref[at, :] * w
@@ -406,7 +398,7 @@
         u_wide, k_wide, k_sum, skew, *beyond
     )
     f, b, send = call(
-        sweep_kernel, [(ROWS, NK)] * 2 + [(BLOCKS * 2 * PLANES, NK)], 8,
+        sweep_kernel, [(ROWS, NK)] * 2 + [(BLOCKS, 2, PLANES * NK)], 8,
         8 * block, 24 * block, "sweep", True,
     )(f0, col, skew_col, got_col, t, q, r, planes)
     got = lax.all_to_all(send, "gx", 0, 0, tiled=True)

time: 52.8 us -> 52.5 us (level)
  no operation moved by 1% of the time
where the time goes in v6:
time: 52.5 us; the launch traced here: 52 us
  blocking collectives  27.7 us (53%)
  starting transfers between devices  15.1 us (29%)
  Pallas kernels  8.36 us (16%)
  between operations  0.8 us (2%)
    all_to_all x1, blocking collectives, body(): got = lax.all_to_all(send, 'gx', 0, 0, tiled=True)  17.9 us
    ppermute x3, starting transfers between devices, body(): lax.ppermute(rows, 'gy', [way for a, b in pairs for way in ((a, b), (b, a...  12.4 us
    all_to_all x1, blocking collectives, body(): mine = lax.all_to_all(values, 'gx', 0, 0, tiled=True)  9.8 us
    ppermute x1, starting transfers between devices, body(): got_col = lax.ppermute(to_half, 'gz', [(0, 1), (1, 0)])  2.74 us
    pallas_call x1, Pallas kernels, body(): call(source_kernel, [spread], 7, 40 * block, 16 * block, 'source')  1.75 us
    pallas_call x1, Pallas kernels, body(): call(pack_kernel, [(NJ, NK)] + [spread] * 3, 2, 6 * block, 20 * block, 'p...  1.38 us
    pallas_call x1, Pallas kernels, body(): call(sweep_kernel, [(ROWS, NK)] * 2 + [(BLOCKS, 2, PLANES * NK)], 8, 8 *...  1.23 us
    pallas_call x1, Pallas kernels, body(): pl.pallas_call(edge_kernel, out_shape=[pltpu.VMEM((2 * NI, NK), F32)] * 3...  1.07 us
  transfers between devices with their start and end apart: 4, of which 0 were waited for; matrix products, arithmetic and copies ran while one was open for 0% of the time, Pallas kernels for 9%

profile of v6, /device:TPU:7, one launch (start us, length us, event | category | flops | bytes accessed | tf_op | source)
XLA Modules:
  0.0 52.0 jit_solution(4271898145007767774)
XLA Ops:
  0.6 0.0 copy-start.1
  0.6 0.0 copy-start
  0.6 1.1 %edges.1 = (f32[128,128]{1,0:T(8,128)S(1)}, f32[128,128]{1,0:T(8,128)S(1)}, f32[128,128]{1,0:T(8,128)S(1)}) custom-call(f32[64,32,1,128]{3,2,1,0:T(1,128)} %bitcast.11, f32[64,32,1,128]{3,2,1,0:T(1,128)} %bitcast.8), custom_call_target="tpu_custom_call" | custom-call | bytes 262144 | tf_op jit(solution)/shard_map/edges/pallas_call | solution.py:364
  1.7 0.0 copy-start.2
  1.7 4.1 %collective-permute-start = (f32[128,128]{1,0:T(8,128)S(1)}, f32[128,128]{1,0:T(8,128)S(1)}, u32[]{:S(2)}, u32[]{:S(2)}) collective-permute-start(f32[128,128]{1,0:T(8,128)S(1)} %get-tuple-element.22), channel_id=1, source_target_pairs={{2,4},{4,2},{6,8},{8,6},{10,12},{12,10},{16,18},{18,16},{20,22},{2... | collective-permute-start | bytes 196616 | tf_op jit(solution)/shard_map/ppermute | solution.py:382
  5.9 7.6 %collective-permute-start.1 = (f32[128,128]{1,0:T(8,128)S(1)}, f32[128,128]{1,0:T(8,128)S(1)}, u32[]{:S(2)}, u32[]{:S(2)}) collective-permute-start(f32[128,128]{1,0:T(8,128)S(1)} %get-tuple-element.23), channel_id=1, source_target_pairs={{0,2},{2,0},{4,6},{6,4},{8,10},{10,8},{14,16},{16,14},{18,20},{20,... | collective-permute-start | bytes 196616 | tf_op jit(solution)/shard_map/ppermute | solution.py:382
  13.5 0.7 %collective-permute-start.2 = (f32[128,128]{1,0:T(8,128)S(1)}, f32[128,128]{1,0:T(8,128)S(1)}, u32[]{:S(2)}, u32[]{:S(2)}) collective-permute-start(f32[128,128]{1,0:T(8,128)S(1)} %get-tuple-element.24), channel_id=1, source_target_pairs={{12,14},{14,12},{13,15},{15,13},{44,46},{46,44},{45,47},{47,45},{7... | collective-permute-start | bytes 196616 | tf_op jit(solution)/shard_map/ppermute | solution.py:382
  14.2 0.0 copy-done.1
  14.2 0.0 copy-done
  14.2 1.4 %pack.1 = (f32[32,128]{1,0:T(8,128)S(1)}, f32[2560,128]{1,0:T(8,128)S(1)}, f32[2560,128]{1,0:T(8,128)S(1)}, f32[2560,128]{1,0:T(8,128)S(1)}) custom-call(f32[2048,128]{1,0:T(8,128)S(1)} %bitcast.12, f32[2048,128]{1,0:T(8,128)S(1)} %bitcast.9), custom_call_target="tpu_custom_call" | custom-call | flops 1572864 | bytes 5242880 | tf_op jit(solution)/shard_map/pack/pallas_call | solution.py:386
  15.6 0.0 collective-permute-done.first_ref
  15.6 0.0 collective-permute-done.1.second_ref
  15.6 0.0 collective-permute-done.2.third_ref
  15.6 0.1 corner.1
  15.7 2.7 %collective-permute-start.3 = (f32[40,128]{1,0:T(8,128)S(1)}, f32[40,128]{1,0:T(8,128)S(1)}, u32[]{:S(2)}, u32[]{:S(2)}) collective-permute-start(f32[40,128]{1,0:T(8,128)S(1)} %corner.1), channel_id=1, source_target_pairs={{0,1},{1,0},{2,3},{3,2},{4,5},{5,4},{6,7},{7,6},{8,9},{9,8},{10,11... | collective-permute-start | bytes 61448 | tf_op jit(solution)/shard_map/ppermute | solution.py:396
  18.5 0.0 copy-done.2
  18.5 0.7 %skew.1 = (f32[32,128]{1,0:T(8,128)S(1)}, f32[2560,128]{1,0:T(8,128)S(1)}) custom-call(bf16[64,32,128]{2,1,0:T(8,128)(2,1)S(1)} %copy-done.2), custom_call_target="tpu_custom_call" | custom-call | flops 262144 | bytes 1572864 | tf_op jit(solution)/shard_map/skew/pallas_call | solution.py:389
  19.2 0.9 %factor.1 = (f32[2048,128]{1,0:T(8,128)S(1)}, f32[2048,128]{1,0:T(8,128)S(1)}, f32[2048,128]{1,0:T(8,128)S(1)}, f32[160,128]{1,0:T(8,128)S(1)}) custom-call(f32[2048,128]{1,0:T(8,128)S(1)} %bitcast.10), custom_call_target="tpu_custom_call" | custom-call | flops 5242880 | bytes 4194304 | tf_op jit(solution)/shard_map/factor/pallas_call | solution.py:392
  20.1 1.7 %source.1.f0_ref = f32[2560,128]{1,0:T(8,128)S(1)} custom-call(f32[2560,128]{1,0:T(8,128)S(1)} %get-tuple-element.18.u_ref, f32[2560,128]{1,0:T(8,128)S(1)} %get-tuple-element.19.k_ref, f32[2560,128]{1,0:T(8,128)S(1)} %get-tuple-element.20.sum_ref, f32[2560,128]{1,0:T(8,128)S(1)} %get-tuple-element.21.skew_ref, ...), custom_call_target="tpu_custom_call" | custom-call | flops 10485760 | bytes 4194304 | tf_op jit(solution)/shard_map/source/pallas_call | solution.py:397
  21.8 0.0 collective-permute-done.3.got_ref
  21.8 1.2 %sweep.1 = (f32[2048,128]{1,0:T(8,128)}, f32[2048,128]{1,0:T(8,128)S(1)}, f32[16,2,896]{2,1,0:T(2,128)S(1)}) custom-call(f32[2560,128]{1,0:T(8,128)S(1)} %source.1.f0_ref, f32[32,128]{1,0:T(8,128)S(1)} %get-tuple-element.25.col_ref, f32[32,128]{1,0:T(8,128)S(1)} %get-tuple-element.26.skew_col_ref, f32[40,128]{1,0:T(8,128)S(1)} %collective-permute-done.3.got_ref, ...), custom_call_target="tpu_custom_call" | custom-call | flops 2097152 | bytes 6291456 | tf_op jit(solution)/shard_map/sweep/pallas_call | solution.py:400
  23.1 17.9 %all_to_all.16.got_ref = f32[16,2,896]{2,1,0:T(2,128)S(1)} all-to-all(f32[16,2,896]{2,1,0:T(2,128)S(1)} %get-tuple-element.32), channel_id=1, replica_groups=mesh['gx'=16,'gy'=16,'gz'=2] {'gx'}, dimensions={0} | all-to-all | bytes 229376 | tf_op jit(solution)/shard_map/all_to_all | solution.py:404
  41.0 0.2 separator.1
  41.2 9.8 %all_to_all.17 = f32[16,4,128]{2,1,0:T(4,128)S(1)} all-to-all(f32[16,4,128]{2,1,0:T(4,128)S(1)} %bitcast.14), channel_id=1, replica_groups=mesh['gx'=16,'gy'=16,'gz'=2] {'gx'}, dimensions={0} | all-to-all | bytes 65536 | tf_op jit(solution)/shard_map/all_to_all | solution.py:408
  51.0 1.0 %back.1 = f32[2048,128]{1,0:T(8,128)} custom-call(f32[64,128]{1,0:T(8,128)S(1)} %bitcast.13, f32[2048,128]{1,0:T(8,128)S(1)} %get-tuple-element.33.b_ref, f32[2048,128]{1,0:T(8,128)S(1)} %get-tuple-element.27.t_ref, f32[2048,128]{1,0:T(8,128)S(1)} %get-tuple-element.28.q_ref), custom_call_target="tpu_custom_call" | custom-call | flops 1048576 | bytes 4194304 | tf_op jit(solution)/shard_map/back/pallas_call | solution.py:409
Async XLA Ops:
  0.6 13.5 %copy-start.1 = (f32[64,32,128]{2,1,0:T(8,128)S(1)}, f32[64,32,128]{2,1,0:T(8,128)}, u32[]{:S(2)}) copy-start(f32[64,32,128]{2,1,0:T(8,128)} %param.3) | copy-start | bytes 3145732
  0.6 13.5 %copy-start = (f32[64,32,128]{2,1,0:T(8,128)S(1)}, f32[64,32,128]{2,1,0:T(8,128)}, u32[]{:S(2)}) copy-start(f32[64,32,128]{2,1,0:T(8,128)} %param.4) | copy-start | bytes 3145732
  1.7 16.7 %copy-start.2 = (bf16[64,32,128]{2,1,0:T(8,128)(2,1)S(1)}, bf16[64,32,128]{2,1,0:T(8,128)(2,1)}, u32[]{:S(2)}) copy-start(bf16[64,32,128]{2,1,0:T(8,128)(2,1)} %skew_ref.1) | copy-start | bytes 1572868
  1.7 13.8 %collective-permute-start = (f32[128,128]{1,0:T(8,128)S(1)}, f32[128,128]{1,0:T(8,128)S(1)}, u32[]{:S(2)}, u32[]{:S(2)}) collective-permute-start(f32[128,128]{1,0:T(8,128)S(1)} %get-tuple-element.22), channel_id=1, source_target_pairs={{2,4},{4,2},{6,8},{8,6},{10,12},{12,10},{16,18},{18,16},{20,22},{2... | collective-permute-start | bytes 196616 | tf_op jit(solution)/shard_map/ppermute | solution.py:382
  5.9 9.7 %collective-permute-start.1 = (f32[128,128]{1,0:T(8,128)S(1)}, f32[128,128]{1,0:T(8,128)S(1)}, u32[]{:S(2)}, u32[]{:S(2)}) collective-permute-start(f32[128,128]{1,0:T(8,128)S(1)} %get-tuple-element.23), channel_id=1, source_target_pairs={{0,2},{2,0},{4,6},{6,4},{8,10},{10,8},{14,16},{16,14},{18,20},{20,... | collective-permute-start | bytes 196616 | tf_op jit(solution)/shard_map/ppermute | solution.py:382
  13.5 2.1 %collective-permute-start.2 = (f32[128,128]{1,0:T(8,128)S(1)}, f32[128,128]{1,0:T(8,128)S(1)}, u32[]{:S(2)}, u32[]{:S(2)}) collective-permute-start(f32[128,128]{1,0:T(8,128)S(1)} %get-tuple-element.24), channel_id=1, source_target_pairs={{12,14},{14,12},{13,15},{15,13},{44,46},{46,44},{45,47},{47,45},{7... | collective-permute-start | bytes 196616 | tf_op jit(solution)/shard_map/ppermute | solution.py:382
  15.7 6.1 %collective-permute-start.3 = (f32[40,128]{1,0:T(8,128)S(1)}, f32[40,128]{1,0:T(8,128)S(1)}, u32[]{:S(2)}, u32[]{:S(2)}) collective-permute-start(f32[40,128]{1,0:T(8,128)S(1)} %corner.1), channel_id=1, source_target_pairs={{0,1},{1,0},{2,3},{3,2},{4,5},{5,4},{6,7},{7,6},{8,9},{9,8},{10,11... | collective-permute-start | bytes 61448 | tf_op jit(solution)/shard_map/ppermute | solution.py:396

commit v7 on v6

--- a/solution.py
+++ b/solution.py
@@ -98,19 +98,12 @@
     col_ref[...] = by_eights(layer, jnp.zeros((NJ, NK), F32))
 
 
-def skew_kernel(skew_ref, col_ref, wide_ref):
-    turn = 1 - lax.axis_index("gz")
-    lane = lanes()
-
-    def layer(i, col):
-        g = skew_ref[i].astype(F32)
-        wide_ref[pl.ds(pl.multiple_of(i * PITCH, 8), NJ), :] = g
-        return jnp.where(lane == i, pltpu.roll(g, i + turn, 1), col)
-
-    col_ref[...] = by_eights(layer, jnp.zeros((NJ, NK), F32))
-
-
-def factor_kernel(k_ref, t_ref, q_ref, r_ref, plane_ref):
+def factor_kernel(k_ref, skew_ref, t_ref, q_ref, r_ref, plane_ref, wide_ref):
+    def widen(i):
+        wide_ref[pl.ds(pl.multiple_of(i * PITCH, 8), NJ), :] = skew_ref[i].astype(F32)
+
+    widen(0)
+    widen(NI - 1)
     half = 0.5 * ratio_x
     zero = jnp.zeros((NJ, NK), F32)
     one = jnp.ones((NJ, NK), F32)
@@ -125,6 +118,7 @@
 
     def layer(i, state):
         here, ground, left, total = state
+        widen(i)
         at = pl.ds(pl.multiple_of(i * NJ, NJ), NJ)
         after = k_ref[pl.ds(pl.multiple_of(i * NJ + NJ, NJ), NJ), :]
         link = half * (here + after)
@@ -219,7 +213,7 @@
 
 
 def sweep_kernel(
-    f0_ref, col_ref, skew_col_ref, got_ref, t_ref, q_ref, r_ref, plane_ref,
+    f0_ref, col_ref, skew_ref, got_ref, t_ref, q_ref, r_ref, plane_ref,
     f_out, b_ref, send_ref, f_ref, sems,
 ):
     right = lax.axis_index("gz") == 0
@@ -231,17 +225,18 @@
     up = jnp.where(row == NJ - 1, above, pltpu.roll(far, NJ - 1, 0))
     down = jnp.where(row == 0, below, pltpu.roll(far, 1, 0))
     sign = jnp.where(right, ratio_mix, -ratio_mix).astype(F32)
-    extra = (0.5 * ratio_z) * (own_k * far + far_k * (far - own)) + (
-        sign * skew_col_ref[...]
-    ) * (up - down)
+    fluxes = (0.5 * ratio_z) * (own_k * far + far_k * (far - own))
+    slopes = sign * (up - down)
     edge = lane == jnp.where(right, NK - 1, 0)
     turn = jnp.where(right, NK - 1, NK)
 
     def layer(i, state):
         s, total = state
         at = pl.ds(pl.multiple_of(i * NJ, NJ), NJ)
-        here = pltpu.roll(extra, (turn - i) & (NK - 1), 1)
-        f = f0_ref[pl.ds(pl.multiple_of(i * PITCH, 8), NJ), :] + jnp.where(edge, here, 0.0)
+        wide = pl.ds(pl.multiple_of(i * PITCH, 8), NJ)
+        shift = (turn - i) & (NK - 1)
+        extra = pltpu.roll(fluxes, shift, 1) + skew_ref[wide, :] * pltpu.roll(slopes, shift, 1)
+        f = f0_ref[wide, :] + jnp.where(edge, extra, 0.0)
         f_ref[at, :] = f
         s = f + s
         b_ref[at, :] = r_ref[at, :] * s
@@ -386,12 +381,9 @@
     col, u_wide, k_wide, k_sum = call(
         pack_kernel, [(NJ, NK)] + [spread] * 3, 2, 6 * block, 20 * block, "pack"
     )(u, k)
-    skew_col, skew = call(skew_kernel, [(NJ, NK), spread], 1, block, 6 * block, "skew")(
-        yz_skew_factor
-    )
-    t, q, r, planes = call(
-        factor_kernel, [(ROWS, NK)] * 3 + [(5 * NJ, NK)], 1, 20 * block, 16 * block, "factor"
-    )(k)
+    t, q, r, planes, skew = call(
+        factor_kernel, [(ROWS, NK)] * 3 + [(5 * NJ, NK), spread], 2, 20 * block, 22 * block, "factor"
+    )(k, yz_skew_factor)
     (to_half,) = call(corner_kernel, [(NJ + 8, NK)], 4, NI * NK, 0, "corner")(*beyond, col)
     got_col = lax.ppermute(to_half, "gz", [(0, 1), (1, 0)])
     (f0,) = call(source_kernel, [spread], 7, 40 * block, 16 * block, "source")(
@@ -400,7 +392,7 @@
     f, b, send = call(
         sweep_kernel, [(ROWS, NK)] * 2 + [(BLOCKS, 2, PLANES * NK)], 8,
         8 * block, 24 * block, "sweep", True,
-    )(f0, col, skew_col, got_col, t, q, r, planes)
+    )(f0, col, skew, got_col, t, q, r, planes)
     got = lax.all_to_all(send, "gx", 0, 0, tiled=True)
     (values,) = call(
         separator_kernel, [(4 * BLOCKS, NK)], 1, block, block, "separator"

time: 52.5 us -> 52.5 us (level)
  waiting for transfers between devices: 0.01 us -> 0.62 us
    pallas_call x2 -> x1, Pallas kernels: 1.58 us -> 0.9 us  [body(): call(factor_kernel, [(ROWS, NK)] * 3 + [(5 * NJ, NK), spread], 2, 20 * bl...]
    ppermute x1, waiting for transfers between devices: 0.01 us -> 0.61 us  [body(): got_col = lax.ppermute(to_half, 'gz', [(0, 1), (1, 0)])]
  transfers between devices with their start and end apart: 4 -> 4, of which waited for: 0 -> 1; matrix products, arithmetic and copies ran while one was open for 0% -> 0% of each run, Pallas kernels for 9% -> 8%
where the time goes in v7:
time: 52.5 us; the launch traced here: 52.2 us
  blocking collectives  27.8 us (53%)
  starting transfers between devices  15.1 us (29%)
  Pallas kernels  7.89 us (15%)
  between operations  0.78 us (1%)
  waiting for transfers between devices  0.62 us (1%)
    all_to_all x1, blocking collectives, body(): got = lax.all_to_all(send, 'gx', 0, 0, tiled=True)  18 us
    ppermute x3, starting transfers between devices, body(): lax.ppermute(rows, 'gy', [way for a, b in pairs for way in ((a, b), (b, a...  12.4 us
    all_to_all x1, blocking collectives, body(): mine = lax.all_to_all(values, 'gx', 0, 0, tiled=True)  9.8 us
    ppermute x1, starting transfers between devices, body(): got_col = lax.ppermute(to_half, 'gz', [(0, 1), (1, 0)])  2.74 us
    pallas_call x1, Pallas kernels, body(): call(source_kernel, [spread], 7, 40 * block, 16 * block, 'source')  1.75 us
    pallas_call x1, Pallas kernels, body(): call(sweep_kernel, [(ROWS, NK)] * 2 + [(BLOCKS, 2, PLANES * NK)], 8, 8 *...  1.44 us
    pallas_call x1, Pallas kernels, body(): call(pack_kernel, [(NJ, NK)] + [spread] * 3, 2, 6 * block, 20 * block, 'p...  1.38 us
    pallas_call x1, Pallas kernels, body(): pl.pallas_call(edge_kernel, out_shape=[pltpu.VMEM((2 * NI, NK), F32)] * 3...  1.07 us
  transfers between devices with their start and end apart: 4, of which 1 were waited for; matrix products, arithmetic and copies ran while one was open for 0% of the time, Pallas kernels for 8%

profile of v7, /device:TPU:7, one launch (start us, length us, event | category | flops | bytes accessed | tf_op | source)
XLA Modules:
  0.0 52.2 jit_solution(5497755222459084913)
XLA Ops:
  0.6 0.0 copy-start.1
  0.6 0.0 copy-start
  0.6 1.1 %edges.1 = (f32[128,128]{1,0:T(8,128)S(1)}, f32[128,128]{1,0:T(8,128)S(1)}, f32[128,128]{1,0:T(8,128)S(1)}) custom-call(f32[64,32,1,128]{3,2,1,0:T(1,128)} %bitcast.11, f32[64,32,1,128]{3,2,1,0:T(1,128)} %bitcast.8), custom_call_target="tpu_custom_call" | custom-call | bytes 262144 | tf_op jit(solution)/shard_map/edges/pallas_call | solution.py:359
  1.7 0.0 copy-start.2
  1.7 4.1 %collective-permute-start = (f32[128,128]{1,0:T(8,128)S(1)}, f32[128,128]{1,0:T(8,128)S(1)}, u32[]{:S(2)}, u32[]{:S(2)}) collective-permute-start(f32[128,128]{1,0:T(8,128)S(1)} %get-tuple-element.21), channel_id=1, source_target_pairs={{2,4},{4,2},{6,8},{8,6},{10,12},{12,10},{16,18},{18,16},{20,22},{2... | collective-permute-start | bytes 196616 | tf_op jit(solution)/shard_map/ppermute | solution.py:377
  5.9 7.6 %collective-permute-start.1 = (f32[128,128]{1,0:T(8,128)S(1)}, f32[128,128]{1,0:T(8,128)S(1)}, u32[]{:S(2)}, u32[]{:S(2)}) collective-permute-start(f32[128,128]{1,0:T(8,128)S(1)} %get-tuple-element.22), channel_id=1, source_target_pairs={{0,2},{2,0},{4,6},{6,4},{8,10},{10,8},{14,16},{16,14},{18,20},{20,... | collective-permute-start | bytes 196616 | tf_op jit(solution)/shard_map/ppermute | solution.py:377
  13.5 0.7 %collective-permute-start.2 = (f32[128,128]{1,0:T(8,128)S(1)}, f32[128,128]{1,0:T(8,128)S(1)}, u32[]{:S(2)}, u32[]{:S(2)}) collective-permute-start(f32[128,128]{1,0:T(8,128)S(1)} %get-tuple-element.23), channel_id=1, source_target_pairs={{12,14},{14,12},{13,15},{15,13},{44,46},{46,44},{45,47},{47,45},{7... | collective-permute-start | bytes 196616 | tf_op jit(solution)/shard_map/ppermute | solution.py:377
  14.2 0.0 copy-done.1
  14.2 0.0 copy-done
  14.2 1.4 %pack.1 = (f32[32,128]{1,0:T(8,128)S(1)}, f32[2560,128]{1,0:T(8,128)S(1)}, f32[2560,128]{1,0:T(8,128)S(1)}, f32[2560,128]{1,0:T(8,128)S(1)}) custom-call(f32[2048,128]{1,0:T(8,128)S(1)} %bitcast.12, f32[2048,128]{1,0:T(8,128)S(1)} %bitcast.9), custom_call_target="tpu_custom_call" | custom-call | flops 1572864 | bytes 5242880 | tf_op jit(solution)/shard_map/pack/pallas_call | solution.py:381
  15.6 0.0 collective-permute-done.first_ref
  15.6 0.0 collective-permute-done.1.second_ref
  15.6 0.0 collective-permute-done.2.third_ref
  15.6 0.1 corner.1
  15.7 2.7 %collective-permute-start.3 = (f32[40,128]{1,0:T(8,128)S(1)}, f32[40,128]{1,0:T(8,128)S(1)}, u32[]{:S(2)}, u32[]{:S(2)}) collective-permute-start(f32[40,128]{1,0:T(8,128)S(1)} %corner.1), channel_id=1, source_target_pairs={{0,1},{1,0},{2,3},{3,2},{4,5},{5,4},{6,7},{7,6},{8,9},{9,8},{10,11... | collective-permute-start | bytes 61448 | tf_op jit(solution)/shard_map/ppermute | solution.py:388
  18.5 0.0 copy-done.2
  18.5 0.9 %factor.1 = (f32[2048,128]{1,0:T(8,128)S(1)}, f32[2048,128]{1,0:T(8,128)S(1)}, f32[2048,128]{1,0:T(8,128)S(1)}, f32[160,128]{1,0:T(8,128)S(1)}, f32[2560,128]{1,0:T(8,128)S(1)}) custom-call(f32[2048,128]{1,0:T(8,128)S(1)} %bitcast.10, bf16[64,32,128]{2,1,0:T(8,128)(2,1)S(1)} %copy-done.2), custom_call_target="tpu_custom_call" | custom-call | flops 5242880 | bytes 5767168 | tf_op jit(solution)/shard_map/factor/pallas_call | solution.py:384
  19.4 1.7 %source.1.f0_ref = f32[2560,128]{1,0:T(8,128)S(1)} custom-call(f32[2560,128]{1,0:T(8,128)S(1)} %get-tuple-element.17.u_ref, f32[2560,128]{1,0:T(8,128)S(1)} %get-tuple-element.18.k_ref, f32[2560,128]{1,0:T(8,128)S(1)} %get-tuple-element.19.sum_ref, f32[2560,128]{1,0:T(8,128)S(1)} %get-tuple-element.20.skew_ref, ...), custom_call_target="tpu_custom_call" | custom-call | flops 10485760 | bytes 4194304 | tf_op jit(solution)/shard_map/source/pallas_call | solution.py:389
  21.1 0.6 %collective-permute-done.3.got_ref = f32[40,128]{1,0:T(8,128)S(1)} collective-permute-done((f32[40,128]{1,0:T(8,128)S(1)}, f32[40,128]{1,0:T(8,128)S(1)}, u32[]{:S(2)}, u32[]{:S(2)}) %collective-permute-start.3) | collective-permute-done | bytes 20512 | tf_op jit(solution)/shard_map/ppermute | solution.py:388
  21.8 1.4 %sweep.1 = (f32[2048,128]{1,0:T(8,128)}, f32[2048,128]{1,0:T(8,128)S(1)}, f32[16,2,896]{2,1,0:T(2,128)S(1)}) custom-call(f32[2560,128]{1,0:T(8,128)S(1)} %source.1.f0_ref, f32[32,128]{1,0:T(8,128)S(1)} %get-tuple-element.24.col_ref, f32[2560,128]{1,0:T(8,128)S(1)} %get-tuple-element.20.skew_ref, f32[40,128]{1,0:T(8,128)S(1)} %collective-permute-done.3.got_ref, ...), custom_call_target="tpu_custom_call" | custom-call | flops 2097152 | bytes 6291456 | tf_op jit(solution)/shard_map/sweep/pallas_call | solution.py:392
  23.2 18.0 %all_to_all.16.got_ref = f32[16,2,896]{2,1,0:T(2,128)S(1)} all-to-all(f32[16,2,896]{2,1,0:T(2,128)S(1)} %get-tuple-element.30), channel_id=1, replica_groups=mesh['gx'=16,'gy'=16,'gz'=2] {'gx'}, dimensions={0} | all-to-all | bytes 229376 | tf_op jit(solution)/shard_map/all_to_all | solution.py:396
  41.2 0.2 separator.1
  41.4 9.8 %all_to_all.17 = f32[16,4,128]{2,1,0:T(4,128)S(1)} all-to-all(f32[16,4,128]{2,1,0:T(4,128)S(1)} %bitcast.14), channel_id=1, replica_groups=mesh['gx'=16,'gy'=16,'gz'=2] {'gx'}, dimensions={0} | all-to-all | bytes 65536 | tf_op jit(solution)/shard_map/all_to_all | solution.py:400
  51.2 1.0 %back.1 = f32[2048,128]{1,0:T(8,128)} custom-call(f32[64,128]{1,0:T(8,128)S(1)} %bitcast.13, f32[2048,128]{1,0:T(8,128)S(1)} %get-tuple-element.31.b_ref, f32[2048,128]{1,0:T(8,128)S(1)} %get-tuple-element.25.t_ref, f32[2048,128]{1,0:T(8,128)S(1)} %get-tuple-element.26.q_ref), custom_call_target="tpu_custom_call" | custom-call | flops 1048576 | bytes 4194304 | tf_op jit(solution)/shard_map/back/pallas_call | solution.py:401
Async XLA Ops:
  0.6 13.5 %copy-start.1 = (f32[64,32,128]{2,1,0:T(8,128)S(1)}, f32[64,32,128]{2,1,0:T(8,128)}, u32[]{:S(2)}) copy-start(f32[64,32,128]{2,1,0:T(8,128)} %param.3) | copy-start | bytes 3145732
  0.6 13.5 %copy-start = (f32[64,32,128]{2,1,0:T(8,128)S(1)}, f32[64,32,128]{2,1,0:T(8,128)}, u32[]{:S(2)}) copy-start(f32[64,32,128]{2,1,0:T(8,128)} %param.4) | copy-start | bytes 3145732
  1.7 16.7 %copy-start.2 = (bf16[64,32,128]{2,1,0:T(8,128)(2,1)S(1)}, bf16[64,32,128]{2,1,0:T(8,128)(2,1)}, u32[]{:S(2)}) copy-start(bf16[64,32,128]{2,1,0:T(8,128)(2,1)} %skew_ref.1) | copy-start | bytes 1572868
  1.7 13.8 %collective-permute-start = (f32[128,128]{1,0:T(8,128)S(1)}, f32[128,128]{1,0:T(8,128)S(1)}, u32[]{:S(2)}, u32[]{:S(2)}) collective-permute-start(f32[128,128]{1,0:T(8,128)S(1)} %get-tuple-element.21), channel_id=1, source_target_pairs={{2,4},{4,2},{6,8},{8,6},{10,12},{12,10},{16,18},{18,16},{20,22},{2... | collective-permute-start | bytes 196616 | tf_op jit(solution)/shard_map/ppermute | solution.py:377
  5.9 9.7 %collective-permute-start.1 = (f32[128,128]{1,0:T(8,128)S(1)}, f32[128,128]{1,0:T(8,128)S(1)}, u32[]{:S(2)}, u32[]{:S(2)}) collective-permute-start(f32[128,128]{1,0:T(8,128)S(1)} %get-tuple-element.22), channel_id=1, source_target_pairs={{0,2},{2,0},{4,6},{6,4},{8,10},{10,8},{14,16},{16,14},{18,20},{20,... | collective-permute-start | bytes 196616 | tf_op jit(solution)/shard_map/ppermute | solution.py:377
  13.5 2.1 %collective-permute-start.2 = (f32[128,128]{1,0:T(8,128)S(1)}, f32[128,128]{1,0:T(8,128)S(1)}, u32[]{:S(2)}, u32[]{:S(2)}) collective-permute-start(f32[128,128]{1,0:T(8,128)S(1)} %get-tuple-element.23), channel_id=1, source_target_pairs={{12,14},{14,12},{13,15},{15,13},{44,46},{46,44},{45,47},{47,45},{7... | collective-permute-start | bytes 196616 | tf_op jit(solution)/shard_map/ppermute | solution.py:377
  15.7 6.0 %collective-permute-start.3 = (f32[40,128]{1,0:T(8,128)S(1)}, f32[40,128]{1,0:T(8,128)S(1)}, u32[]{:S(2)}, u32[]{:S(2)}) collective-permute-start(f32[40,128]{1,0:T(8,128)S(1)} %corner.1), channel_id=1, source_target_pairs={{0,1},{1,0},{2,3},{3,2},{4,5},{5,4},{6,7},{7,6},{8,9},{9,8},{10,11... | collective-permute-start | bytes 61448 | tf_op jit(solution)/shard_map/ppermute | solution.py:388

commit v8 on v6

--- a/solution.py
+++ b/solution.py
@@ -16,6 +16,7 @@
 PLANES = 7
 PART = 512
 PITCH = NJ + 8
+LONG = 31
 F32 = jnp.float32
 
 
@@ -98,19 +99,15 @@
     col_ref[...] = by_eights(layer, jnp.zeros((NJ, NK), F32))
 
 
-def skew_kernel(skew_ref, col_ref, wide_ref):
+def factor_kernel(k_ref, skew_ref, t_ref, q_ref, r_ref, plane_ref, wide_ref, skew_col_ref):
     turn = 1 - lax.axis_index("gz")
     lane = lanes()
 
-    def layer(i, col):
+    def widen(i, col):
         g = skew_ref[i].astype(F32)
         wide_ref[pl.ds(pl.multiple_of(i * PITCH, 8), NJ), :] = g
         return jnp.where(lane == i, pltpu.roll(g, i + turn, 1), col)
 
-    col_ref[...] = by_eights(layer, jnp.zeros((NJ, NK), F32))
-
-
-def factor_kernel(k_ref, t_ref, q_ref, r_ref, plane_ref):
     half = 0.5 * ratio_x
     zero = jnp.zeros((NJ, NK), F32)
     one = jnp.ones((NJ, NK), F32)
@@ -124,7 +121,7 @@
     r_ref[ROWS - NJ : ROWS, :] = zero
 
     def layer(i, state):
-        here, ground, left, total = state
+        here, ground, left, total, col = state
         at = pl.ds(pl.multiple_of(i * NJ, NJ), NJ)
         after = k_ref[pl.ds(pl.multiple_of(i * NJ + NJ, NJ), NJ), :]
         link = half * (here + after)
@@ -134,16 +131,17 @@
         t_ref[at, :] = t
         q_ref[at, :] = q
         r_ref[at, :] = r
-        return after, 1.0 + t * ground, t * left, total + q * ground
+        return after, 1.0 + t * ground, t * left, total + q * ground, widen(i, col)
 
     def some(n, state):
-        for m in range(2):
-            state = layer(1 + n * 2 + m, state)
+        for m in range(LONG):
+            state = layer(1 + n * LONG + m, state)
         return state
 
     second = k_ref[NJ : 2 * NJ, :]
-    start = (second, one, half * (first + second), one)
-    _, ground, left, total = lax.fori_loop(0, (NI - 2) // 2, some, start)
+    start = (second, one, half * (first + second), one, widen(0, zero))
+    _, ground, left, total, col = lax.fori_loop(0, (NI - 2) // LONG, some, start)
+    skew_col_ref[...] = widen(NI - 1, col)
     for c, plane in enumerate((total, left, ground, first, last)):
         plane_ref[c * NJ : c * NJ + NJ, :] = plane
 
@@ -386,12 +384,9 @@
     col, u_wide, k_wide, k_sum = call(
         pack_kernel, [(NJ, NK)] + [spread] * 3, 2, 6 * block, 20 * block, "pack"
     )(u, k)
-    skew_col, skew = call(skew_kernel, [(NJ, NK), spread], 1, block, 6 * block, "skew")(
-        yz_skew_factor
-    )
-    t, q, r, planes = call(
-        factor_kernel, [(ROWS, NK)] * 3 + [(5 * NJ, NK)], 1, 20 * block, 16 * block, "factor"
-    )(k)
+    t, q, r, planes, skew, skew_col = call(
+        factor_kernel, [(ROWS, NK)] * 3 + [(5 * NJ, NK), spread, (NJ, NK)], 2, 20 * block, 22 * block, "factor"
+    )(k, yz_skew_factor)
     (to_half,) = call(corner_kernel, [(NJ + 8, NK)], 4, NI * NK, 0, "corner")(*beyond, col)
     got_col = lax.ppermute(to_half, "gz", [(0, 1), (1, 0)])
     (f0,) = call(source_kernel, [spread], 7, 40 * block, 16 * block, "source")(

time: 52.5 us -> 52.3 us (level)
  Pallas kernels: 8.36 us -> 7.71 us
  waiting for transfers between devices: 0.01 us -> 0.59 us
    pallas_call x2 -> x1, Pallas kernels: 1.58 us -> 0.93 us  [body(): call(factor_kernel, [(ROWS, NK)] * 3 + [(5 * NJ, NK), spread, (NJ, NK)],...]
    ppermute x1, waiting for transfers between devices: 0.01 us -> 0.58 us  [body(): got_col = lax.ppermute(to_half, 'gz', [(0, 1), (1, 0)])]
  transfers between devices with their start and end apart: 4 -> 4, of which waited for: 0 -> 1; matrix products, arithmetic and copies ran while one was open for 0% -> 0% of each run, Pallas kernels for 9% -> 8%
where the time goes in v8:
time: 52.3 us; the launch traced here: 52 us
  blocking collectives  27.8 us (53%)
  starting transfers between devices  15.1 us (29%)
  Pallas kernels  7.71 us (15%)
  between operations  0.78 us (1%)
  waiting for transfers between devices  0.59 us (1%)
    all_to_all x1, blocking collectives, body(): got = lax.all_to_all(send, 'gx', 0, 0, tiled=True)  18 us
    ppermute x3, starting transfers between devices, body(): lax.ppermute(rows, 'gy', [way for a, b in pairs for way in ((a, b), (b, a...  12.4 us
    all_to_all x1, blocking collectives, body(): mine = lax.all_to_all(values, 'gx', 0, 0, tiled=True)  9.8 us
    ppermute x1, starting transfers between devices, body(): got_col = lax.ppermute(to_half, 'gz', [(0, 1), (1, 0)])  2.74 us
    pallas_call x1, Pallas kernels, body(): call(source_kernel, [spread], 7, 40 * block, 16 * block, 'source')  1.75 us
    pallas_call x1, Pallas kernels, body(): call(pack_kernel, [(NJ, NK)] + [spread] * 3, 2, 6 * block, 20 * block, 'p...  1.38 us
    pallas_call x1, Pallas kernels, body(): call(sweep_kernel, [(ROWS, NK)] * 2 + [(BLOCKS, 2, PLANES * NK)], 8, 8 *...  1.22 us
    pallas_call x1, Pallas kernels, body(): pl.pallas_call(edge_kernel, out_shape=[pltpu.VMEM((2 * NI, NK), F32)] * 3...  1.07 us
  transfers between devices with their start and end apart: 4, of which 1 were waited for; matrix products, arithmetic and copies ran while one was open for 0% of the time, Pallas kernels for 8%

profile of v8, /device:TPU:7, one launch (start us, length us, event | category | flops | bytes accessed | tf_op | source)
XLA Modules:
  0.0 52.0 jit_solution(17908845700794970916)
XLA Ops:
  0.6 0.0 copy-start.1
  0.6 0.0 copy-start
  0.6 1.1 %edges.1 = (f32[128,128]{1,0:T(8,128)S(1)}, f32[128,128]{1,0:T(8,128)S(1)}, f32[128,128]{1,0:T(8,128)S(1)}) custom-call(f32[64,32,1,128]{3,2,1,0:T(1,128)} %bitcast.11, f32[64,32,1,128]{3,2,1,0:T(1,128)} %bitcast.8), custom_call_target="tpu_custom_call" | custom-call | bytes 262144 | tf_op jit(solution)/shard_map/edges/pallas_call | solution.py:362
  1.7 0.0 copy-start.2
  1.7 4.1 %collective-permute-start = (f32[128,128]{1,0:T(8,128)S(1)}, f32[128,128]{1,0:T(8,128)S(1)}, u32[]{:S(2)}, u32[]{:S(2)}) collective-permute-start(f32[128,128]{1,0:T(8,128)S(1)} %get-tuple-element.22), channel_id=1, source_target_pairs={{2,4},{4,2},{6,8},{8,6},{10,12},{12,10},{16,18},{18,16},{20,22},{2... | collective-permute-start | bytes 196616 | tf_op jit(solution)/shard_map/ppermute | solution.py:380
  5.9 7.6 %collective-permute-start.1 = (f32[128,128]{1,0:T(8,128)S(1)}, f32[128,128]{1,0:T(8,128)S(1)}, u32[]{:S(2)}, u32[]{:S(2)}) collective-permute-start(f32[128,128]{1,0:T(8,128)S(1)} %get-tuple-element.23), channel_id=1, source_target_pairs={{0,2},{2,0},{4,6},{6,4},{8,10},{10,8},{14,16},{16,14},{18,20},{20,... | collective-permute-start | bytes 196616 | tf_op jit(solution)/shard_map/ppermute | solution.py:380
  13.5 0.7 %collective-permute-start.2 = (f32[128,128]{1,0:T(8,128)S(1)}, f32[128,128]{1,0:T(8,128)S(1)}, u32[]{:S(2)}, u32[]{:S(2)}) collective-permute-start(f32[128,128]{1,0:T(8,128)S(1)} %get-tuple-element.24), channel_id=1, source_target_pairs={{12,14},{14,12},{13,15},{15,13},{44,46},{46,44},{45,47},{47,45},{7... | collective-permute-start | bytes 196616 | tf_op jit(solution)/shard_map/ppermute | solution.py:380
  14.2 0.0 copy-done.1
  14.2 0.0 copy-done
  14.2 1.4 %pack.1 = (f32[32,128]{1,0:T(8,128)S(1)}, f32[2560,128]{1,0:T(8,128)S(1)}, f32[2560,128]{1,0:T(8,128)S(1)}, f32[2560,128]{1,0:T(8,128)S(1)}) custom-call(f32[2048,128]{1,0:T(8,128)S(1)} %bitcast.12, f32[2048,128]{1,0:T(8,128)S(1)} %bitcast.9), custom_call_target="tpu_custom_call" | custom-call | flops 1572864 | bytes 5242880 | tf_op jit(solution)/shard_map/pack/pallas_call | solution.py:384
  15.6 0.0 collective-permute-done.first_ref
  15.6 0.0 collective-permute-done.1.second_ref
  15.6 0.0 collective-permute-done.2.third_ref
  15.6 0.1 corner.1
  15.7 2.7 %collective-permute-start.3 = (f32[40,128]{1,0:T(8,128)S(1)}, f32[40,128]{1,0:T(8,128)S(1)}, u32[]{:S(2)}, u32[]{:S(2)}) collective-permute-start(f32[40,128]{1,0:T(8,128)S(1)} %corner.1), channel_id=1, source_target_pairs={{0,1},{1,0},{2,3},{3,2},{4,5},{5,4},{6,7},{7,6},{8,9},{9,8},{10,11... | collective-permute-start | bytes 61448 | tf_op jit(solution)/shard_map/ppermute | solution.py:391
  18.5 0.0 copy-done.2
  18.5 0.9 %factor.1 = (f32[2048,128]{1,0:T(8,128)S(1)}, f32[2048,128]{1,0:T(8,128)S(1)}, f32[2048,128]{1,0:T(8,128)S(1)}, f32[160,128]{1,0:T(8,128)S(1)}, f32[2560,128]{1,0:T(8,128)S(1)}, /*index=5*/f32[32,128]{1,0:T(8,128)S(1)}) custom-call(f32[2048,128]{1,0:T(8,128)S(1)} %bitcast.10, bf16[64,32,128]{2,1,0:T(8,128)(2,1)S(1)} %copy-done.2), custom_call_target="tpu_custom_call" | custom-call | flops 5242880 | bytes 5767168 | tf_op jit(solution)/shard_map/factor/pallas_call | solution.py:387
  19.4 1.7 %source.1.f0_ref = f32[2560,128]{1,0:T(8,128)S(1)} custom-call(f32[2560,128]{1,0:T(8,128)S(1)} %get-tuple-element.18.u_ref, f32[2560,128]{1,0:T(8,128)S(1)} %get-tuple-element.19.k_ref, f32[2560,128]{1,0:T(8,128)S(1)} %get-tuple-element.20.sum_ref, f32[2560,128]{1,0:T(8,128)S(1)} %get-tuple-element.21.skew_ref, ...), custom_call_target="tpu_custom_call" | custom-call | flops 10485760 | bytes 4194304 | tf_op jit(solution)/shard_map/source/pallas_call | solution.py:392
  21.2 0.6 %collective-permute-done.3.got_ref = f32[40,128]{1,0:T(8,128)S(1)} collective-permute-done((f32[40,128]{1,0:T(8,128)S(1)}, f32[40,128]{1,0:T(8,128)S(1)}, u32[]{:S(2)}, u32[]{:S(2)}) %collective-permute-start.3) | collective-permute-done | bytes 20512 | tf_op jit(solution)/shard_map/ppermute | solution.py:391
  21.8 1.2 %sweep.1 = (f32[2048,128]{1,0:T(8,128)}, f32[2048,128]{1,0:T(8,128)S(1)}, f32[16,2,896]{2,1,0:T(2,128)S(1)}) custom-call(f32[2560,128]{1,0:T(8,128)S(1)} %source.1.f0_ref, f32[32,128]{1,0:T(8,128)S(1)} %get-tuple-element.25.col_ref, f32[32,128]{1,0:T(8,128)S(1)} %get-tuple-element.26.skew_col_ref, f32[40,128]{1,0:T(8,128)S(1)} %collective-permute-done.3.got_ref, ...), custom_call_target="tpu_custom_call" | custom-call | flops 2097152 | bytes 6291456 | tf_op jit(solution)/shard_map/sweep/pallas_call | solution.py:395
  23.0 18.0 %all_to_all.16.got_ref = f32[16,2,896]{2,1,0:T(2,128)S(1)} all-to-all(f32[16,2,896]{2,1,0:T(2,128)S(1)} %get-tuple-element.32), channel_id=1, replica_groups=mesh['gx'=16,'gy'=16,'gz'=2] {'gx'}, dimensions={0} | all-to-all | bytes 229376 | tf_op jit(solution)/shard_map/all_to_all | solution.py:399
  41.0 0.2 separator.1
  41.2 9.8 %all_to_all.17 = f32[16,4,128]{2,1,0:T(4,128)S(1)} all-to-all(f32[16,4,128]{2,1,0:T(4,128)S(1)} %bitcast.14), channel_id=1, replica_groups=mesh['gx'=16,'gy'=16,'gz'=2] {'gx'}, dimensions={0} | all-to-all | bytes 65536 | tf_op jit(solution)/shard_map/all_to_all | solution.py:403
  51.0 1.0 %back.1 = f32[2048,128]{1,0:T(8,128)} custom-call(f32[64,128]{1,0:T(8,128)S(1)} %bitcast.13, f32[2048,128]{1,0:T(8,128)S(1)} %get-tuple-element.33.b_ref, f32[2048,128]{1,0:T(8,128)S(1)} %get-tuple-element.27.t_ref, f32[2048,128]{1,0:T(8,128)S(1)} %get-tuple-element.28.q_ref), custom_call_target="tpu_custom_call" | custom-call | flops 1048576 | bytes 4194304 | tf_op jit(solution)/shard_map/back/pallas_call | solution.py:404
Async XLA Ops:
  0.6 13.5 %copy-start.1 = (f32[64,32,128]{2,1,0:T(8,128)S(1)}, f32[64,32,128]{2,1,0:T(8,128)}, u32[]{:S(2)}) copy-start(f32[64,32,128]{2,1,0:T(8,128)} %param.3) | copy-start | bytes 3145732
  0.6 13.5 %copy-start = (f32[64,32,128]{2,1,0:T(8,128)S(1)}, f32[64,32,128]{2,1,0:T(8,128)}, u32[]{:S(2)}) copy-start(f32[64,32,128]{2,1,0:T(8,128)} %param.4) | copy-start | bytes 3145732
  1.7 16.7 %copy-start.2 = (bf16[64,32,128]{2,1,0:T(8,128)(2,1)S(1)}, bf16[64,32,128]{2,1,0:T(8,128)(2,1)}, u32[]{:S(2)}) copy-start(bf16[64,32,128]{2,1,0:T(8,128)(2,1)} %skew_ref.1) | copy-start | bytes 1572868
  1.7 13.8 %collective-permute-start = (f32[128,128]{1,0:T(8,128)S(1)}, f32[128,128]{1,0:T(8,128)S(1)}, u32[]{:S(2)}, u32[]{:S(2)}) collective-permute-start(f32[128,128]{1,0:T(8,128)S(1)} %get-tuple-element.22), channel_id=1, source_target_pairs={{2,4},{4,2},{6,8},{8,6},{10,12},{12,10},{16,18},{18,16},{20,22},{2... | collective-permute-start | bytes 196616 | tf_op jit(solution)/shard_map/ppermute | solution.py:380
  5.9 9.7 %collective-permute-start.1 = (f32[128,128]{1,0:T(8,128)S(1)}, f32[128,128]{1,0:T(8,128)S(1)}, u32[]{:S(2)}, u32[]{:S(2)}) collective-permute-start(f32[128,128]{1,0:T(8,128)S(1)} %get-tuple-element.23), channel_id=1, source_target_pairs={{0,2},{2,0},{4,6},{6,4},{8,10},{10,8},{14,16},{16,14},{18,20},{20,... | collective-permute-start | bytes 196616 | tf_op jit(solution)/shard_map/ppermute | solution.py:380
  13.5 2.1 %collective-permute-start.2 = (f32[128,128]{1,0:T(8,128)S(1)}, f32[128,128]{1,0:T(8,128)S(1)}, u32[]{:S(2)}, u32[]{:S(2)}) collective-permute-start(f32[128,128]{1,0:T(8,128)S(1)} %get-tuple-element.24), channel_id=1, source_target_pairs={{12,14},{14,12},{13,15},{15,13},{44,46},{46,44},{45,47},{47,45},{7... | collective-permute-start | bytes 196616 | tf_op jit(solution)/shard_map/ppermute | solution.py:380
  15.7 6.0 %collective-permute-start.3 = (f32[40,128]{1,0:T(8,128)S(1)}, f32[40,128]{1,0:T(8,128)S(1)}, u32[]{:S(2)}, u32[]{:S(2)}) collective-permute-start(f32[40,128]{1,0:T(8,128)S(1)} %corner.1), channel_id=1, source_target_pairs={{0,1},{1,0},{2,3},{3,2},{4,5},{5,4},{6,7},{7,6},{8,9},{9,8},{10,11... | collective-permute-start | bytes 61448 | tf_op jit(solution)/shard_map/ppermute | solution.py:391

commit v9 on v8

--- a/solution.py
+++ b/solution.py
@@ -82,7 +82,7 @@
     return lax.fori_loop(0, NI // 8, some, start)
 
 
-def pack_kernel(u_ref, k_ref, col_ref, u_wide_ref, k_wide_ref, sum_ref):
+def pack_kernel(u_ref, k_ref, col_ref, u_wide_ref, k_wide_ref):
     turn = 1 - lax.axis_index("gz")
     lane = lanes()
 
@@ -92,20 +92,22 @@
         u, k = u_ref[at, :], k_ref[at, :]
         u_wide_ref[to, :] = u
         k_wide_ref[to, :] = k
-        sum_ref[to, :] = k + jnp.where(lane == NK - 1, 0.0, pltpu.roll(k, NK - 1, 1))
         col = jnp.where(lane == i, pltpu.roll(u, i + turn, 1), col)
         return jnp.where(lane == i + NI, pltpu.roll(k, (i + (NI + turn)) & (NK - 1), 1), col)
 
     col_ref[...] = by_eights(layer, jnp.zeros((NJ, NK), F32))
 
 
-def factor_kernel(k_ref, skew_ref, t_ref, q_ref, r_ref, plane_ref, wide_ref, skew_col_ref):
+def factor_kernel(k_ref, skew_ref, t_ref, q_ref, r_ref, plane_ref, wide_ref, skew_col_ref, sum_ref):
     turn = 1 - lax.axis_index("gz")
     lane = lanes()
 
     def widen(i, col):
         g = skew_ref[i].astype(F32)
-        wide_ref[pl.ds(pl.multiple_of(i * PITCH, 8), NJ), :] = g
+        k = k_ref[pl.ds(pl.multiple_of(i * NJ, NJ), NJ), :]
+        to = pl.ds(pl.multiple_of(i * PITCH, 8), NJ)
+        wide_ref[to, :] = g
+        sum_ref[to, :] = k + jnp.where(lane == NK - 1, 0.0, pltpu.roll(k, NK - 1, 1))
         return jnp.where(lane == i, pltpu.roll(g, i + turn, 1), col)
 
     half = 0.5 * ratio_x
@@ -381,11 +383,11 @@
         for rows, pairs in zip(sent, swaps)
     ]
     spread = (NI * PITCH, NK)
-    col, u_wide, k_wide, k_sum = call(
-        pack_kernel, [(NJ, NK)] + [spread] * 3, 2, 6 * block, 20 * block, "pack"
+    col, u_wide, k_wide = call(
+        pack_kernel, [(NJ, NK)] + [spread] * 2, 2, 6 * block, 20 * block, "pack"
     )(u, k)
-    t, q, r, planes, skew, skew_col = call(
-        factor_kernel, [(ROWS, NK)] * 3 + [(5 * NJ, NK), spread, (NJ, NK)], 2, 20 * block, 22 * block, "factor"
+    t, q, r, planes, skew, skew_col, k_sum = call(
+        factor_kernel, [(ROWS, NK)] * 3 + [(5 * NJ, NK), spread, (NJ, NK), spread], 2, 20 * block, 22 * block, "factor"
     )(k, yz_skew_factor)
     (to_half,) = call(corner_kernel, [(NJ + 8, NK)], 4, NI * NK, 0, "corner")(*beyond, col)
     got_col = lax.ppermute(to_half, "gz", [(0, 1), (1, 0)])

time: 52.3 us -> 52.3 us (level)
  transfers between devices with their start and end apart: 4 -> 4, of which waited for: 1 -> 1; matrix products, arithmetic and copies ran while one was open for 0% -> 0% of each run, Pallas kernels for 8% -> 7%
where the time goes in v9:
time: 52.3 us; the launch traced here: 52 us
  blocking collectives  28.1 us (54%)
  starting transfers between devices  15.1 us (29%)
  Pallas kernels  7.53 us (14%)
  between operations  0.78 us (1%)
    all_to_all x1, blocking collectives, body(): got = lax.all_to_all(send, 'gx', 0, 0, tiled=True)  18.3 us
    ppermute x3, starting transfers between devices, body(): lax.ppermute(rows, 'gy', [way for a, b in pairs for way in ((a, b), (b, a...  12.4 us
    all_to_all x1, blocking collectives, body(): mine = lax.all_to_all(values, 'gx', 0, 0, tiled=True)  9.8 us
    ppermute x1, starting transfers between devices, body(): got_col = lax.ppermute(to_half, 'gz', [(0, 1), (1, 0)])  2.74 us
    pallas_call x1, Pallas kernels, body(): call(source_kernel, [spread], 7, 40 * block, 16 * block, 'source')  1.75 us
    pallas_call x1, Pallas kernels, body(): call(sweep_kernel, [(ROWS, NK)] * 2 + [(BLOCKS, 2, PLANES * NK)], 8, 8 *...  1.22 us
    pallas_call x1, Pallas kernels, body(): call(pack_kernel, [(NJ, NK)] + [spread] * 2, 2, 6 * block, 20 * block, 'p...  1.13 us
    pallas_call x1, Pallas kernels, body(): pl.pallas_call(edge_kernel, out_shape=[pltpu.VMEM((2 * NI, NK), F32)] * 3...  1.07 us
  transfers between devices with their start and end apart: 4, of which 1 were waited for; matrix products, arithmetic and copies ran while one was open for 0% of the time, Pallas kernels for 7%

profile of v9, /device:TPU:7, one launch (start us, length us, event | category | flops | bytes accessed | tf_op | source)
XLA Modules:
  0.0 52.0 jit_solution(10847434121496160236)
XLA Ops:
  0.6 0.0 copy-start.1
  0.6 0.0 copy-start
  0.6 1.1 %edges.1 = (f32[128,128]{1,0:T(8,128)S(1)}, f32[128,128]{1,0:T(8,128)S(1)}, f32[128,128]{1,0:T(8,128)S(1)}) custom-call(f32[64,32,1,128]{3,2,1,0:T(1,128)} %bitcast.11, f32[64,32,1,128]{3,2,1,0:T(1,128)} %bitcast.8), custom_call_target="tpu_custom_call" | custom-call | bytes 262144 | tf_op jit(solution)/shard_map/edges/pallas_call | solution.py:364
  1.7 0.0 copy-start.2
  1.7 4.1 %collective-permute-start = (f32[128,128]{1,0:T(8,128)S(1)}, f32[128,128]{1,0:T(8,128)S(1)}, u32[]{:S(2)}, u32[]{:S(2)}) collective-permute-start(f32[128,128]{1,0:T(8,128)S(1)} %get-tuple-element.22), channel_id=1, source_target_pairs={{2,4},{4,2},{6,8},{8,6},{10,12},{12,10},{16,18},{18,16},{20,22},{2... | collective-permute-start | bytes 196616 | tf_op jit(solution)/shard_map/ppermute | solution.py:382
  5.9 7.6 %collective-permute-start.1 = (f32[128,128]{1,0:T(8,128)S(1)}, f32[128,128]{1,0:T(8,128)S(1)}, u32[]{:S(2)}, u32[]{:S(2)}) collective-permute-start(f32[128,128]{1,0:T(8,128)S(1)} %get-tuple-element.23), channel_id=1, source_target_pairs={{0,2},{2,0},{4,6},{6,4},{8,10},{10,8},{14,16},{16,14},{18,20},{20,... | collective-permute-start | bytes 196616 | tf_op jit(solution)/shard_map/ppermute | solution.py:382
  13.5 0.7 %collective-permute-start.2 = (f32[128,128]{1,0:T(8,128)S(1)}, f32[128,128]{1,0:T(8,128)S(1)}, u32[]{:S(2)}, u32[]{:S(2)}) collective-permute-start(f32[128,128]{1,0:T(8,128)S(1)} %get-tuple-element.24), channel_id=1, source_target_pairs={{12,14},{14,12},{13,15},{15,13},{44,46},{46,44},{45,47},{47,45},{7... | collective-permute-start | bytes 196616 | tf_op jit(solution)/shard_map/ppermute | solution.py:382
  14.2 0.0 copy-done.1
  14.2 0.0 copy-done
  14.2 1.1 %pack.1 = (f32[32,128]{1,0:T(8,128)S(1)}, f32[2560,128]{1,0:T(8,128)S(1)}, f32[2560,128]{1,0:T(8,128)S(1)}) custom-call(f32[2048,128]{1,0:T(8,128)S(1)} %bitcast.12, f32[2048,128]{1,0:T(8,128)S(1)} %bitcast.9), custom_call_target="tpu_custom_call" | custom-call | flops 1572864 | bytes 5242880 | tf_op jit(solution)/shard_map/pack/pallas_call | solution.py:386
  15.3 0.0 collective-permute-done.first_ref
  15.3 0.0 collective-permute-done.1.second_ref
  15.3 0.0 collective-permute-done.2.third_ref
  15.3 0.1 corner.1
  15.5 2.7 %collective-permute-start.3 = (f32[40,128]{1,0:T(8,128)S(1)}, f32[40,128]{1,0:T(8,128)S(1)}, u32[]{:S(2)}, u32[]{:S(2)}) collective-permute-start(f32[40,128]{1,0:T(8,128)S(1)} %corner.1), channel_id=1, source_target_pairs={{0,1},{1,0},{2,3},{3,2},{4,5},{5,4},{6,7},{7,6},{8,9},{9,8},{10,11... | collective-permute-start | bytes 61448 | tf_op jit(solution)/shard_map/ppermute | solution.py:393
  18.2 0.0 copy-done.2
  18.2 1.0 %factor.1 = (f32[2048,128]{1,0:T(8,128)S(1)}, f32[2048,128]{1,0:T(8,128)S(1)}, f32[2048,128]{1,0:T(8,128)S(1)}, f32[160,128]{1,0:T(8,128)S(1)}, f32[2560,128]{1,...) custom-call(f32[2048,128]{1,0:T(8,128)S(1)} %bitcast.10, bf16[64,32,128]{2,1,0:T(8,128)(2,1)S(1)} %copy-done.2), custom_call_target="tpu_custom_call" | custom-call | flops 5242880 | bytes 5767168 | tf_op jit(solution)/shard_map/factor/pallas_call | solution.py:389
  19.2 1.7 %source.1.f0_ref = f32[2560,128]{1,0:T(8,128)S(1)} custom-call(f32[2560,128]{1,0:T(8,128)S(1)} %get-tuple-element.18.u_ref, f32[2560,128]{1,0:T(8,128)S(1)} %get-tuple-element.19.k_ref, f32[2560,128]{1,0:T(8,128)S(1)} %get-tuple-element.20.sum_ref, f32[2560,128]{1,0:T(8,128)S(1)} %get-tuple-element.21.skew_ref, ...), custom_call_target="tpu_custom_call" | custom-call | flops 10485760 | bytes 4194304 | tf_op jit(solution)/shard_map/source/pallas_call | solution.py:394
  21.0 0.5 collective-permute-done.3.got_ref
  21.5 1.2 %sweep.1 = (f32[2048,128]{1,0:T(8,128)}, f32[2048,128]{1,0:T(8,128)S(1)}, f32[16,2,896]{2,1,0:T(2,128)S(1)}) custom-call(f32[2560,128]{1,0:T(8,128)S(1)} %source.1.f0_ref, f32[32,128]{1,0:T(8,128)S(1)} %get-tuple-element.25.col_ref, f32[32,128]{1,0:T(8,128)S(1)} %get-tuple-element.26.skew_col_ref, f32[40,128]{1,0:T(8,128)S(1)} %collective-permute-done.3.got_ref, ...), custom_call_target="tpu_custom_call" | custom-call | flops 2097152 | bytes 6291456 | tf_op jit(solution)/shard_map/sweep/pallas_call | solution.py:397
  22.7 18.3 %all_to_all.16.got_ref = f32[16,2,896]{2,1,0:T(2,128)S(1)} all-to-all(f32[16,2,896]{2,1,0:T(2,128)S(1)} %get-tuple-element.32), channel_id=1, replica_groups=mesh['gx'=16,'gy'=16,'gz'=2] {'gx'}, dimensions={0} | all-to-all | bytes 229376 | tf_op jit(solution)/shard_map/all_to_all | solution.py:401
  41.0 0.2 separator.1
  41.2 9.8 %all_to_all.17 = f32[16,4,128]{2,1,0:T(4,128)S(1)} all-to-all(f32[16,4,128]{2,1,0:T(4,128)S(1)} %bitcast.14), channel_id=1, replica_groups=mesh['gx'=16,'gy'=16,'gz'=2] {'gx'}, dimensions={0} | all-to-all | bytes 65536 | tf_op jit(solution)/shard_map/all_to_all | solution.py:405
  51.0 1.0 %back.1 = f32[2048,128]{1,0:T(8,128)} custom-call(f32[64,128]{1,0:T(8,128)S(1)} %bitcast.13, f32[2048,128]{1,0:T(8,128)S(1)} %get-tuple-element.33.b_ref, f32[2048,128]{1,0:T(8,128)S(1)} %get-tuple-element.27.t_ref, f32[2048,128]{1,0:T(8,128)S(1)} %get-tuple-element.28.q_ref), custom_call_target="tpu_custom_call" | custom-call | flops 1048576 | bytes 4194304 | tf_op jit(solution)/shard_map/back/pallas_call | solution.py:406
Async XLA Ops:
  0.6 13.5 %copy-start.1 = (f32[64,32,128]{2,1,0:T(8,128)S(1)}, f32[64,32,128]{2,1,0:T(8,128)}, u32[]{:S(2)}) copy-start(f32[64,32,128]{2,1,0:T(8,128)} %param.3) | copy-start | bytes 3145732
  0.6 13.5 %copy-start = (f32[64,32,128]{2,1,0:T(8,128)S(1)}, f32[64,32,128]{2,1,0:T(8,128)}, u32[]{:S(2)}) copy-start(f32[64,32,128]{2,1,0:T(8,128)} %param.4) | copy-start | bytes 3145732
  1.7 16.5 %copy-start.2 = (bf16[64,32,128]{2,1,0:T(8,128)(2,1)S(1)}, bf16[64,32,128]{2,1,0:T(8,128)(2,1)}, u32[]{:S(2)}) copy-start(bf16[64,32,128]{2,1,0:T(8,128)(2,1)} %skew_ref.1) | copy-start | bytes 1572868
  1.7 13.6 %collective-permute-start = (f32[128,128]{1,0:T(8,128)S(1)}, f32[128,128]{1,0:T(8,128)S(1)}, u32[]{:S(2)}, u32[]{:S(2)}) collective-permute-start(f32[128,128]{1,0:T(8,128)S(1)} %get-tuple-element.22), channel_id=1, source_target_pairs={{2,4},{4,2},{6,8},{8,6},{10,12},{12,10},{16,18},{18,16},{20,22},{2... | collective-permute-start | bytes 196616 | tf_op jit(solution)/shard_map/ppermute | solution.py:382
  5.9 9.5 %collective-permute-start.1 = (f32[128,128]{1,0:T(8,128)S(1)}, f32[128,128]{1,0:T(8,128)S(1)}, u32[]{:S(2)}, u32[]{:S(2)}) collective-permute-start(f32[128,128]{1,0:T(8,128)S(1)} %get-tuple-element.23), channel_id=1, source_target_pairs={{0,2},{2,0},{4,6},{6,4},{8,10},{10,8},{14,16},{16,14},{18,20},{20,... | collective-permute-start | bytes 196616 | tf_op jit(solution)/shard_map/ppermute | solution.py:382
  13.5 1.9 %collective-permute-start.2 = (f32[128,128]{1,0:T(8,128)S(1)}, f32[128,128]{1,0:T(8,128)S(1)}, u32[]{:S(2)}, u32[]{:S(2)}) collective-permute-start(f32[128,128]{1,0:T(8,128)S(1)} %get-tuple-element.24), channel_id=1, source_target_pairs={{12,14},{14,12},{13,15},{15,13},{44,46},{46,44},{45,47},{47,45},{7... | collective-permute-start | bytes 196616 | tf_op jit(solution)/shard_map/ppermute | solution.py:382
  15.5 6.0 %collective-permute-start.3 = (f32[40,128]{1,0:T(8,128)S(1)}, f32[40,128]{1,0:T(8,128)S(1)}, u32[]{:S(2)}, u32[]{:S(2)}) collective-permute-start(f32[40,128]{1,0:T(8,128)S(1)} %corner.1), channel_id=1, source_target_pairs={{0,1},{1,0},{2,3},{3,2},{4,5},{5,4},{6,7},{7,6},{8,9},{9,8},{10,11... | collective-permute-start | bytes 61448 | tf_op jit(solution)/shard_map/ppermute | solution.py:393

commit v10 on v8

--- a/solution.py
+++ b/solution.py
@@ -16,7 +16,7 @@
 PLANES = 7
 PART = 512
 PITCH = NJ + 8
-LONG = 31
+LONG = 62
 F32 = jnp.float32
 
 

time: 52.3 us -> 52.3 us (level)
  no operation moved by 1% of the time
where the time goes in v10:
time: 52.3 us; the launch traced here: 52 us
  blocking collectives  27.8 us (53%)
  starting transfers between devices  15.1 us (29%)
  Pallas kernels  7.64 us (15%)
  between operations  0.78 us (1%)
  waiting for transfers between devices  0.65 us (1%)
    all_to_all x1, blocking collectives, body(): got = lax.all_to_all(send, 'gx', 0, 0, tiled=True)  18 us
    ppermute x3, starting transfers between devices, body(): lax.ppermute(rows, 'gy', [way for a, b in pairs for way in ((a, b), (b, a...  12.4 us
    all_to_all x1, blocking collectives, body(): mine = lax.all_to_all(values, 'gx', 0, 0, tiled=True)  9.8 us
    ppermute x1, starting transfers between devices, body(): got_col = lax.ppermute(to_half, 'gz', [(0, 1), (1, 0)])  2.74 us
    pallas_call x1, Pallas kernels, body(): call(source_kernel, [spread], 7, 40 * block, 16 * block, 'source')  1.75 us
    pallas_call x1, Pallas kernels, body(): call(pack_kernel, [(NJ, NK)] + [spread] * 3, 2, 6 * block, 20 * block, 'p...  1.38 us
    pallas_call x1, Pallas kernels, body(): call(sweep_kernel, [(ROWS, NK)] * 2 + [(BLOCKS, 2, PLANES * NK)], 8, 8 *...  1.22 us
    pallas_call x1, Pallas kernels, body(): pl.pallas_call(edge_kernel, out_shape=[pltpu.VMEM((2 * NI, NK), F32)] * 3...  1.07 us
  transfers between devices with their start and end apart: 4, of which 1 were waited for; matrix products, arithmetic and copies ran while one was open for 0% of the time, Pallas kernels for 8%

profile of v10, /device:TPU:7, one launch (start us, length us, event | category | flops | bytes accessed | tf_op | source)
XLA Modules:
  0.0 52.0 jit_solution(6098068912255093485)
XLA Ops:
  0.6 0.0 copy-start.1
  0.6 0.0 copy-start
  0.6 1.1 %edges.1 = (f32[128,128]{1,0:T(8,128)S(1)}, f32[128,128]{1,0:T(8,128)S(1)}, f32[128,128]{1,0:T(8,128)S(1)}) custom-call(f32[64,32,1,128]{3,2,1,0:T(1,128)} %bitcast.11, f32[64,32,1,128]{3,2,1,0:T(1,128)} %bitcast.8), custom_call_target="tpu_custom_call" | custom-call | bytes 262144 | tf_op jit(solution)/shard_map/edges/pallas_call | solution.py:362
  1.7 0.0 copy-start.2
  1.7 4.1 %collective-permute-start = (f32[128,128]{1,0:T(8,128)S(1)}, f32[128,128]{1,0:T(8,128)S(1)}, u32[]{:S(2)}, u32[]{:S(2)}) collective-permute-start(f32[128,128]{1,0:T(8,128)S(1)} %get-tuple-element.22), channel_id=1, source_target_pairs={{2,4},{4,2},{6,8},{8,6},{10,12},{12,10},{16,18},{18,16},{20,22},{2... | collective-permute-start | bytes 196616 | tf_op jit(solution)/shard_map/ppermute | solution.py:380
  5.9 7.6 %collective-permute-start.1 = (f32[128,128]{1,0:T(8,128)S(1)}, f32[128,128]{1,0:T(8,128)S(1)}, u32[]{:S(2)}, u32[]{:S(2)}) collective-permute-start(f32[128,128]{1,0:T(8,128)S(1)} %get-tuple-element.23), channel_id=1, source_target_pairs={{0,2},{2,0},{4,6},{6,4},{8,10},{10,8},{14,16},{16,14},{18,20},{20,... | collective-permute-start | bytes 196616 | tf_op jit(solution)/shard_map/ppermute | solution.py:380
  13.5 0.7 %collective-permute-start.2 = (f32[128,128]{1,0:T(8,128)S(1)}, f32[128,128]{1,0:T(8,128)S(1)}, u32[]{:S(2)}, u32[]{:S(2)}) collective-permute-start(f32[128,128]{1,0:T(8,128)S(1)} %get-tuple-element.24), channel_id=1, source_target_pairs={{12,14},{14,12},{13,15},{15,13},{44,46},{46,44},{45,47},{47,45},{7... | collective-permute-start | bytes 196616 | tf_op jit(solution)/shard_map/ppermute | solution.py:380
  14.2 0.0 copy-done.1
  14.2 0.0 copy-done
  14.2 1.4 %pack.1 = (f32[32,128]{1,0:T(8,128)S(1)}, f32[2560,128]{1,0:T(8,128)S(1)}, f32[2560,128]{1,0:T(8,128)S(1)}, f32[2560,128]{1,0:T(8,128)S(1)}) custom-call(f32[2048,128]{1,0:T(8,128)S(1)} %bitcast.12, f32[2048,128]{1,0:T(8,128)S(1)} %bitcast.9), custom_call_target="tpu_custom_call" | custom-call | flops 1572864 | bytes 5242880 | tf_op jit(solution)/shard_map/pack/pallas_call | solution.py:384
  15.6 0.0 collective-permute-done.first_ref
  15.6 0.0 collective-permute-done.1.second_ref
  15.6 0.0 collective-permute-done.2.third_ref
  15.6 0.1 corner.1
  15.7 2.7 %collective-permute-start.3 = (f32[40,128]{1,0:T(8,128)S(1)}, f32[40,128]{1,0:T(8,128)S(1)}, u32[]{:S(2)}, u32[]{:S(2)}) collective-permute-start(f32[40,128]{1,0:T(8,128)S(1)} %corner.1), channel_id=1, source_target_pairs={{0,1},{1,0},{2,3},{3,2},{4,5},{5,4},{6,7},{7,6},{8,9},{9,8},{10,11... | collective-permute-start | bytes 61448 | tf_op jit(solution)/shard_map/ppermute | solution.py:391
  18.5 0.0 copy-done.2
  18.5 0.9 %factor.1 = (f32[2048,128]{1,0:T(8,128)S(1)}, f32[2048,128]{1,0:T(8,128)S(1)}, f32[2048,128]{1,0:T(8,128)S(1)}, f32[160,128]{1,0:T(8,128)S(1)}, f32[2560,128]{1,0:T(8,128)S(1)}, /*index=5*/f32[32,128]{1,0:T(8,128)S(1)}) custom-call(f32[2048,128]{1,0:T(8,128)S(1)} %bitcast.10, bf16[64,32,128]{2,1,0:T(8,128)(2,1)S(1)} %copy-done.2), custom_call_target="tpu_custom_call" | custom-call | flops 5242880 | bytes 5767168 | tf_op jit(solution)/shard_map/factor/pallas_call | solution.py:387
  19.4 1.7 %source.1.f0_ref = f32[2560,128]{1,0:T(8,128)S(1)} custom-call(f32[2560,128]{1,0:T(8,128)S(1)} %get-tuple-element.18.u_ref, f32[2560,128]{1,0:T(8,128)S(1)} %get-tuple-element.19.k_ref, f32[2560,128]{1,0:T(8,128)S(1)} %get-tuple-element.20.sum_ref, f32[2560,128]{1,0:T(8,128)S(1)} %get-tuple-element.21.skew_ref, ...), custom_call_target="tpu_custom_call" | custom-call | flops 10485760 | bytes 4194304 | tf_op jit(solution)/shard_map/source/pallas_call | solution.py:392
  21.1 0.6 %collective-permute-done.3.got_ref = f32[40,128]{1,0:T(8,128)S(1)} collective-permute-done((f32[40,128]{1,0:T(8,128)S(1)}, f32[40,128]{1,0:T(8,128)S(1)}, u32[]{:S(2)}, u32[]{:S(2)}) %collective-permute-start.3) | collective-permute-done | bytes 20512 | tf_op jit(solution)/shard_map/ppermute | solution.py:391
  21.8 1.2 %sweep.1 = (f32[2048,128]{1,0:T(8,128)}, f32[2048,128]{1,0:T(8,128)S(1)}, f32[16,2,896]{2,1,0:T(2,128)S(1)}) custom-call(f32[2560,128]{1,0:T(8,128)S(1)} %source.1.f0_ref, f32[32,128]{1,0:T(8,128)S(1)} %get-tuple-element.25.col_ref, f32[32,128]{1,0:T(8,128)S(1)} %get-tuple-element.26.skew_col_ref, f32[40,128]{1,0:T(8,128)S(1)} %collective-permute-done.3.got_ref, ...), custom_call_target="tpu_custom_call" | custom-call | flops 2097152 | bytes 6291456 | tf_op jit(solution)/shard_map/sweep/pallas_call | solution.py:395
  23.0 18.0 %all_to_all.16.got_ref = f32[16,2,896]{2,1,0:T(2,128)S(1)} all-to-all(f32[16,2,896]{2,1,0:T(2,128)S(1)} %get-tuple-element.32), channel_id=1, replica_groups=mesh['gx'=16,'gy'=16,'gz'=2] {'gx'}, dimensions={0} | all-to-all | bytes 229376 | tf_op jit(solution)/shard_map/all_to_all | solution.py:399
  41.0 0.2 separator.1
  41.2 9.8 %all_to_all.17 = f32[16,4,128]{2,1,0:T(4,128)S(1)} all-to-all(f32[16,4,128]{2,1,0:T(4,128)S(1)} %bitcast.14), channel_id=1, replica_groups=mesh['gx'=16,'gy'=16,'gz'=2] {'gx'}, dimensions={0} | all-to-all | bytes 65536 | tf_op jit(solution)/shard_map/all_to_all | solution.py:403
  51.0 1.0 %back.1 = f32[2048,128]{1,0:T(8,128)} custom-call(f32[64,128]{1,0:T(8,128)S(1)} %bitcast.13, f32[2048,128]{1,0:T(8,128)S(1)} %get-tuple-element.33.b_ref, f32[2048,128]{1,0:T(8,128)S(1)} %get-tuple-element.27.t_ref, f32[2048,128]{1,0:T(8,128)S(1)} %get-tuple-element.28.q_ref), custom_call_target="tpu_custom_call" | custom-call | flops 1048576 | bytes 4194304 | tf_op jit(solution)/shard_map/back/pallas_call | solution.py:404
Async XLA Ops:
  0.6 13.5 %copy-start.1 = (f32[64,32,128]{2,1,0:T(8,128)S(1)}, f32[64,32,128]{2,1,0:T(8,128)}, u32[]{:S(2)}) copy-start(f32[64,32,128]{2,1,0:T(8,128)} %param.3) | copy-start | bytes 3145732
  0.6 13.5 %copy-start = (f32[64,32,128]{2,1,0:T(8,128)S(1)}, f32[64,32,128]{2,1,0:T(8,128)}, u32[]{:S(2)}) copy-start(f32[64,32,128]{2,1,0:T(8,128)} %param.4) | copy-start | bytes 3145732
  1.7 16.7 %copy-start.2 = (bf16[64,32,128]{2,1,0:T(8,128)(2,1)S(1)}, bf16[64,32,128]{2,1,0:T(8,128)(2,1)}, u32[]{:S(2)}) copy-start(bf16[64,32,128]{2,1,0:T(8,128)(2,1)} %skew_ref.1) | copy-start | bytes 1572868
  1.7 13.8 %collective-permute-start = (f32[128,128]{1,0:T(8,128)S(1)}, f32[128,128]{1,0:T(8,128)S(1)}, u32[]{:S(2)}, u32[]{:S(2)}) collective-permute-start(f32[128,128]{1,0:T(8,128)S(1)} %get-tuple-element.22), channel_id=1, source_target_pairs={{2,4},{4,2},{6,8},{8,6},{10,12},{12,10},{16,18},{18,16},{20,22},{2... | collective-permute-start | bytes 196616 | tf_op jit(solution)/shard_map/ppermute | solution.py:380
  5.9 9.7 %collective-permute-start.1 = (f32[128,128]{1,0:T(8,128)S(1)}, f32[128,128]{1,0:T(8,128)S(1)}, u32[]{:S(2)}, u32[]{:S(2)}) collective-permute-start(f32[128,128]{1,0:T(8,128)S(1)} %get-tuple-element.23), channel_id=1, source_target_pairs={{0,2},{2,0},{4,6},{6,4},{8,10},{10,8},{14,16},{16,14},{18,20},{20,... | collective-permute-start | bytes 196616 | tf_op jit(solution)/shard_map/ppermute | solution.py:380
  13.5 2.1 %collective-permute-start.2 = (f32[128,128]{1,0:T(8,128)S(1)}, f32[128,128]{1,0:T(8,128)S(1)}, u32[]{:S(2)}, u32[]{:S(2)}) collective-permute-start(f32[128,128]{1,0:T(8,128)S(1)} %get-tuple-element.24), channel_id=1, source_target_pairs={{12,14},{14,12},{13,15},{15,13},{44,46},{46,44},{45,47},{47,45},{7... | collective-permute-start | bytes 196616 | tf_op jit(solution)/shard_map/ppermute | solution.py:380
  15.7 6.0 %collective-permute-start.3 = (f32[40,128]{1,0:T(8,128)S(1)}, f32[40,128]{1,0:T(8,128)S(1)}, u32[]{:S(2)}, u32[]{:S(2)}) collective-permute-start(f32[40,128]{1,0:T(8,128)S(1)} %corner.1), channel_id=1, source_target_pairs={{0,1},{1,0},{2,3},{3,2},{4,5},{5,4},{6,7},{7,6},{8,9},{9,8},{10,11... | collective-permute-start | bytes 61448 | tf_op jit(solution)/shard_map/ppermute | solution.py:391
